TPU v7x, 512 devices: a whole 4x8x8 slice. The times are simulated.
512 devices in a mesh: row: 32 (over y, x), col: 16 (over z, core).
Axes of the slice: x: 4, y: 8, z: 8, core: 2. Of those that a mesh axis runs over, the one named last changes fastest.
Arguments:
- inputs: bfloat16 [2048, 16384], P('col', 'row'), may hold values from -6 to 6
- out_grad: bfloat16 [2048, 16384], P('col', 'row'), may hold values from -6 to 6
- gate_pre: bfloat16 [2048, 6656], P('row', 'col'), may hold values from -6 to 6
- up_pre: bfloat16 [2048, 6656], P('row', 'col'), may hold values from -6 to 6
- w_gate: bfloat16 [16384, 6656], P('row', 'col'), may hold values from -0.046875 to 0.046875
- w_up: bfloat16 [16384, 6656], P('row', 'col'), may hold values from -0.046875 to 0.046875
- w_down: bfloat16 [6656, 16384], P('col', 'row'), may hold values from -0.078125 to 0.078125
- segment_ids: int32 [2048], P('col'), may hold values from 0 to 63, never falling along the last dimension, each value on 1 to 64 neighbouring positions
Outputs:
- in_grad: bfloat16 [2048, 16384], P('col', 'row')
- grad_gate: bfloat16 [16384, 6656], P('row', 'col')
- grad_up: bfloat16 [16384, 6656], P('row', 'col')
- grad_down: bfloat16 [6656, 16384], P('col', 'row')
Inputs may be any that keep to these rules, and one draw needn't show every extreme that they name: `segment_ids`: ids never fall along the tokens; every id from 0 up to the largest occurs; odd ids mark tool-result documents.
All inputs are finite; a program needn't handle non-finite values.
Results may differ from a plain program's by a relative error of at most 0.033.
Values may be sent and summed in bfloat16 or wider, within the bound.
No kernel may reach another device: no remote copies, remote signals or barrier semaphores. Data moves between devices by JAX's collectives and lax.ppermute only.
A program may use at most 64 MiB of HBM per device.

v0:
```python
import jax
import jax.numpy as jnp
from jax import lax
from jax.sharding import PartitionSpec as P


def swiglu_back(gate_pre, up_pre, hidden_grad):
    gate = gate_pre.astype(jnp.float32)
    up = up_pre.astype(jnp.float32)
    sig = jax.nn.sigmoid(gate)
    silu = gate * sig
    hidden = (silu * up).astype(jnp.bfloat16)
    gate_grad = (hidden_grad * up * sig * (1.0 + gate * (1.0 - sig))).astype(jnp.bfloat16)
    up_grad = (hidden_grad * silu).astype(jnp.bfloat16)
    return (gate_grad, up_grad, hidden)


def body(inputs, out_grad, gate_pre, up_pre, w_gate, w_up, w_down, segment_ids):
    keep = (segment_ids % 2 == 1).astype(jnp.bfloat16)
    masked = out_grad * keep[:, None]
    grad_rows, input_rows = (
        lax.all_gather(masked, "col", axis=0, tiled=True),
        lax.all_gather(inputs, "col", axis=0, tiled=True),
    )
    total_rows = grad_rows.shape[0]
    scale = total_rows ** (-0.5)
    hidden_grad = lax.psum_scatter(
        jnp.einsum("td,fd->tf", grad_rows, w_down, preferred_element_type=jnp.float32).astype(
            jnp.bfloat16
        ),
        "row",
        scatter_dimension=0,
        tiled=True,
    ).astype(jnp.float32)
    gate_local, up_local, hidden_local = swiglu_back(gate_pre, up_pre, hidden_grad)
    gate_grad, up_grad, hidden = (
        lax.all_gather(gate_local, "row", axis=0, tiled=True),
        lax.all_gather(up_local, "row", axis=0, tiled=True),
        lax.all_gather(hidden_local, "row", axis=0, tiled=True),
    )
    grad_gate = (
        jnp.einsum("td,tf->df", input_rows, gate_grad, preferred_element_type=jnp.float32) * scale
    ).astype(jnp.bfloat16)
    grad_up = (
        jnp.einsum("td,tf->df", input_rows, up_grad, preferred_element_type=jnp.float32) * scale
    ).astype(jnp.bfloat16)
    grad_down = (
        jnp.einsum("tf,td->fd", hidden, grad_rows, preferred_element_type=jnp.float32) * scale
    ).astype(jnp.bfloat16)
    first = jnp.einsum("tf,df->td", gate_grad, w_gate, preferred_element_type=jnp.float32)
    in_grad = lax.psum_scatter(
        (first + jnp.einsum("tf,df->td", up_grad, w_up, preferred_element_type=jnp.float32)).astype(
            jnp.bfloat16
        ),
        "col",
        scatter_dimension=0,
        tiled=True,
    )
    return (in_grad, grad_gate, grad_up, grad_down)


def solution(mesh):
    placed = (
        P("col", "row"),
        P("col", "row"),
        P("row", "col"),
        P("row", "col"),
        P("row", "col"),
        P("row", "col"),
        P("col", "row"),
        P("col"),
    )
    return jax.shard_map(
        body,
        mesh=mesh,
        in_specs=placed,
        out_specs=(P("col", "row"), P("row", "col"), P("row", "col"), P("col", "row")),
        check_vma=False,
    )
```

profile of v0, /device:TPU:1, one launch (start us, length us, event | category | flops | bytes accessed | tf_op | source)
XLA Modules:
  0.0 650.6 jit_solution(3425979707606893207)
XLA Ops:
  7.2 0.0 copy-start
  7.2 0.0 all-gather.6.cloned.1.call-start
  7.2 0.7 compare_convert_fusion
  7.9 1.6 broadcast_multiply_fusion
  9.6 0.0 all-gather.6.cloned.1.call-update
  9.6 0.0 reduce-scatter.3.cloned.1.call-start
  9.7 50.2 %all-gather.6.cloned.1.call-done = bf16[2048,512]{1,0:T(8,128)(2,1)} async-done(((bf16[128,512]{1,0:T(8,128)(2,1)}), bf16[2048,512]{1,0:T(8,128)(2,1)}) %all-gather.6.cloned.1.call-update) | async-done | bytes 2097168 | tf_op jit(solution)/shard_map/all_gather | solution.py:22
  59.8 4.2 convolution_convert_fusion
  64.1 0.0 reduce-scatter.3.cloned.1.call-update
  64.1 0.0 all-gather.8.cloned.1.call-start
  64.2 214.1 %reduce-scatter.3.cloned.1.call-done = bf16[64,416]{1,0:T(8,128)(2,1)} async-done(((bf16[2048,416]{1,0:T(8,128)(2,1)}), bf16[64,416]{1,0:T(8,128)(2,1)}) %reduce-scatter.3.cloned.1.call-update) | async-done | bytes 53264 | tf_op jit(solution)/shard_map/reduce_scatter | solution.py:27
  278.3 1.6 fusion.9
  279.8 0.0 all-gather.8.cloned.1.call-update
  279.9 0.0 all-gather.10.cloned.1.call-start
  279.9 0.5 all-gather.10.cloned.1.call-update
  280.4 0.0 all-gather.12.cloned.1.call-start
  280.5 0.5 all-gather.12.cloned.1.call-update
  281.0 0.0 all-gather.14.cloned.1.call-start
  281.1 0.5 all-gather.14.cloned.1.call-update
  281.6 0.0 copy-start.3
  281.6 0.0 reduce-scatter.5.cloned.1.call-start
  281.7 84.2 %all-gather.8.cloned.1.call-done = bf16[2048,416]{1,0:T(8,128)(2,1)} async-done(((bf16[64,416]{1,0:T(8,128)(2,1)}), bf16[2048,416]{1,0:T(8,128)(2,1)}) %all-gather.8.cloned.1.call-update) | async-done | bytes 1703952 | tf_op jit(solution)/shard_map/all_gather | solution.py:37
  365.8 4.8 fusion.15
  370.6 80.1 %all-gather.10.cloned.1.call-done = bf16[2048,416]{1,0:T(8,128)(2,1)} async-done(((bf16[64,416]{1,0:T(8,128)(2,1)}), bf16[2048,416]{1,0:T(8,128)(2,1)}) %all-gather.10.cloned.1.call-update) | async-done | bytes 1703952 | tf_op jit(solution)/shard_map/all_gather | solution.py:38
  450.7 5.4 add_convert_fusion
  456.1 0.0 reduce-scatter.5.cloned.1.call-update
  456.1 41.6 %all-gather.12.cloned.1.call-done = bf16[2048,512]{1,0:T(8,128)(2,1)} async-done(((bf16[128,512]{1,0:T(8,128)(2,1)}), bf16[2048,512]{1,0:T(8,128)(2,1)}) %all-gather.12.cloned.1.call-update) | async-done | bytes 2097168 | tf_op jit(solution)/shard_map/all_gather | solution.py:23
  497.7 4.2 fusion.3
  501.9 1.8 fusion.4
  503.8 75.3 %all-gather.14.cloned.1.call-done = bf16[2048,416]{1,0:T(8,128)(2,1)} async-done(((bf16[64,416]{1,0:T(8,128)(2,1)}), bf16[2048,416]{1,0:T(8,128)(2,1)}) %all-gather.14.cloned.1.call-update) | async-done | bytes 1703952 | tf_op jit(solution)/shard_map/all_gather | solution.py:39
  579.0 4.1 fusion.2
  583.1 60.7 %reduce-scatter.5.cloned.1.call-done = bf16[128,512]{1,0:T(8,128)(2,1)} async-done(((bf16[2048,512]{1,0:T(8,128)(2,1)}), bf16[128,512]{1,0:T(8,128)(2,1)}) %reduce-scatter.5.cloned.1.call-update) | async-done | bytes 131088 | tf_op jit(solution)/shard_map/reduce_scatter | solution.py:51
  (10 shorter events, 0.0 us)
Async XLA Ops:
  7.2 358.7 %copy-start = (bf16[512,416]{0,1:T(8,128)(2,1)S(1)}, bf16[512,416]{0,1:T(8,128)(2,1)}, u32[]{:S(2)}) copy-start(bf16[512,416]{0,1:T(8,128)(2,1)} %param.12) | copy-start | bytes 1277956
  7.2 52.7 %all-gather.6.cloned.1.call-start = ((), (), s32[]{:S(2)}) async-start(), calls=%async_computation.2 | async-start | bytes 2228224 | tf_op jit(solution)/shard_map/all_gather | solution.py:22
  9.6 268.6 %reduce-scatter.3.cloned.1.call-start = ((), (), s32[]{:S(2)}) async-start(), calls=%async_computation.3 | async-start | bytes 2162688 | tf_op jit(solution)/shard_map/reduce_scatter | solution.py:27
  64.1 214.2 %copy-start.4 = (bf16[64,416]{1,0:T(8,128)(2,1)S(1)}, bf16[64,416]{1,0:T(8,128)(2,1)}, u32[]{:S(2)}) copy-start(bf16[64,416]{1,0:T(8,128)(2,1)} %param.11) | copy-start | bytes 159748
  64.1 214.2 %copy-start.5 = (bf16[64,416]{1,0:T(8,128)(2,1)S(1)}, bf16[64,416]{1,0:T(8,128)(2,1)}, u32[]{:S(2)}) copy-start(bf16[64,416]{1,0:T(8,128)(2,1)} %param.10) | copy-start | bytes 159748
  64.1 301.7 %all-gather.8.cloned.1.call-start = ((), (), s32[]{:S(2)}) async-start(), calls=%async_computation.4 | async-start | bytes 2162688 | tf_op jit(solution)/shard_map/all_gather | solution.py:37
  279.9 170.8 %all-gather.10.cloned.1.call-start = ((), (), s32[]{:S(2)}) async-start(), calls=%async_computation.5 | async-start | bytes 2162688 | tf_op jit(solution)/shard_map/all_gather | solution.py:38
  280.4 217.2 %all-gather.12.cloned.1.call-start = ((), (), s32[]{:S(2)}) async-start(), calls=%async_computation.7 | async-start | bytes 2228224 | tf_op jit(solution)/shard_map/all_gather | solution.py:23
  281.0 298.0 %all-gather.14.cloned.1.call-start = ((), (), s32[]{:S(2)}) async-start(), calls=%async_computation.8 | async-start | bytes 2162688 | tf_op jit(solution)/shard_map/all_gather | solution.py:39
  281.6 169.1 %copy-start.3 = (bf16[512,416]{0,1:T(8,128)(2,1)S(1)}, bf16[512,416]{0,1:T(8,128)(2,1)}, u32[]{:S(2)}) copy-start(bf16[512,416]{0,1:T(8,128)(2,1)} %param.13) | copy-start | bytes 1277956
  281.6 362.1 %reduce-scatter.5.cloned.1.call-start = ((), (), s32[]{:S(2)}) async-start(), calls=%async_computation.6 | async-start | bytes 2228224 | tf_op jit(solution)/shard_map/reduce_scatter | solution.py:51
  456.1 45.8 %copy-start.1 = (bf16[2048,416]{1,0:T(8,128)(2,1)S(1)}, bf16[2048,416]{1,0:T(8,128)(2,1)}, u32[]{:S(2)}) copy-start(bf16[2048,416]{1,0:T(8,128)(2,1)} %all-gather.8.cloned.1.call-done) | copy-start | bytes 5111812
  497.7 4.2 copy-start.2
Sparse Core Ops, SparseCore 0:
  10.7 49.0 all-gather.5
  64.2 213.9 reduce-scatter.2
  282.5 83.3 all-gather.7
  369.9 80.7 all-gather.9
  452.9 44.7 all-gather.11
  501.8 77.1 all-gather.13
  582.6 61.0 reduce-scatter.4
where the time goes:
time: 653 us; the launch traced here: 651 us
  waiting for transfers between devices  608 us (93%)
  matrix products  24.5 us (4%)
  between operations  14.2 us (2%)
    reduce_scatter x1, waiting for transfers between devices, body(): lax.psum_scatter(jnp.einsum('td,fd->tf', grad_rows, w_down, preferred_ele...  214 us
    all_gather x1, waiting for transfers between devices, body(): lax.all_gather(gate_local, 'row', axis=0, tiled=True)  84.2 us
    all_gather x1, waiting for transfers between devices, body(): lax.all_gather(up_local, 'row', axis=0, tiled=True)  80.1 us
    all_gather x1, waiting for transfers between devices, body(): lax.all_gather(hidden_local, 'row', axis=0, tiled=True)  75.3 us
    reduce_scatter x1, waiting for transfers between devices, body(): lax.psum_scatter((first + jnp.einsum('tf,df->td', up_grad, w_up, preferre...  60.7 us
    all_gather x1, waiting for transfers between devices, body(): lax.all_gather(masked, 'col', axis=0, tiled=True)  50.2 us
    all_gather x1, waiting for transfers between devices, body(): lax.all_gather(inputs, 'col', axis=0, tiled=True)  41.6 us
  transfers between devices with their start and end apart: 7, of which 7 were waited for; matrix products, arithmetic and copies ran while one was open for 3% of the time, Pallas kernels for 0%

commit v1 on v0

v1 whole, which is shorter than its diff:
```python
import jax
import jax.numpy as jnp
from jax import lax
from jax.sharding import Mesh, PartitionSpec as P

BF = jnp.bfloat16
F32 = jnp.float32


def tied(value, other):
    return lax.optimization_barrier((value, other))[0]


def make_body(ny, nx, nz):
    def shift_x(v, s):
        return lax.ppermute(v, "x", [(i, (i + s) % nx) for i in range(nx)])

    def swap_core(v):
        return lax.ppermute(v, "core", [(0, 1), (1, 0)])

    def body(inputs, out_grad, gate_pre, up_pre, w_gate, w_up, w_down, segment_ids):
        x, core = lax.axis_index("x"), lax.axis_index("core")
        tokens, width = inputs.shape
        units = w_down.shape[0]
        part = tokens // nx
        total = tokens * nz * 2
        scale = total ** (-0.5)

        def place_x(blocks, axis):
            shape = list(blocks[0].shape)
            shape.insert(axis, nx)
            out = jnp.zeros(shape, blocks[0].dtype)
            for s, block in enumerate(blocks):
                out = lax.dynamic_update_slice_in_dim(
                    out, jnp.expand_dims(block, axis), (x - s) % nx, axis
                )
            return out

        def gather_x(v):
            return place_x([v] + [shift_x(v, s) for s in range(1, nx)], 0)

        keep = (segment_ids % 2 == 1).astype(BF)
        masked = out_grad * keep[:, None]

        saved = lax.all_gather(jnp.stack([gate_pre, up_pre]), ("y", "x"), axis=0)

        pieces = jnp.broadcast_to(
            masked.reshape(nx, 1, part, width), (nx, nz, part, width)
        ).reshape(nx * nz * part, width)
        got = lax.all_to_all(pieces, ("x", "z"), 0, 0, tiled=True)
        got = got.reshape(nx, nz * part, width)

        down_own = gather_x(w_down)
        down_other = swap_core(down_own)

        def partial_hidden(weights):
            return jnp.einsum("xtd,xfd->tf", got, weights, preferred_element_type=F32).astype(BF)

        hidden_part = jnp.stack(
            [
                partial_hidden(down_own).reshape(ny, part, units),
                partial_hidden(down_other).reshape(ny, part, units),
            ],
            axis=1,
        )

        weights = gather_x(jnp.concatenate([tied(w_gate, got), w_up], axis=0))
        weights_other = swap_core(weights)

        rows = lax.all_gather(
            tied(jnp.concatenate([masked, inputs], axis=1), got), ("z", "core"), axis=0, tiled=True
        )

        terms = lax.all_to_all(
            hidden_part.reshape(ny * 2 * part, units), "y", 0, 0, tiled=True
        ).reshape(ny, 2 * part, units)
        hidden_sum = jnp.sum(terms.astype(F32), axis=0).astype(BF)
        copies = jnp.broadcast_to(hidden_sum[None], (ny, 2 * part, units))
        hidden_all = lax.all_to_all(
            copies.reshape(ny * 2 * part, units), "y", 0, 0, tiled=True
        ).reshape(ny, 2, part, units)
        hg_own, hg_other = hidden_all[:, 0], hidden_all[:, 1]

        saved = saved.reshape(ny, 2, nx // 2, 2, 2, part, units)
        gate_all = saved[:, :, :, 0].reshape(ny, 2, nx, part, units)
        up_all = saved[:, :, :, 1].reshape(ny, 2, nx, part, units)

        def pick(k):
            def one(a):
                return lax.dynamic_slice(a, (0, k, x, 0, 0), (ny, 1, 1, part, units)).reshape(
                    ny, part, units
                )

            return jnp.stack([one(gate_all), one(up_all)])

        saved_own = pick(core)
        saved_other = swap_core(pick(1 - core))

        def back(hidden_grad, gate_b, up_b):
            gate, up, grad = gate_b.astype(F32), up_b.astype(F32), hidden_grad.astype(F32)
            sig = jax.nn.sigmoid(gate)
            silu = gate * sig
            gate_grad = (grad * up * sig * (1.0 + gate * (1.0 - sig))).astype(BF)
            return gate_grad, (grad * silu).astype(BF), (silu * up).astype(BF)

        def partial_input(hg, pair, w):
            gate_grad, up_grad, _ = back(hg, pair[0], pair[1])
            w = w.reshape(nx, 2, width, units)
            grads = gate_grad.reshape(nz * part, units), up_grad.reshape(nz * part, units)
            return jnp.einsum(
                "tf,xdf->xtd", grads[0], w[:, 0], preferred_element_type=F32
            ) + jnp.einsum("tf,xdf->xtd", grads[1], w[:, 1], preferred_element_type=F32)

        input_part = (
            partial_input(hg_own, saved_own, weights)
            + partial_input(hg_other, saved_other, weights_other)
        ).astype(BF)
        input_terms = lax.all_to_all(
            input_part.reshape(nx * nz * part, width), ("x", "z"), 0, 0, tiled=True
        ).reshape(nx, nz, part, width)
        in_grad = jnp.sum(input_terms.astype(F32), axis=1).astype(BF).reshape(tokens, width)

        hg_here = jnp.zeros((ny, 2, part, units), BF)
        hg_here = lax.dynamic_update_slice_in_dim(hg_here, hg_own[:, None], core, 1)
        hg_here = lax.dynamic_update_slice_in_dim(
            hg_here, swap_core(hg_other)[:, None], 1 - core, 1
        )
        hg_all = place_x([hg_here] + [shift_x(hg_here, s) for s in range(1, nx)], 2)
        gate_grad, up_grad, hidden = (
            v.reshape(total, units) for v in back(hg_all, gate_all, up_all)
        )
        masked_rows, input_rows = rows[:, :width], rows[:, width:]

        def weight_grad(spec, a, b):
            return (jnp.einsum(spec, a, b, preferred_element_type=F32) * scale).astype(BF)

        grad_gate = weight_grad("td,tf->df", input_rows, gate_grad)
        grad_up = weight_grad("td,tf->df", input_rows, up_grad)
        grad_down = weight_grad("tf,td->fd", hidden, masked_rows)
        return in_grad, grad_gate, grad_up, grad_down

    return body


def solution(mesh):
    nx = 4 if mesh.shape["row"] >= 16 else 2
    ny, nz = mesh.shape["row"] // nx, mesh.shape["col"] // 2
    grid = Mesh(mesh.devices.reshape(ny, nx, nz, 2), ("y", "x", "z", "core"))
    row, col = ("y", "x"), ("z", "core")
    return jax.shard_map(
        make_body(ny, nx, nz),
        mesh=grid,
        in_specs=(
            P(col, row), P(col, row), P(row, col), P(row, col),
            P(row, col), P(row, col), P(col, row), P(col),
        ),
        out_specs=(P(col, row), P(row, col), P(row, col), P(col, row)),
        check_vma=False,
    )
```

time: 653 us -> 270 us (0.41)
  waiting for transfers between devices: 608 us -> 82.4 us
  starting transfers between devices: 0.28 us -> 74.2 us
  local copies, waits for them, and re-layouts: 0.03 us -> 66.1 us
  other arithmetic: 3.95 us -> 12.9 us
  matrix products: 24.5 us -> 16.2 us
    all_gather x5 -> x2, waiting for transfers between devices: 331 us -> 0.01 us  [the longest x1 0.01 us: body(): saved = lax.all_gather(jnp.stack([gate_pre, up_pre]), ('y', 'x'), axis=0)]
    reduce_scatter x2 -> x0, waiting for transfers between devices: 275 us -> none  [the longest x1 214 us: body(): lax.psum_scatter(jnp.einsum('td,fd->tf', grad_rows, w_down, preferred_ele...]
    ppermute x0 -> x13, waiting for transfers between devices: none -> 61 us  [the longest x9 61 us: shift_x(): return lax.ppermute(v, 'x', [(i, (i + s) % nx) for i in range(nx)])]
    ppermute x0 -> x13, starting transfers between devices: none -> 40.9 us  [the longest x9 29.8 us: shift_x(): return lax.ppermute(v, 'x', [(i, (i + s) % nx) for i in range(nx)])]
    all_to_all x0 -> x4, starting transfers between devices: none -> 33.2 us  [the longest x1 12.7 us: body(): got = lax.all_to_all(pieces, ('x', 'z'), 0, 0, tiled=True)]
    all_to_all x0 -> x4, waiting for transfers between devices: none -> 21.3 us  [the longest x1 11.7 us: body(): lax.all_to_all(input_part.reshape(nx * nz * part, width), ('x', 'z'), 0,...]
    slice x0 -> x5, local copies, waits for them, and re-layouts: none -> 17.9 us  [the longest x1 5.96 us: partial_input(): w[:, 1]]
    reshape x0 -> x2, local copies, waits for them, and re-layouts: none -> 15.3 us  [partial_input(): w = w.reshape(nx, 2, width, units)]
  transfers between devices with their start and end apart: 7 -> 19, of which waited for: 7 -> 7; matrix products, arithmetic and copies ran while one was open for 3% -> 30% of each run, Pallas kernels for 0% -> 0%
where the time goes in v1:
time: 270 us; the launch traced here: 266 us
  waiting for transfers between devices  82.4 us (31%)
  starting transfers between devices  74.2 us (27%)
  local copies, waits for them, and re-layouts  66.1 us (24%)
  matrix products  16.2 us (6%)
  between operations  14.6 us (5%)
  other arithmetic  12.9 us (5%)
    ppermute x9, waiting for transfers between devices, shift_x(): return lax.ppermute(v, 'x', [(i, (i + s) % nx) for i in range(nx)])  61 us
    ppermute x9, starting transfers between devices, shift_x(): return lax.ppermute(v, 'x', [(i, (i + s) % nx) for i in range(nx)])  29.8 us
    reshape x2, local copies, waits for them, and re-layouts, partial_input(): w = w.reshape(nx, 2, width, units)  15.3 us
    all_to_all x1, starting transfers between devices, body(): got = lax.all_to_all(pieces, ('x', 'z'), 0, 0, tiled=True)  12.7 us
    dynamic_update_slice x12, local copies, waits for them, and re-layouts, place_x(): lax.dynamic_update_slice_in_dim(out, jnp.expand_dims(block, axis), (x - s...  12.6 us
    all_to_all x1, waiting for transfers between devices, body(): lax.all_to_all(input_part.reshape(nx * nz * part, width), ('x', 'z'), 0,...  11.7 us
    ppermute x4, starting transfers between devices, swap_core(): return lax.ppermute(v, 'core', [(0, 1), (1, 0)])  11.1 us
    all_to_all x1, waiting for transfers between devices, body(): lax.all_to_all(copies.reshape(ny * 2 * part, units), 'y', 0, 0, tiled=True)  9.68 us
  transfers between devices with their start and end apart: 19, of which 7 were waited for; matrix products, arithmetic and copies ran while one was open for 30% of the time, Pallas kernels for 0%

profile of v1, /device:TPU:1, one launch (start us, length us, event | category | flops | bytes accessed | tf_op | source)
XLA Modules:
  0.0 266.3 jit_solution(2151848630624730806)
XLA Ops:
  8.8 4.0 %collective-permute-start.3 = (bf16[416,512]{1,0:T(8,128)(2,1)}, bf16[416,512]{1,0:T(8,128)(2,1)S(1)}, u32[]{:S(2)}, u32[]{:S(2)}) collective-permute-start(bf16[416,512]{1,0:T(8,128)(2,1)} %param.14), channel_id=1, source_target_pairs={{0,16},{16,32},{32,48},{48,0},{1,17},{17,33},{33,49},{49,1},{2,18}... | collective-permute-start | bytes 1277960 | tf_op jit(solution)/shard_map/ppermute | solution.py:16
  15.6 12.7 %all-to-all-start = ((bf16[32,32,512]{2,1,0:T(8,128)(2,1)}), bf16[32,32,512]{2,1,0:T(8,128)(2,1)}, u32[]{:S(2)}, u32[]{:S(2)}) async-start(bf16[32,32,512]{2,1,0:T(8,128)(2,1)} %bitcast.1), calls=%async_computation | async-start | bytes 2097152 | tf_op jit(solution)/shard_map/all_to_all | solution.py:50
  28.3 4.6 %collective-permute-start.4 = (bf16[416,512]{1,0:T(8,128)(2,1)S(1)}, bf16[416,512]{1,0:T(8,128)(2,1)S(1)}, u32[]{:S(2)}, u32[]{:S(2)}) collective-permute-start(bf16[416,512]{1,0:T(8,128)(2,1)S(1)} %copy-done.10), channel_id=1, source_target_pairs={{0,32},{16,48},{32,0},{48,16},{1,33},{17,49},{33,1},{49,17},{2,34}... | collective-permute-start | bytes 1277960 | tf_op jit(solution)/shard_map/ppermute | solution.py:16
  32.9 2.8 %collective-permute-start.5 = (bf16[416,512]{1,0:T(8,128)(2,1)S(1)}, bf16[416,512]{1,0:T(8,128)(2,1)S(1)}, u32[]{:S(2)}, u32[]{:S(2)}) collective-permute-start(bf16[416,512]{1,0:T(8,128)(2,1)S(1)} %copy-done.10), channel_id=1, source_target_pairs={{0,48},{16,0},{32,16},{48,32},{1,49},{17,1},{33,17},{49,33},{2,50}... | collective-permute-start | bytes 1277960 | tf_op jit(solution)/shard_map/ppermute | solution.py:16
  36.0 19.1 %collective-permute-done.4 = bf16[416,512]{1,0:T(8,128)(2,1)S(1)} collective-permute-done((bf16[416,512]{1,0:T(8,128)(2,1)S(1)}, bf16[416,512]{1,0:T(8,128)(2,1)S(1)}, u32[]{:S(2)}, u32[]{:S(2)}) %collective-permute-start.4) | collective-permute-done | bytes 426016 | tf_op jit(solution)/shard_map/ppermute | solution.py:16
  55.2 8.9 %collective-permute-done.5 = bf16[416,512]{1,0:T(8,128)(2,1)S(1)} collective-permute-done((bf16[416,512]{1,0:T(8,128)(2,1)S(1)}, bf16[416,512]{1,0:T(8,128)(2,1)S(1)}, u32[]{:S(2)}, u32[]{:S(2)}) %collective-permute-start.5) | collective-permute-done | bytes 426016 | tf_op jit(solution)/shard_map/ppermute | solution.py:16
  64.1 2.6 collective-permute-start.6
  68.9 3.0 %collective-permute-start = (bf16[1024,416]{0,1:T(8,128)(2,1)S(1)}, bf16[1024,416]{0,1:T(8,128)(2,1)}, u32[]{:S(2)}, u32[]{:S(2)}) collective-permute-start(bf16[1024,416]{0,1:T(8,128)(2,1)S(1)} %constant_dynamic-update-slice_fusion), channel_id=1, source_target_pairs={{0,16},{16,32},{32,48},{48,0},{1,17},{17,33},{33,49},{49,1},{2,18}... | collective-permute-start | bytes 2555912 | tf_op jit(solution)/shard_map/ppermute | solution.py:16
  71.9 4.3 %collective-permute-start.1 = (bf16[1024,416]{0,1:T(8,128)(2,1)S(1)}, bf16[1024,416]{0,1:T(8,128)(2,1)}, u32[]{:S(2)}, u32[]{:S(2)}) collective-permute-start(bf16[1024,416]{0,1:T(8,128)(2,1)S(1)} %constant_dynamic-update-slice_fusion), channel_id=1, source_target_pairs={{0,32},{16,48},{32,0},{48,16},{1,33},{17,49},{33,1},{49,17},{2,34}... | collective-permute-start | bytes 2555912 | tf_op jit(solution)/shard_map/ppermute | solution.py:16
  76.2 2.2 collective-permute-start.2
  80.4 2.2 broadcast_in_dim.65
  83.6 2.5 fusion.42
  87.1 6.8 %all-to-all-start.1 = ((bf16[8,64,416]{2,1,0:T(8,128)(2,1)}), bf16[8,64,416]{2,1,0:T(8,128)(2,1)S(1)}, u32[]{:S(2)}, u32[]{:S(2)}) async-start(bf16[8,64,416]{2,1,0:T(8,128)(2,1)} %bitcast.16), calls=%async_computation.1 | async-start | bytes 1048576 | tf_op jit(solution)/shard_map/all_to_all | solution.py:74
  93.9 4.1 %collective-permute-done = bf16[1024,416]{0,1:T(8,128)(2,1)} collective-permute-done((bf16[1024,416]{0,1:T(8,128)(2,1)S(1)}, bf16[1024,416]{0,1:T(8,128)(2,1)}, u32[]{:S(2)}, u32[]{:S(2)}) %collective-permute-start) | collective-permute-done | bytes 852000 | tf_op jit(solution)/shard_map/ppermute | solution.py:16
  100.1 28.3 %collective-permute-done.1 = bf16[1024,416]{0,1:T(8,128)(2,1)} collective-permute-done((bf16[1024,416]{0,1:T(8,128)(2,1)S(1)}, bf16[1024,416]{0,1:T(8,128)(2,1)}, u32[]{:S(2)}, u32[]{:S(2)}) %collective-permute-start.1) | collective-permute-done | bytes 852000 | tf_op jit(solution)/shard_map/ppermute | solution.py:16
  132.7 2.9 %collective-permute-start.7 = (bf16[4,1024,416]{1,2,0:T(8,128)(2,1)}, bf16[4,1024,416]{1,2,0:T(8,128)(2,1)}, u32[]{:S(2)}, u32[]{:S(2)}) collective-permute-start(bf16[4,1024,416]{1,2,0:T(8,128)(2,1)} %bitcast_dynamic-update-slice_fusion), channel_id=1, source_target_pairs={{0,1},{1,0},{2,3},{3,2},{4,5},{5,4},{6,7},{7,6},{8,9},{9,8},{10,11... | collective-permute-start | bytes 10223624 | tf_op jit(solution)/shard_map/ppermute | solution.py:19
  136.6 6.9 %all-to-all-start.2 = ((bf16[8,64,416]{2,1,0:T(8,128)(2,1)}), bf16[8,64,416]{2,1,0:T(8,128)(2,1)}, u32[]{:S(2)}, u32[]{:S(2)}) async-start(bf16[8,64,416]{2,1,0:T(8,128)(2,1)} %broadcast_in_dim.77), calls=%async_computation.2 | async-start | bytes 1048576 | tf_op jit(solution)/shard_map/all_to_all | solution.py:79
  144.3 7.6 %reshape.196 = bf16[4,2,512,416]{2,1,3,0:T(2,128)(2,1)S(1)} reshape(bf16[4,1024,416]{1,2,0:T(8,128)(2,1)} %bitcast_dynamic-update-slice_fusion) | data formatting | bytes 6815744 | tf_op jit(solution)/shard_map/reshape | solution.py:108
  151.9 9.7 %all-to-all-done.2 = bf16[8,64,416]{2,1,0:T(8,128)(2,1)} async-done(((bf16[8,64,416]{2,1,0:T(8,128)(2,1)}), bf16[8,64,416]{2,1,0:T(8,128)(2,1)}, u32[]{:S(2)}, u32[]{:S(2)}) %all-to-all-start.2) | async-done | bytes 426016 | tf_op jit(solution)/shard_map/all_to_all | solution.py:79
  162.5 2.4 collective-permute-start.9
  168.2 2.4 collective-permute-start.10
  170.6 6.0 %fusion.64 = (bf16[4,1,512,416]{2,1,3,0:T(2,128)(2,1)}, bf16[4,1,512,416]{2,1,3,0:T(2,128)(2,1)}) fusion(bf16[4,2,512,416]{2,1,3,0:T(2,128)(2,1)S(1)} %reshape.196), kind=kLoop, calls=%fused_computation.111 | loop fusion | bytes 6815744 | tf_op jit(solution)/shard_map/slice | solution.py:112
  176.6 4.3 %collective-permute-start.11 = (bf16[8,2,32,416]{3,2,0,1:T(8,128)(2,1)}, bf16[8,2,32,416]{3,2,0,1:T(8,128)(2,1)}, u32[]{:S(2)}, u32[]{:S(2)}) collective-permute-start(bf16[8,2,32,416]{3,2,0,1:T(8,128)(2,1)} %bitcast_dynamic-update-slice_fusion.12), channel_id=1, source_target_pairs={{0,32},{16,48},{32,0},{48,16},{1,33},{17,49},{33,1},{49,17},{2,34}... | collective-permute-start | bytes 1277960 | tf_op jit(solution)/shard_map/ppermute | solution.py:16
  180.9 2.2 collective-permute-start.12
  186.5 7.6 %reshape.199 = bf16[4,2,512,416]{2,1,3,0:T(2,128)(2,1)S(1)} reshape(bf16[4,1024,416]{1,2,0:T(8,128)(2,1)} %collective-permute-done.7) | data formatting | bytes 6815744 | tf_op jit(solution)/shard_map/reshape | solution.py:108
  194.1 5.9 %fusion.63 = (bf16[4,1,512,416]{2,1,3,0:T(2,128)(2,1)}, bf16[4,1,512,416]{2,1,3,0:T(2,128)(2,1)}) fusion(bf16[4,2,512,416]{2,1,3,0:T(2,128)(2,1)S(1)} %reshape.199), kind=kLoop, calls=%fused_computation.110 | loop fusion | bytes 6815744 | tf_op jit(solution)/shard_map/slice | solution.py:111
  200.1 5.6 %fusion.62 = (bf16[8,2,2,1,2,32,416]{6,5,4,3,2,1,0:T(8,128)(2,1)}, bf16[8,2,2,1,2,32,416]{6,5,4,2,1,0,3:T(8,128)(2,1)S(1)}, bf16[8,2,2,1,2,32,416]{6,5,4,2,1,0,3...) fusion(bf16[8,2,2,2,2,32,416]{6,5,4,3,2,1,0:T(8,128)(2,1)} %bitcast.187), kind=kLoop, calls=%fused_computation.109 | loop fusion | bytes 10223616 | tf_op jit(solution)/shard_map/slice | solution.py:85
  206.2 3.2 %collective-permute-start.8 = (bf16[2,8,32,416]{3,2,1,0:T(8,128)(2,1)S(1)}, bf16[2,8,32,416]{3,2,1,0:T(8,128)(2,1)S(1)}, u32[]{:S(2)}, u32[]{:S(2)}) collective-permute-start(bf16[2,8,32,416]{3,2,1,0:T(8,128)(2,1)S(1)} %pad_maximum_fusion.1), channel_id=1, source_target_pairs={{0,1},{1,0},{2,3},{3,2},{4,5},{5,4},{6,7},{7,6},{8,9},{9,8},{10,11... | collective-permute-start | bytes 1277960 | tf_op jit(solution)/shard_map/ppermute | solution.py:19
  218.7 6.8 %all-to-all-start.3 = ((bf16[32,32,512]{2,1,0:T(8,128)(2,1)}), bf16[32,32,512]{2,1,0:T(8,128)(2,1)S(1)}, u32[]{:S(2)}, u32[]{:S(2)}) async-start(bf16[32,32,512]{2,1,0:T(8,128)(2,1)} %bitcast.49), calls=%async_computation.3 | async-start | bytes 2097152 | tf_op jit(solution)/shard_map/all_to_all | solution.py:118
  229.4 3.6 %fusion.3 = (bf16[8,2,4,32,416]{4,3,0,2,1:T(8,128)(2,1)S(1)}, bf16[8,2,4,32,416]{4,3,0,2,1:T(8,128)(2,1)S(1)}) fusion(bf16[8,2,4,32,416]{4,3,0,2,1:T(8,128)(2,1)} %bitcast_dynamic-update-slice_fusion.7, bf16[8,2,4,32,416]{4,3,0,2,1:T(8,128)(2,1)S(1)} %bitcast.186, bf16[8,2,4,32,416]{4,3,0,2,1:T(8,128)(2,1)S(1)} %bitcast.183), kind=kLoop, calls=%fused_computation.10 | loop fusion | flops 13631488 | bytes 8519680 | tf_op jit(solution)/shard_map/convert_element_type | solution.py:104
  239.1 11.7 %all-to-all-done.3 = bf16[32,32,512]{2,1,0:T(8,128)(2,1)S(1)} async-done(((bf16[32,32,512]{2,1,0:T(8,128)(2,1)}), bf16[32,32,512]{2,1,0:T(8,128)(2,1)S(1)}, u32[]{:S(2)}, u32[]{:S(2)}) %all-to-all-start.3) | async-done | bytes 1048608 | tf_op jit(solution)/shard_map/all_to_all | solution.py:118
  251.5 4.2 %fusion.38 = bf16[512,416]{0,1:T(8,128)(2,1)} fusion(bf16[2048,416]{1,0:T(8,128)(2,1)} %bitcast.188, bf16[2048,1024]{1,0:T(8,128)(2,1)} %all-gather.4.cloned.1.call-done), kind=kOutput, calls=%fused_computation.40 | convolution fusion | flops 872841216 | bytes 4620288 | tf_op jit(solution)/shard_map/td,tf->df/dot_general | solution.py:135
  (91 shorter events, 50.7 us)
Async XLA Ops:
  7.2 21.2 %copy-start.10 = (bf16[416,512]{1,0:T(8,128)(2,1)S(1)}, bf16[416,512]{1,0:T(8,128)(2,1)}, u32[]{:S(2)}) copy-start(bf16[416,512]{1,0:T(8,128)(2,1)} %param.14) | copy-start | bytes 1277956
  7.2 192.9 %all-gather.6.cloned.1.call-start = ((), (), s32[]{:S(2)}) async-start(), calls=%async_computation.5 | async-start | bytes 4325376 | tf_op jit(solution)/shard_map/all_gather | solution.py:45
  8.8 27.2 %collective-permute-start.3 = (bf16[416,512]{1,0:T(8,128)(2,1)}, bf16[416,512]{1,0:T(8,128)(2,1)S(1)}, u32[]{:S(2)}, u32[]{:S(2)}) collective-permute-start(bf16[416,512]{1,0:T(8,128)(2,1)} %param.14), channel_id=1, source_target_pairs={{0,16},{16,32},{32,48},{48,0},{1,17},{17,33},{33,49},{49,1},{2,18}... | collective-permute-start | bytes 1277960 | tf_op jit(solution)/shard_map/ppermute | solution.py:16
  15.6 51.1 %all-to-all-start = ((bf16[32,32,512]{2,1,0:T(8,128)(2,1)}), bf16[32,32,512]{2,1,0:T(8,128)(2,1)}, u32[]{:S(2)}, u32[]{:S(2)}) async-start(bf16[32,32,512]{2,1,0:T(8,128)(2,1)} %bitcast.1), calls=%async_computation | async-start | bytes 2097152 | tf_op jit(solution)/shard_map/all_to_all | solution.py:50
  28.3 26.8 %collective-permute-start.4 = (bf16[416,512]{1,0:T(8,128)(2,1)S(1)}, bf16[416,512]{1,0:T(8,128)(2,1)S(1)}, u32[]{:S(2)}, u32[]{:S(2)}) collective-permute-start(bf16[416,512]{1,0:T(8,128)(2,1)S(1)} %copy-done.10), channel_id=1, source_target_pairs={{0,32},{16,48},{32,0},{48,16},{1,33},{17,49},{33,1},{49,17},{2,34}... | collective-permute-start | bytes 1277960 | tf_op jit(solution)/shard_map/ppermute | solution.py:16
  32.9 31.1 %collective-permute-start.5 = (bf16[416,512]{1,0:T(8,128)(2,1)S(1)}, bf16[416,512]{1,0:T(8,128)(2,1)S(1)}, u32[]{:S(2)}, u32[]{:S(2)}) collective-permute-start(bf16[416,512]{1,0:T(8,128)(2,1)S(1)} %copy-done.10), channel_id=1, source_target_pairs={{0,48},{16,0},{32,16},{48,32},{1,49},{17,1},{33,17},{49,33},{2,50}... | collective-permute-start | bytes 1277960 | tf_op jit(solution)/shard_map/ppermute | solution.py:16
  64.1 19.5 %collective-permute-start.6 = (bf16[4,416,512]{2,1,0:T(8,128)(2,1)S(1)}, bf16[4,416,512]{2,1,0:T(8,128)(2,1)}, u32[]{:S(2)}, u32[]{:S(2)}) collective-permute-start(bf16[4,416,512]{2,1,0:T(8,128)(2,1)S(1)} %bitcast_dynamic-update-slice_fusion.8), channel_id=1, source_target_pairs={{0,1},{1,0},{2,3},{3,2},{4,5},{5,4},{6,7},{7,6},{8,9},{9,8},{10,11... | collective-permute-start | bytes 5111816 | tf_op jit(solution)/shard_map/ppermute | solution.py:19
  68.9 29.2 %collective-permute-start = (bf16[1024,416]{0,1:T(8,128)(2,1)S(1)}, bf16[1024,416]{0,1:T(8,128)(2,1)}, u32[]{:S(2)}, u32[]{:S(2)}) collective-permute-start(bf16[1024,416]{0,1:T(8,128)(2,1)S(1)} %constant_dynamic-update-slice_fusion), channel_id=1, source_target_pairs={{0,16},{16,32},{32,48},{48,0},{1,17},{17,33},{33,49},{49,1},{2,18}... | collective-permute-start | bytes 2555912 | tf_op jit(solution)/shard_map/ppermute | solution.py:16
  71.9 56.5 %collective-permute-start.1 = (bf16[1024,416]{0,1:T(8,128)(2,1)S(1)}, bf16[1024,416]{0,1:T(8,128)(2,1)}, u32[]{:S(2)}, u32[]{:S(2)}) collective-permute-start(bf16[1024,416]{0,1:T(8,128)(2,1)S(1)} %constant_dynamic-update-slice_fusion), channel_id=1, source_target_pairs={{0,32},{16,48},{32,0},{48,16},{1,33},{17,49},{33,1},{49,17},{2,34}... | collective-permute-start | bytes 2555912 | tf_op jit(solution)/shard_map/ppermute | solution.py:16
  76.2 54.3 %collective-permute-start.2 = (bf16[1024,416]{0,1:T(8,128)(2,1)S(1)}, bf16[1024,416]{0,1:T(8,128)(2,1)}, u32[]{:S(2)}, u32[]{:S(2)}) collective-permute-start(bf16[1024,416]{0,1:T(8,128)(2,1)S(1)} %constant_dynamic-update-slice_fusion), channel_id=1, source_target_pairs={{0,48},{16,0},{32,16},{48,32},{1,49},{17,1},{33,17},{49,33},{2,50}... | collective-permute-start | bytes 2555912 | tf_op jit(solution)/shard_map/ppermute | solution.py:16
  87.1 48.5 %all-to-all-start.1 = ((bf16[8,64,416]{2,1,0:T(8,128)(2,1)}), bf16[8,64,416]{2,1,0:T(8,128)(2,1)S(1)}, u32[]{:S(2)}, u32[]{:S(2)}) async-start(bf16[8,64,416]{2,1,0:T(8,128)(2,1)} %bitcast.16), calls=%async_computation.1 | async-start | bytes 1048576 | tf_op jit(solution)/shard_map/all_to_all | solution.py:74
  130.5 13.0 %copy-start.11 = (bf16[128,512]{1,0:T(8,128)(2,1)S(1)}, bf16[128,512]{1,0:T(8,128)(2,1)}, u32[]{:S(2)}) copy-start(bf16[128,512]{1,0:T(8,128)(2,1)} %param.8) | copy-start | bytes 393220
  132.7 53.8 %collective-permute-start.7 = (bf16[4,1024,416]{1,2,0:T(8,128)(2,1)}, bf16[4,1024,416]{1,2,0:T(8,128)(2,1)}, u32[]{:S(2)}, u32[]{:S(2)}) collective-permute-start(bf16[4,1024,416]{1,2,0:T(8,128)(2,1)} %bitcast_dynamic-update-slice_fusion), channel_id=1, source_target_pairs={{0,1},{1,0},{2,3},{3,2},{4,5},{5,4},{6,7},{7,6},{8,9},{9,8},{10,11... | collective-permute-start | bytes 10223624 | tf_op jit(solution)/shard_map/ppermute | solution.py:19
  136.6 25.0 %all-to-all-start.2 = ((bf16[8,64,416]{2,1,0:T(8,128)(2,1)}), bf16[8,64,416]{2,1,0:T(8,128)(2,1)}, u32[]{:S(2)}, u32[]{:S(2)}) async-start(bf16[8,64,416]{2,1,0:T(8,128)(2,1)} %broadcast_in_dim.77), calls=%async_computation.2 | async-start | bytes 1048576 | tf_op jit(solution)/shard_map/all_to_all | solution.py:79
  143.4 108.1 %all-gather.4.cloned.1.call-start = ((), (), s32[]{:S(2)}) async-start(), calls=%async_computation.4 | async-start | bytes 4456448 | tf_op jit(solution)/shard_map/all_gather | solution.py:70
  162.5 4.9 %collective-permute-start.9 = (bf16[8,32,416]{2,1,0:T(8,128)(2,1)S(1)}, bf16[8,32,416]{2,1,0:T(8,128)(2,1)S(1)}, u32[]{:S(2)}, u32[]{:S(2)}) collective-permute-start(bf16[8,32,416]{2,1,0:T(8,128)(2,1)S(1)} %slice_bitcast_fusion.3), channel_id=1, source_target_pairs={{0,1},{1,0},{2,3},{3,2},{4,5},{5,4},{6,7},{7,6},{8,9},{9,8},{10,11... | collective-permute-start | bytes 638984 | tf_op jit(solution)/shard_map/ppermute | solution.py:19
  168.2 16.9 %collective-permute-start.10 = (bf16[8,2,32,416]{3,2,0,1:T(8,128)(2,1)}, bf16[8,2,32,416]{3,2,0,1:T(8,128)(2,1)S(1)}, u32[]{:S(2)}, u32[]{:S(2)}) collective-permute-start(bf16[8,2,32,416]{3,2,0,1:T(8,128)(2,1)} %bitcast_dynamic-update-slice_fusion.12), channel_id=1, source_target_pairs={{0,16},{16,32},{32,48},{48,0},{1,17},{17,33},{33,49},{49,1},{2,18}... | collective-permute-start | bytes 1277960 | tf_op jit(solution)/shard_map/ppermute | solution.py:16
  176.6 48.9 %collective-permute-start.11 = (bf16[8,2,32,416]{3,2,0,1:T(8,128)(2,1)}, bf16[8,2,32,416]{3,2,0,1:T(8,128)(2,1)}, u32[]{:S(2)}, u32[]{:S(2)}) collective-permute-start(bf16[8,2,32,416]{3,2,0,1:T(8,128)(2,1)} %bitcast_dynamic-update-slice_fusion.12), channel_id=1, source_target_pairs={{0,32},{16,48},{32,0},{48,16},{1,33},{17,49},{33,1},{49,17},{2,34}... | collective-permute-start | bytes 1277960 | tf_op jit(solution)/shard_map/ppermute | solution.py:16
  180.9 46.6 %collective-permute-start.12 = (bf16[8,2,32,416]{3,2,0,1:T(8,128)(2,1)}, bf16[8,2,32,416]{3,2,0,1:T(8,128)(2,1)}, u32[]{:S(2)}, u32[]{:S(2)}) collective-permute-start(bf16[8,2,32,416]{3,2,0,1:T(8,128)(2,1)} %bitcast_dynamic-update-slice_fusion.12), channel_id=1, source_target_pairs={{0,48},{16,0},{32,16},{48,32},{1,49},{17,1},{33,17},{49,33},{2,50}... | collective-permute-start | bytes 1277960 | tf_op jit(solution)/shard_map/ppermute | solution.py:16
  185.2 1.3 copy-start.2
  206.0 5.4 %copy-start = (bf16[8,2,2,1,2,32,416]{6,5,0,4,2,1,3:T(8,128)(2,1)}, bf16[8,2,2,1,2,32,416]{6,5,0,4,2,1,3:T(8,128)(2,1)S(1)}, u32[]{:S(2)}) copy-start(bf16[8,2,2,1,2,32,416]{6,5,0,4,2,1,3:T(8,128)(2,1)S(1)} %copy.79) | copy-start | bytes 5111812
  206.0 4.6 %copy-start.7 = (bf16[4,1,512,416]{2,1,3,0:T(2,128)(2,1)S(1)}, bf16[4,1,512,416]{2,1,3,0:T(2,128)(2,1)}, u32[]{:S(2)}) copy-start(bf16[4,1,512,416]{2,1,3,0:T(2,128)(2,1)} %get-tuple-element.17) | copy-start | bytes 5111812
  206.2 7.2 %collective-permute-start.8 = (bf16[2,8,32,416]{3,2,1,0:T(8,128)(2,1)S(1)}, bf16[2,8,32,416]{3,2,1,0:T(8,128)(2,1)S(1)}, u32[]{:S(2)}, u32[]{:S(2)}) collective-permute-start(bf16[2,8,32,416]{3,2,1,0:T(8,128)(2,1)S(1)} %pad_maximum_fusion.1), channel_id=1, source_target_pairs={{0,1},{1,0},{2,3},{3,2},{4,5},{5,4},{6,7},{7,6},{8,9},{9,8},{10,11... | collective-permute-start | bytes 1277960 | tf_op jit(solution)/shard_map/ppermute | solution.py:19
  210.7 2.0 copy-start.6
  212.6 2.3 copy-start.8
  214.9 2.0 copy-start.5
  218.7 32.1 %all-to-all-start.3 = ((bf16[32,32,512]{2,1,0:T(8,128)(2,1)}), bf16[32,32,512]{2,1,0:T(8,128)(2,1)S(1)}, u32[]{:S(2)}, u32[]{:S(2)}) async-start(bf16[32,32,512]{2,1,0:T(8,128)(2,1)} %bitcast.49), calls=%async_computation.3 | async-start | bytes 2097152 | tf_op jit(solution)/shard_map/all_to_all | solution.py:118
  225.5 3.9 %copy-start.1 = (bf16[8,2,2,1,2,32,416]{6,5,0,4,2,1,3:T(8,128)(2,1)S(1)}, bf16[8,2,2,1,2,32,416]{6,5,0,4,2,1,3:T(8,128)(2,1)}, u32[]{:S(2)}) copy-start(bf16[8,2,2,1,2,32,416]{6,5,0,4,2,1,3:T(8,128)(2,1)} %copy-done) | copy-start | bytes 5111812
  234.6 2.3 copy-start.3
  234.6 3.0 %copy-start.4 = (bf16[8,2,2,1,2,32,416]{6,5,4,3,2,1,0:T(8,128)(2,1)S(1)}, bf16[8,2,2,1,2,32,416]{6,5,4,3,2,1,0:T(8,128)(2,1)}, u32[]{:S(2)}) copy-start(bf16[8,2,2,1,2,32,416]{6,5,4,3,2,1,0:T(8,128)(2,1)} %get-tuple-element.11) | copy-start | bytes 5111812
  251.5 4.2 %copy-start.9 = (bf16[8,2,4,32,416]{4,3,2,1,0:T(8,128)(2,1)S(1)}, bf16[8,2,4,32,416]{4,3,2,1,0:T(8,128)(2,1)}, u32[]{:S(2)}) copy-start(bf16[8,2,4,32,416]{4,3,2,1,0:T(8,128)(2,1)} %copy.97) | copy-start | bytes 5111812
  251.5 4.2 %copy-start.12 = (bf16[2048,1024]{1,0:T(8,128)(2,1)S(1)}, bf16[2048,1024]{1,0:T(8,128)(2,1)}, u32[]{:S(2)}) copy-start(bf16[2048,1024]{1,0:T(8,128)(2,1)} %all-gather.4.cloned.1.call-done) | copy-start | bytes 12582916
Sparse Core Ops, SparseCore 0:
  11.7 126.9 all-gather.5
  147.0 45.0 all-gather.3

commit v2 on v1

v2 whole, which is shorter than its diff:
```python
import functools
import jax
import jax.numpy as jnp
from jax import lax
from jax.experimental import pallas as pl
from jax.experimental.pallas import tpu as pltpu
from jax.sharding import Mesh, PartitionSpec as P

BF = jnp.bfloat16
F32 = jnp.float32
NT = (((1,), (1,)), ((), ()))
TN = (((0,), (0,)), ((), ()))


def tied(value, *others):
    return lax.optimization_barrier((value, *others))[0]


def back(hidden_grad, gate_b, up_b):
    gate, up, grad = gate_b.astype(F32), up_b.astype(F32), hidden_grad.astype(F32)
    sig = 1.0 / (1.0 + jnp.exp(-gate))
    silu = gate * sig
    gate_grad = (grad * up * sig * (1.0 + gate * (1.0 - sig))).astype(BF)
    return gate_grad, (grad * silu).astype(BF), (silu * up).astype(BF)


def hidden_kernel(nx, x_ref, got_ref, *refs):
    own, other, out_ref = refs[:nx], refs[nx : 2 * nx], refs[2 * nx]
    ny, two_part, units = out_ref.shape
    part = two_part // 2
    for half, blocks in enumerate((own, other)):
        total = None
        for s in range(nx):
            left = got_ref[lax.rem(x_ref[0] + nx - s, nx)]
            term = lax.dot_general(left, blocks[s][...], NT, preferred_element_type=F32)
            total = term if total is None else total + term
        out_ref[:, half * part : (half + 1) * part, :] = total.astype(BF).reshape(ny, part, units)


def input_kernel(hg_ref, own_ref, other_ref, w_own, w_other, out_ref, grads):
    nx, ny, two_part, units = hg_ref.shape
    part = two_part // 2
    total = None
    for half, (saved, w) in enumerate(((own_ref, w_own), (other_ref, w_other))):
        for x in range(nx):
            hg = hg_ref[x, :, half * part : (half + 1) * part, :].reshape(ny * part, units)
            both = saved[:, x // 2, x % 2].reshape(ny * part, 2 * units)
            gate_grad, up_grad, _ = back(hg, both[:, :units], both[:, units:])
            grads[half, :, x, :, :units] = gate_grad.reshape(ny, part, units)
            grads[half, :, x, :, units:] = up_grad.reshape(ny, part, units)
        left = grads[half].reshape(ny * nx * part, 2 * units)
        term = jnp.dot(left, w[...], preferred_element_type=F32)
        total = term if total is None else total + term
    out_ref[...] = total.astype(BF)


def down_kernel(scale, rows_ref, saved_ref, out_ref):
    units, width = out_ref.shape
    gate = saved_ref[:, :units].astype(F32)
    up = saved_ref[:, units:].astype(F32)
    hidden = (gate * (1.0 / (1.0 + jnp.exp(-gate))) * up).astype(BF)
    out = lax.dot_general(hidden, rows_ref[:, :width], TN, preferred_element_type=F32)
    out_ref[...] = (out * scale).astype(BF)


def weight_kernel(scale, place_ref, rows_ref, saved_ref, hg_ref, swapped_ref, *refs):
    gate_out, up_out, gate_all, up_all = refs
    nx, ny, two_part, units = hg_ref.shape
    part, width = two_part // 2, gate_out.shape[1]
    for half in range(2):
        core = place_ref[0] if half == 0 else 1 - place_ref[0]
        for x in range(nx):
            hg = hg_ref[x, :, :part, :] if half == 0 else swapped_ref[x]
            both = saved_ref[:, pl.ds(core, 1), x // 2, x % 2].reshape(ny * part, 2 * units)
            results = back(hg.reshape(ny * part, units), both[:, :units], both[:, units:])
            for ref, v in zip((gate_all, up_all), results):
                ref[:, pl.ds(core, 1), x] = v.reshape(ny, 1, part, units)
    inputs = rows_ref[:, width:]
    for out_ref, ref in ((gate_out, gate_all), (up_out, up_all)):
        left = ref[...].reshape(rows_ref.shape[0], units)
        out = lax.dot_general(left, inputs, TN, preferred_element_type=F32)
        out_ref[...] = (out * scale).astype(BF)


def call(kernel, out_shape, scratch, flops, *args):
    outs = [jax.ShapeDtypeStruct(shape, BF) for shape in out_shape]
    spaces = [pltpu.SMEM if a.dtype == jnp.int32 else pltpu.VMEM for a in args]
    return pl.pallas_call(
        kernel,
        out_shape=outs,
        in_specs=[pl.BlockSpec(memory_space=space) for space in spaces],
        out_specs=[pl.BlockSpec(memory_space=pltpu.VMEM)] * len(outs),
        scratch_shapes=[pltpu.VMEM(shape, BF) for shape in scratch],
        compiler_params=pltpu.CompilerParams(vmem_limit_bytes=48 * 1024 * 1024),
        cost_estimate=pl.CostEstimate(
            flops=flops, bytes_accessed=sum(a.size * 2 for a in args), transcendentals=0
        ),
    )(*args)


def make_body(ny, nx, nz):
    def shift_x(v, s):
        return lax.ppermute(v, "x", [(i, (i + s) % nx) for i in range(nx)])

    def swap_core(v):
        return lax.ppermute(v, "core", [(0, 1), (1, 0)])

    def body(inputs, out_grad, gate_pre, up_pre, w_gate, w_up, w_down, segment_ids):
        x, core = lax.axis_index("x"), lax.axis_index("core")
        place = jnp.stack([x]).astype(jnp.int32)
        tokens, width = inputs.shape
        units = w_down.shape[0]
        part = tokens // nx
        total = tokens * nz * 2
        scale = total ** (-0.5)

        down = [w_down] + [shift_x(w_down, s) for s in range(1, nx)]
        down_other = [swap_core(v) for v in down]
        both_w = jnp.concatenate([w_gate.T, w_up.T], axis=0)
        w_other = swap_core(both_w)

        saved = lax.all_gather(
            jnp.concatenate([gate_pre, up_pre], axis=1), ("y", "x"), axis=0
        ).reshape(ny, 2, nx // 2, 2, part, 2 * units)

        keep = (segment_ids % 2 == 1).astype(BF)
        masked = out_grad * keep[:, None]
        pieces = jnp.broadcast_to(
            (tied(out_grad) * keep[:, None]).reshape(nx, 1, part, width), (nx, nz, part, width)
        ).reshape(nx * nz * part, width)
        got = lax.all_to_all(pieces, ("x", "z"), 0, 0, tiled=True)
        got = got.reshape(nx, nz * part, width)

        (hidden_part,) = call(
            functools.partial(hidden_kernel, nx),
            [(ny, 2 * part, units)], [], 2 * total * units * width // 2,
            place, got, *down, *down_other,
        )
        rows = lax.all_gather(
            tied(jnp.concatenate([masked, inputs], axis=1), hidden_part),
            ("z", "core"), axis=0, tiled=True,
        )

        def spread(v, axis, count):
            shape = (count,) + v.shape
            copies = jnp.broadcast_to(v[None], shape).reshape((-1,) + v.shape[1:])
            return lax.all_to_all(copies, axis, 0, 0, tiled=True).reshape(shape)

        terms = lax.all_to_all(
            hidden_part.reshape(ny * 2 * part, units), "y", 0, 0, tiled=True
        ).reshape(ny, 2 * part, units)
        hidden_sum = jnp.sum(terms.astype(F32), axis=0).astype(BF)
        hidden_all = spread(spread(hidden_sum, "y", ny), "x", nx)
        swapped = swap_core(hidden_all[:, :, part:])

        def saved_at(k):
            return lax.dynamic_index_in_dim(saved, k, 1, keepdims=False)

        saved_other = swap_core(saved_at(1 - core))
        (input_part,) = call(
            input_kernel, [(nz * nx * part, width)], [(2, ny, nx, part, 2 * units)],
            2 * total * units * width,
            hidden_all, saved_at(core), saved_other, both_w, w_other,
        )
        input_terms = lax.all_to_all(tied(input_part, swapped), "z", 0, 0, tiled=True)

        (grad_down,) = call(
            functools.partial(down_kernel, scale),
            [(units, width)], [], 2 * total * units * width,
            rows, saved.reshape(total, 2 * units),
        )
        grad_gate, grad_up = call(
            functools.partial(weight_kernel, scale),
            [(units, width)] * 2, [(ny, 2, nx, part, units)] * 2, 4 * total * units * width,
            jnp.stack([core]).astype(jnp.int32), rows, saved, hidden_all, swapped,
        )

        input_terms = tied(input_terms, grad_gate, grad_up, grad_down)
        input_terms = input_terms.reshape(nz, tokens, width)
        in_grad = jnp.sum(input_terms.astype(F32), axis=0).astype(BF)
        return in_grad, grad_gate.T, grad_up.T, grad_down

    return body


def solution(mesh):
    nx = 4 if mesh.shape["row"] >= 16 else 2
    ny, nz = mesh.shape["row"] // nx, mesh.shape["col"] // 2
    grid = Mesh(mesh.devices.reshape(ny, nx, nz, 2), ("y", "x", "z", "core"))
    row, col = ("y", "x"), ("z", "core")
    return jax.shard_map(
        make_body(ny, nx, nz),
        mesh=grid,
        in_specs=(
            P(col, row), P(col, row), P(row, col), P(row, col),
            P(row, col), P(row, col), P(col, row), P(col),
        ),
        out_specs=(P(col, row), P(row, col), P(row, col), P(col, row)),
        check_vma=False,
    )
```

time: 270 us -> 212 us (0.79)
  local copies, waits for them, and re-layouts: 66.1 us -> 12.1 us
  blocking collectives: 0 us -> 52.7 us
  waiting for transfers between devices: 82.4 us -> 44.8 us
  Pallas kernels: 0 us -> 24.4 us
  starting transfers between devices: 74.2 us -> 57.3 us
  matrix products: 16.2 us -> 0 us
  other arithmetic: 12.9 us -> 5.01 us
    all_to_all x0 -> x2, blocking collectives: none -> 52.7 us  [the longest x1 28.3 us: body(): lax.all_to_all(hidden_part.reshape(ny * 2 * part, units), 'y', 0, 0, tile...]
    ppermute x9 -> x3, waiting for transfers between devices: 61 us -> 18.2 us  [shift_x(): return lax.ppermute(v, 'x', [(i, (i + s) % nx) for i in range(nx)])]
    pallas_call x0 -> x4, Pallas kernels: none -> 24.4 us  [call(): pl.pallas_call(kernel, out_shape=outs, in_specs=[pl.BlockSpec(memory_spac...]
    ppermute x9 -> x3, starting transfers between devices: 29.8 us -> 10.5 us  [shift_x(): return lax.ppermute(v, 'x', [(i, (i + s) % nx) for i in range(nx)])]
    slice x5 -> x1, local copies, waits for them, and re-layouts: 17.9 us -> 0.07 us  [body(): swapped = swap_core(hidden_all[:, :, part:])]
    dot_general x9 -> x0, matrix products: 16.2 us -> none  [the longest x3 7.91 us: weight_grad(): jnp.einsum(spec, a, b, preferred_element_type=F32) * scale]
    reshape x2 -> x0, local copies, waits for them, and re-layouts: 15.3 us -> none  [partial_input(): w = w.reshape(nx, 2, width, units)]
    dynamic_update_slice x14 -> x0, local copies, waits for them, and re-layouts: 15 us -> none  [the longest x12 12.6 us: place_x(): lax.dynamic_update_slice_in_dim(out, jnp.expand_dims(block, axis), (x - s...]
  transfers between devices with their start and end apart: 19 -> 15, of which waited for: 7 -> 5; matrix products, arithmetic and copies ran while one was open for 30% -> 5% of each run, Pallas kernels for 0% -> 12%
where the time goes in v2:
time: 212 us; the launch traced here: 211 us
  starting transfers between devices  57.3 us (27%)
  blocking collectives  52.7 us (25%)
  waiting for transfers between devices  44.8 us (21%)
  Pallas kernels  24.4 us (12%)
  between operations  14.3 us (7%)
  local copies, waits for them, and re-layouts  12.1 us (6%)
  other arithmetic  5.01 us (2%)
    all_to_all x1, blocking collectives, body(): lax.all_to_all(hidden_part.reshape(ny * 2 * part, units), 'y', 0, 0, tile...  28.3 us
    all_to_all x1, blocking collectives, spread(): return lax.all_to_all(copies, axis, 0, 0, tiled=True).reshape(shape)  24.5 us
    pallas_call x4, Pallas kernels, call(): pl.pallas_call(kernel, out_shape=outs, in_specs=[pl.BlockSpec(memory_spac...  24.4 us
    ppermute x7, starting transfers between devices, swap_core(): return lax.ppermute(v, 'core', [(0, 1), (1, 0)])  23.3 us
    ppermute x3, waiting for transfers between devices, shift_x(): return lax.ppermute(v, 'x', [(i, (i + s) % nx) for i in range(nx)])  18.2 us
    all_to_all x1, starting transfers between devices, body(): got = lax.all_to_all(pieces, ('x', 'z'), 0, 0, tiled=True)  13.7 us
    all_to_all x1, waiting for transfers between devices, spread(): return lax.all_to_all(copies, axis, 0, 0, tiled=True).reshape(shape)  13.4 us
    all_to_all x1, waiting for transfers between devices, body(): lax.all_to_all(tied(input_part, swapped), 'z', 0, 0, tiled=True)  12.8 us
  transfers between devices with their start and end apart: 15, of which 5 were waited for; matrix products, arithmetic and copies ran while one was open for 5% of the time, Pallas kernels for 12%

profile of v2, /device:TPU:1, one launch (start us, length us, event | category | flops | bytes accessed | tf_op | source)
XLA Modules:
  0.0 210.6 jit_solution(12218071473636803498)
XLA Ops:
  7.2 1.6 pad_maximum_fusion.2
  9.5 1.0 broadcast_multiply_fusion
  10.6 1.1 broadcast_in_dim.9
  11.7 13.7 %all-to-all-start = ((bf16[32,32,512]{2,1,0:T(8,128)(2,1)}), bf16[32,32,512]{2,1,0:T(8,128)(2,1)S(1)}, u32[]{:S(2)}, u32[]{:S(2)}) async-start(bf16[32,32,512]{2,1,0:T(8,128)(2,1)} %bitcast.2), calls=%async_computation | async-start | bytes 2097152 | tf_op jit(solution)/shard_map/all_to_all | solution.py:131
  25.5 3.1 %collective-permute-start = (bf16[416,512]{1,0:T(8,128)(2,1)S(1)}, bf16[416,512]{1,0:T(8,128)(2,1)S(1)}, u32[]{:S(2)}, u32[]{:S(2)}) collective-permute-start(bf16[416,512]{1,0:T(8,128)(2,1)S(1)} %copy-done.6), channel_id=1, source_target_pairs={{0,16},{16,32},{32,48},{48,0},{1,17},{17,33},{33,49},{49,1},{2,18}... | collective-permute-start | bytes 1277960 | tf_op jit(solution)/shard_map/ppermute | solution.py:103
  28.6 4.3 %collective-permute-start.1 = (bf16[416,512]{1,0:T(8,128)(2,1)S(1)}, bf16[416,512]{1,0:T(8,128)(2,1)S(1)}, u32[]{:S(2)}, u32[]{:S(2)}) collective-permute-start(bf16[416,512]{1,0:T(8,128)(2,1)S(1)} %copy-done.6), channel_id=1, source_target_pairs={{0,32},{16,48},{32,0},{48,16},{1,33},{17,49},{33,1},{49,17},{2,34}... | collective-permute-start | bytes 1277960 | tf_op jit(solution)/shard_map/ppermute | solution.py:103
  33.0 3.1 %collective-permute-start.2 = (bf16[416,512]{1,0:T(8,128)(2,1)S(1)}, bf16[416,512]{1,0:T(8,128)(2,1)S(1)}, u32[]{:S(2)}, u32[]{:S(2)}) collective-permute-start(bf16[416,512]{1,0:T(8,128)(2,1)S(1)} %copy-done.6), channel_id=1, source_target_pairs={{0,48},{16,0},{32,16},{48,32},{1,49},{17,1},{33,17},{49,33},{2,50}... | collective-permute-start | bytes 1277960 | tf_op jit(solution)/shard_map/ppermute | solution.py:103
  36.0 4.0 %collective-permute-start.3 = (bf16[416,512]{1,0:T(8,128)(2,1)S(1)}, bf16[416,512]{1,0:T(8,128)(2,1)S(1)}, u32[]{:S(2)}, u32[]{:S(2)}) collective-permute-start(bf16[416,512]{1,0:T(8,128)(2,1)S(1)} %copy-done.6), channel_id=1, source_target_pairs={{0,1},{1,0},{2,3},{3,2},{4,5},{5,4},{6,7},{7,6},{8,9},{9,8},{10,11... | collective-permute-start | bytes 1277960 | tf_op jit(solution)/shard_map/ppermute | solution.py:106
  40.0 11.5 %collective-permute-done.refs_1_ = bf16[416,512]{1,0:T(8,128)(2,1)S(1)} collective-permute-done((bf16[416,512]{1,0:T(8,128)(2,1)S(1)}, bf16[416,512]{1,0:T(8,128)(2,1)S(1)}, u32[]{:S(2)}, u32[]{:S(2)}) %collective-permute-start) | collective-permute-done | bytes 426016 | tf_op jit(solution)/shard_map/ppermute | solution.py:103
  51.5 2.6 %collective-permute-start.4 = (bf16[416,512]{1,0:T(8,128)(2,1)S(1)}, bf16[416,512]{1,0:T(8,128)(2,1)}, u32[]{:S(2)}, u32[]{:S(2)}) collective-permute-start(bf16[416,512]{1,0:T(8,128)(2,1)S(1)} %collective-permute-done.refs_1_), channel_id=1, source_target_pairs={{0,1},{1,0},{2,3},{3,2},{4,5},{5,4},{6,7},{7,6},{8,9},{9,8},{10,11... | collective-permute-start | bytes 1277960 | tf_op jit(solution)/shard_map/ppermute | solution.py:106
  54.2 6.6 %collective-permute-done.1.refs_2_ = bf16[416,512]{1,0:T(8,128)(2,1)S(1)} collective-permute-done((bf16[416,512]{1,0:T(8,128)(2,1)S(1)}, bf16[416,512]{1,0:T(8,128)(2,1)S(1)}, u32[]{:S(2)}, u32[]{:S(2)}) %collective-permute-start.1) | collective-permute-done | bytes 426016 | tf_op jit(solution)/shard_map/ppermute | solution.py:103
  60.8 3.3 %collective-permute-start.5 = (bf16[416,512]{1,0:T(8,128)(2,1)S(1)}, bf16[416,512]{1,0:T(8,128)(2,1)}, u32[]{:S(2)}, u32[]{:S(2)}) collective-permute-start(bf16[416,512]{1,0:T(8,128)(2,1)S(1)} %collective-permute-done.1.refs_2_), channel_id=1, source_target_pairs={{0,1},{1,0},{2,3},{3,2},{4,5},{5,4},{6,7},{7,6},{8,9},{9,8},{10,11... | collective-permute-start | bytes 1277960 | tf_op jit(solution)/shard_map/ppermute | solution.py:106
  64.1 1.9 collective-permute-start.6
  67.9 1.0 copy-done.8
  68.9 2.5 %shard_map.111 = bf16[8,64,416]{2,1,0:T(8,128)(2,1)S(1)} custom-call(s32[1]{0:T(128)} %bitcast.x_ref, bf16[4,256,512]{2,1,0:T(8,128)(2,1)S(1)} %bitcast.24, bf16[416,512]{1,0:T(8,128)(2,1)S(1)} %copy-done.6, bf16[416,512]{1,0:T(8,128)(2,1)S(1)} %collective-permute-done.refs_1_, bf16[416,512]{1,0:T(8,128)(2,1)S(1)} %collective-permute-done.1.refs_2_, ...), custom_call_target="tpu_custom_call" | custom-call | flops 436207616 | bytes 4456450 | tf_op jit(solution)/shard_map/pallas_call | solution.py:88
  71.4 28.3 %all_to_all.38 = bf16[8,64,416]{2,1,0:T(8,128)(2,1)S(1)} all-to-all(bf16[8,64,416]{2,1,0:T(8,128)(2,1)S(1)} %shard_map.111), channel_id=1, replica_groups=mesh['y'=8,'x'=4,'z'=8,'core'=2] {'y'}, dimensions={0} | all-to-all | bytes 851968 | tf_op jit(solution)/shard_map/all_to_all | solution.py:149
  99.9 24.5 %all_to_all.39 = bf16[8,64,416]{2,1,0:T(8,128)(2,1)S(1)} all-to-all(bf16[8,64,416]{2,1,0:T(8,128)(2,1)S(1)} %broadcast_in_dim.10), channel_id=1, replica_groups=mesh['y'=8,'x'=4,'z'=8,'core'=2] {'y'}, dimensions={0} | all-to-all | bytes 851968 | tf_op jit(solution)/shard_map/all_to_all | solution.py:147
  124.3 1.6 broadcast_in_dim.11
  125.9 3.6 %all-to-all-start.3 = ((bf16[32,64,416]{2,1,0:T(8,128)(2,1)}), bf16[32,64,416]{2,1,0:T(8,128)(2,1)S(1)}, u32[]{:S(2)}, u32[]{:S(2)}) async-start(bf16[32,64,416]{2,1,0:T(8,128)(2,1)} %bitcast.25), calls=%async_computation.3 | async-start | bytes 4194304 | tf_op jit(solution)/shard_map/all_to_all | solution.py:147
  129.6 4.4 %dynamic-slice_bitcast_fusion = (bf16[8,2,2,32,832]{4,3,2,1,0:T(8,128)(2,1)}, bf16[8,2,2,32,832]{4,3,2,1,0:T(8,128)(2,1)}) fusion(bf16[8,2,2,2,32,832]{5,4,3,2,1,0:T(8,128)(2,1)} %bitcast.19, s32[]{:T(128)S(6)} %select_n.16, s32[]{:T(128)S(6)} %select_n.15), kind=kLoop, calls=%fused_computation | loop fusion | bytes 6815752 | tf_op jit(solution)/shard_map/jit(dynamic_index_in_dim)/squeeze | solution.py:157
  134.0 4.2 %collective-permute-start.7 = (bf16[8,2,2,32,832]{4,3,2,1,0:T(8,128)(2,1)}, bf16[8,2,2,32,832]{4,3,2,1,0:T(8,128)(2,1)}, u32[]{:S(2)}, u32[]{:S(2)}) collective-permute-start(bf16[8,2,2,32,832]{4,3,2,1,0:T(8,128)(2,1)} %get-tuple-element.14), channel_id=1, source_target_pairs={{0,1},{1,0},{2,3},{3,2},{4,5},{5,4},{6,7},{7,6},{8,9},{9,8},{10,11... | collective-permute-start | bytes 5111816 | tf_op jit(solution)/shard_map/ppermute | solution.py:106
  138.3 1.9 collective-permute-start.8
  140.2 13.4 %all-to-all-done.3 = bf16[32,64,416]{2,1,0:T(8,128)(2,1)S(1)} async-done(((bf16[32,64,416]{2,1,0:T(8,128)(2,1)}), bf16[32,64,416]{2,1,0:T(8,128)(2,1)S(1)}, u32[]{:S(2)}, u32[]{:S(2)}) %all-to-all-start.3) | async-done | bytes 1703968 | tf_op jit(solution)/shard_map/all_to_all | solution.py:147
  153.7 5.4 %collective-permute-start.9 = (bf16[4,8,32,416]{3,2,1,0:T(8,128)(2,1)S(1)}, bf16[4,8,32,416]{3,2,1,0:T(8,128)(2,1)S(1)}, u32[]{:S(2)}, u32[]{:S(2)}) collective-permute-start(bf16[4,8,32,416]{3,2,1,0:T(8,128)(2,1)S(1)} %slice.4), channel_id=1, source_target_pairs={{0,1},{1,0},{2,3},{3,2},{4,5},{5,4},{6,7},{7,6},{8,9},{9,8},{10,11... | collective-permute-start | bytes 2555912 | tf_op jit(solution)/shard_map/ppermute | solution.py:106
  159.1 7.5 %shard_map.112 = bf16[1024,512]{1,0:T(8,128)(2,1)} custom-call(bf16[4,8,64,416]{3,2,1,0:T(8,128)(2,1)} %bitcast.22, bf16[8,2,2,32,832]{4,3,2,1,0:T(8,128)(2,1)S(1)} %copy-done.3, bf16[8,2,2,32,832]{4,3,2,1,0:T(8,128)(2,1)} %collective-permute-done.7.other_ref, bf16[832,512]{1,0:T(8,128)(2,1)S(1)} %pad_maximum_fusion.w_own, ...), custom_call_target="tpu_custom_call" | custom-call | flops 872415232 | bytes 6815744 | tf_op jit(solution)/shard_map/pallas_call | solution.py:88
  166.6 1.0 copy-done.4
  167.6 6.1 %all-to-all-start.4 = ((bf16[8,128,512]{2,1,0:T(8,128)(2,1)}), bf16[8,128,512]{2,1,0:T(8,128)(2,1)S(1)}, u32[]{:S(2)}, u32[]{:S(2)}) async-start(bf16[8,128,512]{2,1,0:T(8,128)(2,1)} %bitcast.11), calls=%async_computation.4 | async-start | bytes 2097152 | tf_op jit(solution)/shard_map/all_to_all | solution.py:165
  173.7 2.0 copy-done
  175.8 5.6 %shard_map.114 = bf16[416,512]{1,0:T(8,128)(2,1)} custom-call(bf16[2048,1024]{1,0:T(8,128)(2,1)} %all-gather.4.cloned.1.call-done.rows_ref, bf16[2048,832]{1,0:T(8,128)(2,1)S(1)} %copy-done), custom_call_target="tpu_custom_call" | custom-call | flops 872415232 | bytes 7602176 | tf_op jit(solution)/shard_map/pallas_call | solution.py:88
  181.3 8.8 %shard_map.113 = (bf16[416,512]{1,0:T(8,128)(2,1)}, bf16[416,512]{1,0:T(8,128)(2,1)}) custom-call(s32[1]{0:T(128)} %bitcast.13.place_ref, bf16[2048,1024]{1,0:T(8,128)(2,1)} %all-gather.4.cloned.1.call-done.rows_ref, bf16[8,2,2,2,32,832]{5,4,3,2,1,0:T(8,128)(2,1)} %bitcast.20, bf16[4,8,64,416]{3,2,1,0:T(8,128)(2,1)S(1)} %bitcast.23, ...), custom_call_target="tpu_custom_call" | custom-call | flops 1744830464 | bytes 10158082 | tf_op jit(solution)/shard_map/pallas_call | solution.py:88
  190.2 12.8 %all-to-all-done.4 = bf16[8,128,512]{2,1,0:T(8,128)(2,1)S(1)} async-done(((bf16[8,128,512]{2,1,0:T(8,128)(2,1)}), bf16[8,128,512]{2,1,0:T(8,128)(2,1)S(1)}, u32[]{:S(2)}, u32[]{:S(2)}) %all-to-all-start.4) | async-done | bytes 1048608 | tf_op jit(solution)/shard_map/all_to_all | solution.py:165
  203.0 0.8 reduce_sum.25
  (42 shorter events, 3.0 us)
Async XLA Ops:
  7.2 122.4 %all-gather.6.cloned.1.call-start = ((), (), s32[]{:S(2)}) async-start(), calls=%async_computation.6 | async-start | bytes 3784704 | tf_op jit(solution)/shard_map/all_gather | solution.py:122
  9.5 15.9 %copy-start.6 = (bf16[416,512]{1,0:T(8,128)(2,1)S(1)}, bf16[416,512]{1,0:T(8,128)(2,1)}, u32[]{:S(2)}) copy-start(bf16[416,512]{1,0:T(8,128)(2,1)} %refs_0_.1) | copy-start | bytes 1277956
  9.5 56.5 %copy-start.11 = (bf16[128,512]{1,0:T(8,128)(2,1)S(1)}, bf16[128,512]{1,0:T(8,128)(2,1)}, u32[]{:S(2)}) copy-start(bf16[128,512]{1,0:T(8,128)(2,1)} %param.8) | copy-start | bytes 393220
  11.7 56.2 %all-to-all-start = ((bf16[32,32,512]{2,1,0:T(8,128)(2,1)}), bf16[32,32,512]{2,1,0:T(8,128)(2,1)S(1)}, u32[]{:S(2)}, u32[]{:S(2)}) async-start(bf16[32,32,512]{2,1,0:T(8,128)(2,1)} %bitcast.2), calls=%async_computation | async-start | bytes 2097152 | tf_op jit(solution)/shard_map/all_to_all | solution.py:131
  25.4 148.3 %all-gather.4.cloned.1.call-start = ((), (), s32[]{:S(2)}) async-start(), calls=%async_computation.5 | async-start | bytes 4456448 | tf_op jit(solution)/shard_map/all_gather | solution.py:139
  25.5 26.1 %collective-permute-start = (bf16[416,512]{1,0:T(8,128)(2,1)S(1)}, bf16[416,512]{1,0:T(8,128)(2,1)S(1)}, u32[]{:S(2)}, u32[]{:S(2)}) collective-permute-start(bf16[416,512]{1,0:T(8,128)(2,1)S(1)} %copy-done.6), channel_id=1, source_target_pairs={{0,16},{16,32},{32,48},{48,0},{1,17},{17,33},{33,49},{49,1},{2,18}... | collective-permute-start | bytes 1277960 | tf_op jit(solution)/shard_map/ppermute | solution.py:103
  28.6 32.2 %collective-permute-start.1 = (bf16[416,512]{1,0:T(8,128)(2,1)S(1)}, bf16[416,512]{1,0:T(8,128)(2,1)S(1)}, u32[]{:S(2)}, u32[]{:S(2)}) collective-permute-start(bf16[416,512]{1,0:T(8,128)(2,1)S(1)} %copy-done.6), channel_id=1, source_target_pairs={{0,32},{16,48},{32,0},{48,16},{1,33},{17,49},{33,1},{49,17},{2,34}... | collective-permute-start | bytes 1277960 | tf_op jit(solution)/shard_map/ppermute | solution.py:103
  33.0 31.1 %collective-permute-start.2 = (bf16[416,512]{1,0:T(8,128)(2,1)S(1)}, bf16[416,512]{1,0:T(8,128)(2,1)S(1)}, u32[]{:S(2)}, u32[]{:S(2)}) collective-permute-start(bf16[416,512]{1,0:T(8,128)(2,1)S(1)} %copy-done.6), channel_id=1, source_target_pairs={{0,48},{16,0},{32,16},{48,32},{1,49},{17,1},{33,17},{49,33},{2,50}... | collective-permute-start | bytes 1277960 | tf_op jit(solution)/shard_map/ppermute | solution.py:103
  36.0 30.7 %collective-permute-start.3 = (bf16[416,512]{1,0:T(8,128)(2,1)S(1)}, bf16[416,512]{1,0:T(8,128)(2,1)S(1)}, u32[]{:S(2)}, u32[]{:S(2)}) collective-permute-start(bf16[416,512]{1,0:T(8,128)(2,1)S(1)} %copy-done.6), channel_id=1, source_target_pairs={{0,1},{1,0},{2,3},{3,2},{4,5},{5,4},{6,7},{7,6},{8,9},{9,8},{10,11... | collective-permute-start | bytes 1277960 | tf_op jit(solution)/shard_map/ppermute | solution.py:106
  51.5 16.0 %collective-permute-start.4 = (bf16[416,512]{1,0:T(8,128)(2,1)S(1)}, bf16[416,512]{1,0:T(8,128)(2,1)}, u32[]{:S(2)}, u32[]{:S(2)}) collective-permute-start(bf16[416,512]{1,0:T(8,128)(2,1)S(1)} %collective-permute-done.refs_1_), channel_id=1, source_target_pairs={{0,1},{1,0},{2,3},{3,2},{4,5},{5,4},{6,7},{7,6},{8,9},{9,8},{10,11... | collective-permute-start | bytes 1277960 | tf_op jit(solution)/shard_map/ppermute | solution.py:106
  60.8 6.7 %collective-permute-start.5 = (bf16[416,512]{1,0:T(8,128)(2,1)S(1)}, bf16[416,512]{1,0:T(8,128)(2,1)}, u32[]{:S(2)}, u32[]{:S(2)}) collective-permute-start(bf16[416,512]{1,0:T(8,128)(2,1)S(1)} %collective-permute-done.1.refs_2_), channel_id=1, source_target_pairs={{0,1},{1,0},{2,3},{3,2},{4,5},{5,4},{6,7},{7,6},{8,9},{9,8},{10,11... | collective-permute-start | bytes 1277960 | tf_op jit(solution)/shard_map/ppermute | solution.py:106
  64.1 3.8 %collective-permute-start.6 = (bf16[416,512]{1,0:T(8,128)(2,1)S(1)}, bf16[416,512]{1,0:T(8,128)(2,1)}, u32[]{:S(2)}, u32[]{:S(2)}) collective-permute-start(bf16[416,512]{1,0:T(8,128)(2,1)S(1)} %collective-permute-done.2.refs_3_), channel_id=1, source_target_pairs={{0,1},{1,0},{2,3},{3,2},{4,5},{5,4},{6,7},{7,6},{8,9},{9,8},{10,11... | collective-permute-start | bytes 1277960 | tf_op jit(solution)/shard_map/ppermute | solution.py:106
  66.8 0.8 copy-start.7
  67.9 1.0 copy-start.8
  125.9 27.7 %all-to-all-start.3 = ((bf16[32,64,416]{2,1,0:T(8,128)(2,1)}), bf16[32,64,416]{2,1,0:T(8,128)(2,1)S(1)}, u32[]{:S(2)}, u32[]{:S(2)}) async-start(bf16[32,64,416]{2,1,0:T(8,128)(2,1)} %bitcast.25), calls=%async_computation.3 | async-start | bytes 4194304 | tf_op jit(solution)/shard_map/all_to_all | solution.py:147
  129.6 8.6 %copy-start.9 = (bf16[512,416]{0,1:T(8,128)(2,1)S(1)}, bf16[512,416]{0,1:T(8,128)(2,1)}, u32[]{:S(2)}) copy-start(bf16[512,416]{0,1:T(8,128)(2,1)} %param.13) | copy-start | bytes 1277956
  129.6 8.6 %copy-start.10 = (bf16[512,416]{0,1:T(8,128)(2,1)S(1)}, bf16[512,416]{0,1:T(8,128)(2,1)}, u32[]{:S(2)}) copy-start(bf16[512,416]{0,1:T(8,128)(2,1)} %param.12) | copy-start | bytes 1277956
  134.0 25.1 %collective-permute-start.7 = (bf16[8,2,2,32,832]{4,3,2,1,0:T(8,128)(2,1)}, bf16[8,2,2,32,832]{4,3,2,1,0:T(8,128)(2,1)}, u32[]{:S(2)}, u32[]{:S(2)}) collective-permute-start(bf16[8,2,2,32,832]{4,3,2,1,0:T(8,128)(2,1)} %get-tuple-element.14), channel_id=1, source_target_pairs={{0,1},{1,0},{2,3},{3,2},{4,5},{5,4},{6,7},{7,6},{8,9},{9,8},{10,11... | collective-permute-start | bytes 5111816 | tf_op jit(solution)/shard_map/ppermute | solution.py:106
  138.3 20.8 %collective-permute-start.8 = (bf16[832,512]{1,0:T(8,128)(2,1)S(1)}, bf16[832,512]{1,0:T(8,128)(2,1)}, u32[]{:S(2)}, u32[]{:S(2)}) collective-permute-start(bf16[832,512]{1,0:T(8,128)(2,1)S(1)} %pad_maximum_fusion.w_own), channel_id=1, source_target_pairs={{0,1},{1,0},{2,3},{3,2},{4,5},{5,4},{6,7},{7,6},{8,9},{9,8},{10,11... | collective-permute-start | bytes 2555912 | tf_op jit(solution)/shard_map/ppermute | solution.py:106
  153.6 5.5 %copy-start.1 = (bf16[32,64,416]{2,1,0:T(8,128)(2,1)}, bf16[32,64,416]{2,1,0:T(8,128)(2,1)S(1)}, u32[]{:S(2)}) copy-start(bf16[32,64,416]{2,1,0:T(8,128)(2,1)S(1)} %all-to-all-done.3) | copy-start | bytes 5111812
  153.6 5.5 %copy-start.3 = (bf16[8,2,2,32,832]{4,3,2,1,0:T(8,128)(2,1)S(1)}, bf16[8,2,2,32,832]{4,3,2,1,0:T(8,128)(2,1)}, u32[]{:S(2)}) copy-start(bf16[8,2,2,32,832]{4,3,2,1,0:T(8,128)(2,1)} %get-tuple-element.15.own_ref) | copy-start | bytes 5111812
  153.7 12.9 %collective-permute-start.9 = (bf16[4,8,32,416]{3,2,1,0:T(8,128)(2,1)S(1)}, bf16[4,8,32,416]{3,2,1,0:T(8,128)(2,1)S(1)}, u32[]{:S(2)}, u32[]{:S(2)}) collective-permute-start(bf16[4,8,32,416]{3,2,1,0:T(8,128)(2,1)S(1)} %slice.4), channel_id=1, source_target_pairs={{0,1},{1,0},{2,3},{3,2},{4,5},{5,4},{6,7},{7,6},{8,9},{9,8},{10,11... | collective-permute-start | bytes 2555912 | tf_op jit(solution)/shard_map/ppermute | solution.py:106
  166.6 1.0 copy-start.4
  167.6 35.4 %all-to-all-start.4 = ((bf16[8,128,512]{2,1,0:T(8,128)(2,1)}), bf16[8,128,512]{2,1,0:T(8,128)(2,1)S(1)}, u32[]{:S(2)}, u32[]{:S(2)}) async-start(bf16[8,128,512]{2,1,0:T(8,128)(2,1)} %bitcast.11), calls=%async_computation.4 | async-start | bytes 2097152 | tf_op jit(solution)/shard_map/all_to_all | solution.py:165
  173.7 2.0 copy-start
  175.7 5.6 %copy-start.2 = (bf16[32,64,416]{2,1,0:T(8,128)(2,1)S(1)}, bf16[32,64,416]{2,1,0:T(8,128)(2,1)}, u32[]{:S(2)}) copy-start(bf16[32,64,416]{2,1,0:T(8,128)(2,1)} %copy-done.1) | copy-start | bytes 5111812
  175.8 5.6 %copy-start.5 = (bf16[4,8,32,416]{3,2,1,0:T(8,128)(2,1)S(1)}, bf16[4,8,32,416]{3,2,1,0:T(8,128)(2,1)}, u32[]{:S(2)}) copy-start(bf16[4,8,32,416]{3,2,1,0:T(8,128)(2,1)} %copy-done.4) | copy-start | bytes 2555908
Sparse Core Ops, SparseCore 0:
  11.7 111.6 all-gather.5
  126.1 45.4 all-gather.3

commit v3 on v2

v3 whole, which is shorter than its diff:
```python
import functools
import jax
import jax.numpy as jnp
from jax import lax
from jax.experimental import pallas as pl
from jax.experimental.pallas import tpu as pltpu
from jax.sharding import Mesh, PartitionSpec as P

BF = jnp.bfloat16
F32 = jnp.float32
NT = (((1,), (1,)), ((), ()))
TN = (((0,), (0,)), ((), ()))


def tied(value, *others):
    return lax.optimization_barrier((value, *others))[0]


def fetch(refs, bufs, sems):
    copies = [pltpu.make_async_copy(r, b, sems.at[i]) for i, (r, b) in enumerate(zip(refs, bufs))]
    for copy in copies:
        copy.start()
    return copies


def hidden_kernel(nx, x_ref, *refs):
    count = 2 * nx + 1
    sources, out_ref, bufs, sems = refs[:count], refs[-count - 2], refs[-count - 1 : -1], refs[-1]
    copies = fetch(sources, bufs, sems)
    ny, part, units = out_ref.shape[0], out_ref.shape[1], out_ref.shape[2] // 2
    copies[0].wait()
    for half in range(2):
        total = None
        for s in range(nx):
            i = 1 + half * nx + s
            copies[i].wait()
            left = bufs[0][lax.rem(x_ref[0] + nx - s, nx)]
            term = lax.dot_general(left, bufs[i][...], NT, preferred_element_type=F32)
            total = term if total is None else total + term
        total = total.astype(BF).reshape(ny, part, units)
        out_ref[:, :, half * units : (half + 1) * units] = total


def factor_kernel(core_ref, saved_ref, own_ref, send_ref, hidden_ref):
    ny, nx, part, units = own_ref.shape[1:]
    for half, ref in enumerate((own_ref, send_ref)):
        core = core_ref[0] if half == 0 else 1 - core_ref[0]

        for x in range(nx):
            both = saved_ref[:, pl.ds(core, 1), x].reshape(ny * part, 2 * units)
            gate, up = both[:, :units].astype(F32), both[:, units:].astype(F32)
            sig = 1.0 / (1.0 + jnp.exp(-gate))
            silu = gate * sig
            slope = (up * sig * (1.0 + gate * (1.0 - sig))).astype(BF)
            ref[0, :, x] = slope.reshape(ny, part, units)
            ref[1, :, x] = silu.astype(BF).reshape(ny, part, units)
            hidden = (silu * up).astype(BF).reshape(ny, 1, part, units)
            hidden_ref[:, pl.ds(core, 1), x] = hidden


def input_kernel(*refs):
    sources, (out_ref, send_ref, grads), bufs, sems = refs[:5], refs[6:9], refs[9:14], refs[14]
    copies = fetch(sources, bufs, sems)
    hg_ref = bufs[0]
    nx, ny, part, units = send_ref.shape
    copies[0].wait()
    total = None
    for half in range(2):
        factors, w = bufs[1 + 2 * half], bufs[2 + 2 * half]
        copies[1 + 2 * half].wait()

        for x in range(nx):
            hg = hg_ref[x, :, :, half * units : (half + 1) * units]
            if half == 1:
                send_ref[x] = hg
            grads[half, :, x, :, :units] = hg * factors[0, :, x]
            grads[half, :, x, :, units:] = hg * factors[1, :, x]
        copies[2 + 2 * half].wait()
        left = grads[half].reshape(ny * nx * part, 2 * units)
        term = jnp.dot(left, w[...], preferred_element_type=F32)
        total = term if total is None else total + term
    out_ref[...] = total.astype(BF)


def weight_kernel(scale, core_ref, rows_ref, hg_ref, swapped_ref, own_ref, send_ref, *refs):
    hidden_ref, gate_out, up_out, down_out, gate_all, up_all = refs
    nx, ny, part, units = swapped_ref.shape
    width = gate_out.shape[1]

    def dot(out_ref, a, b):
        out = lax.dot_general(
            a.reshape(rows_ref.shape[0], units), b, TN, preferred_element_type=F32
        )
        out_ref[...] = (out * scale).astype(BF)

    for half, factors in enumerate((own_ref, send_ref)):
        core = core_ref[0] if half == 0 else 1 - core_ref[0]

        for x in range(nx):
            hg = hg_ref[x, :, :, :units] if half == 0 else swapped_ref[x]
            gate_all[:, pl.ds(core, 1), x] = (hg * factors[0, :, x])[:, None]
            up_all[:, pl.ds(core, 1), x] = (hg * factors[1, :, x])[:, None]

    dot(down_out, hidden_ref[...], rows_ref[:, :width])
    dot(gate_out, gate_all[...], rows_ref[:, width:])
    dot(up_out, up_all[...], rows_ref[:, width:])


def mark_kernel(*refs):
    refs[-1][...] = jnp.zeros_like(refs[-1])


def order(us, *args):
    return pl.pallas_call(
        mark_kernel,
        out_shape=jax.ShapeDtypeStruct((16, 128), BF),
        in_specs=[pl.BlockSpec(memory_space=pl.ANY)] * len(args),
        cost_estimate=pl.CostEstimate(
            flops=us * 10**9, bytes_accessed=us * 3 * 10**6, transcendentals=0
        ),
    )(*args)


def call(kernel, out_shape, scratch, flops, *args, fetched=0):
    outs = [jax.ShapeDtypeStruct(shape, BF) for shape in out_shape]
    spaces = [pltpu.SMEM if a.dtype == jnp.int32 else pltpu.VMEM for a in args]
    scratches = [pltpu.VMEM(shape, BF) for shape in scratch]
    if fetched:
        spaces = [space if space == pltpu.SMEM else pl.ANY for space in spaces]
        big = [a for a in args if a.dtype != jnp.int32][:fetched]
        scratches += [pltpu.VMEM(a.shape, BF) for a in big] + [pltpu.SemaphoreType.DMA((fetched,))]
    return pl.pallas_call(
        kernel,
        out_shape=outs,
        in_specs=[pl.BlockSpec(memory_space=space) for space in spaces],
        out_specs=[pl.BlockSpec(memory_space=pltpu.VMEM)] * len(outs),
        scratch_shapes=scratches,
        compiler_params=pltpu.CompilerParams(vmem_limit_bytes=63 * 1024 * 1024),
        cost_estimate=pl.CostEstimate(
            flops=flops, bytes_accessed=sum(a.size * 2 for a in args), transcendentals=0
        ),
    )(*args)


def make_body(ny, nx, nz):
    def shift_x(v, s):
        return lax.ppermute(v, "x", [(i, (i + s) % nx) for i in range(nx)])

    def swap_core(v):
        return lax.ppermute(v, "core", [(0, 1), (1, 0)])

    def body(inputs, out_grad, gate_pre, up_pre, w_gate, w_up, w_down, segment_ids):
        x, core = lax.axis_index("x"), lax.axis_index("core")
        x_id, core_id = x.astype(jnp.int32).reshape(1), core.astype(jnp.int32).reshape(1)
        tokens, width = inputs.shape
        units = w_down.shape[0]
        part = tokens // nx
        total = tokens * nz * 2
        scale = total ** (-0.5)

        down = [w_down] + [shift_x(w_down, s) for s in range(1, nx)]
        down_other = [swap_core(v) for v in down]
        both_w = jnp.concatenate([w_gate.T, w_up.T], axis=0)
        w_other = swap_core(both_w)

        keep = (segment_ids % 2 == 1).astype(BF)
        masked = out_grad * keep[:, None]
        pieces = jnp.broadcast_to(
            masked.reshape(nx, 1, part, width), (nx, nz, part, width)
        ).reshape(nx * nz * part, width)
        saved = lax.all_gather(
            tied(jnp.concatenate([gate_pre, up_pre], axis=1), pieces), ("y", "x"), axis=0
        ).reshape(ny, 2, nx, part, 2 * units)
        got = lax.all_to_all(pieces, ("x", "z"), 0, 0, tiled=True)
        got = got.reshape(nx, nz * part, width)

        mark = order(20, *down[1:])
        (hidden_part,) = call(
            functools.partial(hidden_kernel, nx),
            [(ny, part, 2 * units)], [], 2 * total * units * width // 2,
            x_id, got, *down, *down_other, mark, fetched=2 * nx + 1,
        )
        rows = lax.all_gather(
            tied(jnp.concatenate([masked, inputs], axis=1), hidden_part),
            ("z", "core"), axis=0, tiled=True,
        )

        def spread(v, axis, count):
            shape = (count,) + v.shape
            copies = jnp.broadcast_to(v[None], shape).reshape((-1,) + v.shape[1:])
            return lax.all_to_all(copies, axis, 0, 0, tiled=True).reshape(shape)

        terms = lax.all_to_all(
            hidden_part.reshape(ny * part, 2 * units), "y", 0, 0, tiled=True
        ).reshape(ny, part, 2 * units)
        hidden_sum = jnp.sum(terms.astype(F32), axis=0).astype(BF)
        hidden_y = spread(hidden_sum, "y", ny)
        hidden_all = spread(hidden_y, "x", nx)

        pair = (2, ny, nx, part, units)
        factors, factors_send, hidden = call(
            factor_kernel, [pair, pair, (ny, 2, nx, part, units)], [],
            15000 * total * units, core_id, tied(saved, hidden_y),
        )
        factors_other = swap_core(factors_send)
        input_part, hg_send = call(
            input_kernel, [(nz * nx * part, width), (nx, ny, part, units)],
            [(2, ny, nx, part, 2 * units)], 2 * total * units * width,
            hidden_all, factors, both_w, factors_other, w_other, order(60, hidden_all), fetched=5,
        )
        swapped = swap_core(hg_send)
        input_terms = lax.all_to_all(input_part, "z", 0, 0, tiled=True)
        grad_gate, grad_up, grad_down = call(
            functools.partial(weight_kernel, scale),
            [(units, width)] * 3, [(ny, 2, nx, part, units)] * 2, 200 * total * units * width,
            core_id, rows, hidden_all, swapped, factors, factors_send, hidden,
        )

        input_terms = tied(input_terms, grad_gate, grad_up, grad_down)
        input_terms = input_terms.reshape(nz, tokens, width)
        in_grad = jnp.sum(input_terms.astype(F32), axis=0).astype(BF)
        return in_grad, grad_gate.T, grad_up.T, grad_down

    return body


def solution(mesh):
    nx = 4 if mesh.shape["row"] >= 16 else 2
    ny, nz = mesh.shape["row"] // nx, mesh.shape["col"] // 2
    grid = Mesh(mesh.devices.reshape(ny, nx, nz, 2), ("y", "x", "z", "core"))
    row, col = ("y", "x"), ("z", "core")
    return jax.shard_map(
        make_body(ny, nx, nz),
        mesh=grid,
        in_specs=(
            P(col, row), P(col, row), P(row, col), P(row, col),
            P(row, col), P(row, col), P(col, row), P(col),
        ),
        out_specs=(P(col, row), P(row, col), P(row, col), P(col, row)),
        check_vma=False,
    )
```

time: 212 us -> 197 us (0.929)
  blocking collectives: 52.7 us -> 20.6 us
  starting transfers between devices: 57.3 us -> 70.4 us
  local copies, waits for them, and re-layouts: 12.1 us -> 3.43 us
  waiting for transfers between devices: 44.8 us -> 52.5 us
  Pallas kernels: 24.4 us -> 28.6 us
    all_to_all x2 -> x1, blocking collectives: 52.7 us -> 20.6 us  [body(): lax.all_to_all(hidden_part.reshape(ny * part, 2 * units), 'y', 0, 0, tile...]
    ppermute x3, waiting for transfers between devices: 18.2 us -> 0.01 us  [shift_x(): return lax.ppermute(v, 'x', [(i, (i + s) % nx) for i in range(nx)])]
    all_to_all x1, waiting for transfers between devices: 0.01 us -> 12.7 us  [body(): got = lax.all_to_all(pieces, ('x', 'z'), 0, 0, tiled=True)]
    all_to_all x1, starting transfers between devices: 6.09 us -> 12.7 us  [body(): input_terms = lax.all_to_all(input_part, 'z', 0, 0, tiled=True)]
    all_to_all x1 -> x2, starting transfers between devices: 3.61 us -> 9.05 us  [spread(): return lax.all_to_all(copies, axis, 0, 0, tiled=True).reshape(shape)]
    unnamed x24, local copies, waits for them, and re-layouts: 4.81 us -> 0.06 us
    all_to_all x1, waiting for transfers between devices: 12.8 us -> 17.4 us  [body(): input_terms = lax.all_to_all(input_part, 'z', 0, 0, tiled=True)]
    ppermute x7, waiting for transfers between devices: 0.37 us -> 4.94 us  [swap_core(): return lax.ppermute(v, 'core', [(0, 1), (1, 0)])]
  transfers between devices with their start and end apart: 15 -> 16, of which waited for: 5 -> 6; matrix products, arithmetic and copies ran while one was open for 5% -> 3% of each run, Pallas kernels for 12% -> 15%
where the time goes in v3:
time: 197 us; the launch traced here: 196 us
  starting transfers between devices  70.4 us (36%)
  waiting for transfers between devices  52.5 us (27%)
  Pallas kernels  28.6 us (15%)
  blocking collectives  20.6 us (10%)
  between operations  14.4 us (7%)
  other arithmetic  6.22 us (3%)
  local copies, waits for them, and re-layouts  3.43 us (2%)
    pallas_call x4, Pallas kernels, call(): pl.pallas_call(kernel, out_shape=outs, in_specs=[pl.BlockSpec(memory_spac...  27.4 us
    ppermute x7, starting transfers between devices, swap_core(): return lax.ppermute(v, 'core', [(0, 1), (1, 0)])  26.6 us
    all_to_all x1, blocking collectives, body(): lax.all_to_all(hidden_part.reshape(ny * part, 2 * units), 'y', 0, 0, tile...  20.6 us
    all_to_all x1, waiting for transfers between devices, body(): input_terms = lax.all_to_all(input_part, 'z', 0, 0, tiled=True)  17.4 us
    all_to_all x2, waiting for transfers between devices, spread(): return lax.all_to_all(copies, axis, 0, 0, tiled=True).reshape(shape)  14.4 us
    all_to_all x1, starting transfers between devices, body(): input_terms = lax.all_to_all(input_part, 'z', 0, 0, tiled=True)  12.7 us
    all_to_all x1, waiting for transfers between devices, body(): got = lax.all_to_all(pieces, ('x', 'z'), 0, 0, tiled=True)  12.7 us
    ppermute x3, starting transfers between devices, shift_x(): return lax.ppermute(v, 'x', [(i, (i + s) % nx) for i in range(nx)])  11.4 us
  transfers between devices with their start and end apart: 16, of which 6 were waited for; matrix products, arithmetic and copies ran while one was open for 3% of the time, Pallas kernels for 15%

profile of v3, /device:TPU:1, one launch (start us, length us, event | category | flops | bytes accessed | tf_op | source)
XLA Modules:
  0.0 196.1 jit_solution(9331212270675591570)
XLA Ops:
  7.2 1.6 pad_maximum_fusion.2
  8.9 4.0 %collective-permute-start = (bf16[416,512]{1,0:T(8,128)(2,1)}, bf16[416,512]{1,0:T(8,128)(2,1)S(1)}, u32[]{:S(2)}, u32[]{:S(2)}) collective-permute-start(bf16[416,512]{1,0:T(8,128)(2,1)} %refs_1_.1), channel_id=1, source_target_pairs={{0,16},{16,32},{32,48},{48,0},{1,17},{17,33},{33,49},{49,1},{2,18}... | collective-permute-start | bytes 1277960 | tf_op jit(solution)/shard_map/ppermute | solution.py:147
  12.9 4.4 %collective-permute-start.1 = (bf16[416,512]{1,0:T(8,128)(2,1)}, bf16[416,512]{1,0:T(8,128)(2,1)S(1)}, u32[]{:S(2)}, u32[]{:S(2)}) collective-permute-start(bf16[416,512]{1,0:T(8,128)(2,1)} %refs_1_.1), channel_id=1, source_target_pairs={{0,32},{16,48},{32,0},{48,16},{1,33},{17,49},{33,1},{49,17},{2,34}... | collective-permute-start | bytes 1277960 | tf_op jit(solution)/shard_map/ppermute | solution.py:147
  17.2 3.1 %collective-permute-start.2 = (bf16[416,512]{1,0:T(8,128)(2,1)}, bf16[416,512]{1,0:T(8,128)(2,1)S(1)}, u32[]{:S(2)}, u32[]{:S(2)}) collective-permute-start(bf16[416,512]{1,0:T(8,128)(2,1)} %refs_1_.1), channel_id=1, source_target_pairs={{0,48},{16,0},{32,16},{48,32},{1,49},{17,1},{33,17},{49,33},{2,50}... | collective-permute-start | bytes 1277960 | tf_op jit(solution)/shard_map/ppermute | solution.py:147
  21.0 1.0 broadcast_multiply_fusion
  22.0 1.1 broadcast_in_dim.9
  23.0 10.6 %all-to-all-start = ((bf16[32,32,512]{2,1,0:T(8,128)(2,1)}), bf16[32,32,512]{2,1,0:T(8,128)(2,1)}, u32[]{:S(2)}, u32[]{:S(2)}) async-start(bf16[32,32,512]{2,1,0:T(8,128)(2,1)} %bitcast.2), calls=%async_computation | async-start | bytes 2097152 | tf_op jit(solution)/shard_map/all_to_all | solution.py:174
  33.7 3.7 %collective-permute-start.3 = (bf16[416,512]{1,0:T(8,128)(2,1)S(1)}, bf16[416,512]{1,0:T(8,128)(2,1)S(1)}, u32[]{:S(2)}, u32[]{:S(2)}) collective-permute-start(bf16[416,512]{1,0:T(8,128)(2,1)S(1)} %copy-done.1), channel_id=1, source_target_pairs={{0,1},{1,0},{2,3},{3,2},{4,5},{5,4},{6,7},{7,6},{8,9},{9,8},{10,11... | collective-permute-start | bytes 1277960 | tf_op jit(solution)/shard_map/ppermute | solution.py:150
  37.4 1.9 collective-permute-start.4
  39.3 2.4 %collective-permute-start.5 = (bf16[416,512]{1,0:T(8,128)(2,1)S(1)}, bf16[416,512]{1,0:T(8,128)(2,1)S(1)}, u32[]{:S(2)}, u32[]{:S(2)}) collective-permute-start(bf16[416,512]{1,0:T(8,128)(2,1)S(1)} %collective-permute-done.1.refs_1_.refs_3_), channel_id=1, source_target_pairs={{0,1},{1,0},{2,3},{3,2},{4,5},{5,4},{6,7},{7,6},{8,9},{9,8},{10,11... | collective-permute-start | bytes 1277960 | tf_op jit(solution)/shard_map/ppermute | solution.py:150
  41.8 1.9 collective-permute-start.6
  44.4 1.1 collective-permute-done.6.refs_8_
  45.4 12.7 %all-to-all-done = bf16[32,32,512]{2,1,0:T(8,128)(2,1)} async-done(((bf16[32,32,512]{2,1,0:T(8,128)(2,1)}), bf16[32,32,512]{2,1,0:T(8,128)(2,1)}, u32[]{:S(2)}, u32[]{:S(2)}) %all-to-all-start) | async-done | bytes 1048608 | tf_op jit(solution)/shard_map/all_to_all | solution.py:174
  58.1 4.3 %shard_map.112 = bf16[8,32,832]{2,1,0:T(8,128)(2,1)} custom-call(s32[1]{0:T(128)} %bitcast.x_ref, bf16[4,256,512]{2,1,0:T(8,128)(2,1)} %bitcast.3.refs_0_, bf16[416,512]{1,0:T(8,128)(2,1)} %refs_1_.1, bf16[416,512]{1,0:T(8,128)(2,1)} %copy-done.2, bf16[416,512]{1,0:T(8,128)(2,1)} %copy-done.3, bf16[416,512]{1,0:T(8,128)(2,1)} %copy-done.4, ...), custom_call_target="tpu_custom_call" | custom-call | flops 436207616 | bytes 4460546 | tf_op jit(solution)/shard_map/pallas_call | solution.py:132
  62.4 20.6 %all_to_all.38 = bf16[8,32,832]{2,1,0:T(8,128)(2,1)S(1)} all-to-all(bf16[8,32,832]{2,1,0:T(8,128)(2,1)} %shard_map.112), channel_id=1, replica_groups=mesh['y'=8,'x'=4,'z'=8,'core'=2] {'y'}, dimensions={0} | all-to-all | bytes 851968 | tf_op jit(solution)/shard_map/all_to_all | solution.py:193
  83.1 0.9 broadcast_in_dim.10
  83.9 4.5 %all-to-all-start.2 = ((bf16[8,32,832]{2,1,0:T(8,128)(2,1)}), bf16[8,32,832]{2,1,0:T(8,128)(2,1)S(1)}, u32[]{:S(2)}, u32[]{:S(2)}) async-start(bf16[8,32,832]{2,1,0:T(8,128)(2,1)} %broadcast_in_dim.10), calls=%async_computation.2 | async-start | bytes 917504 | tf_op jit(solution)/shard_map/all_to_all | solution.py:191
  88.5 0.7 pad_maximum_fusion.1
  89.3 14.4 %all-to-all-done.2 = bf16[8,32,832]{2,1,0:T(8,128)(2,1)S(1)} async-done(((bf16[8,32,832]{2,1,0:T(8,128)(2,1)}), bf16[8,32,832]{2,1,0:T(8,128)(2,1)S(1)}, u32[]{:S(2)}, u32[]{:S(2)}) %all-to-all-start.2) | async-done | bytes 426016 | tf_op jit(solution)/shard_map/all_to_all | solution.py:191
  103.7 1.4 broadcast_in_dim.22
  105.1 4.5 %all-to-all-start.3 = ((bf16[32,32,832]{2,1,0:T(8,128)(2,1)}), bf16[32,32,832]{2,1,0:T(8,128)(2,1)}, u32[]{:S(2)}, u32[]{:S(2)}) async-start(bf16[32,32,832]{2,1,0:T(8,128)(2,1)} %bitcast.4), calls=%async_computation.3 | async-start | bytes 3670016 | tf_op jit(solution)/shard_map/all_to_all | solution.py:191
  109.7 12.0 %collective-permute-start.8 = (bf16[832,512]{1,0:T(8,128)(2,1)S(1)}, bf16[832,512]{1,0:T(8,128)(2,1)}, u32[]{:S(2)}, u32[]{:S(2)}) collective-permute-start(bf16[832,512]{1,0:T(8,128)(2,1)S(1)} %pad_maximum_fusion.refs_2_), channel_id=1, source_target_pairs={{0,1},{1,0},{2,3},{3,2},{4,5},{5,4},{6,7},{7,6},{8,9},{9,8},{10,11... | collective-permute-start | bytes 2555912 | tf_op jit(solution)/shard_map/ppermute | solution.py:150
  121.8 6.5 %shard_map.113 = (bf16[2,8,4,32,416]{4,3,2,1,0:T(8,128)(2,1)}, bf16[2,8,4,32,416]{4,3,2,1,0:T(8,128)(2,1)}, bf16[8,2,4,32,416]{4,3,2,1,0:T(8,128)(2,1)}) custom-call(s32[1]{0:T(128)} %bitcast.6.core_ref, bf16[8,2,4,32,832]{4,3,2,1,0:T(8,128)(2,1)} %bitcast.19), custom_call_target="tpu_custom_call" | custom-call | flops 12779520000 | bytes 3407874 | tf_op jit(solution)/shard_map/pallas_call | solution.py:132
  128.3 1.9 collective-permute-start.7
  130.8 3.9 %collective-permute-done.7.refs_3_ = bf16[2,8,4,32,416]{4,3,2,1,0:T(8,128)(2,1)} collective-permute-done((bf16[2,8,4,32,416]{4,3,2,1,0:T(8,128)(2,1)}, bf16[2,8,4,32,416]{4,3,2,1,0:T(8,128)(2,1)}, u32[]{:S(2)}, u32[]{:S(2)}) %collective-permute-start.7) | collective-permute-done | bytes 1703968 | tf_op jit(solution)/shard_map/ppermute | solution.py:150
  134.6 7.7 %shard_map.115 = (bf16[1024,512]{1,0:T(8,128)(2,1)}, bf16[4,8,32,416]{3,2,1,0:T(8,128)(2,1)}) custom-call(bf16[4,8,32,832]{3,2,1,0:T(8,128)(2,1)} %bitcast.5.refs_0_.hg_ref, bf16[2,8,4,32,416]{4,3,2,1,0:T(8,128)(2,1)} %get-tuple-element.14.refs_1_.own_ref, bf16[832,512]{1,0:T(8,128)(2,1)} %copy-done, ...), custom_call_target="tpu_custom_call" | custom-call | flops 872415232 | bytes 6819840 | tf_op jit(solution)/shard_map/pallas_call | solution.py:132
  142.3 2.7 %collective-permute-start.9 = (bf16[4,8,32,416]{3,2,1,0:T(8,128)(2,1)}, bf16[4,8,32,416]{3,2,1,0:T(8,128)(2,1)}, u32[]{:S(2)}, u32[]{:S(2)}) collective-permute-start(bf16[4,8,32,416]{3,2,1,0:T(8,128)(2,1)} %get-tuple-element.18), channel_id=1, source_target_pairs={{0,1},{1,0},{2,3},{3,2},{4,5},{5,4},{6,7},{7,6},{8,9},{9,8},{10,11... | collective-permute-start | bytes 2555912 | tf_op jit(solution)/shard_map/ppermute | solution.py:150
  145.1 12.7 %all-to-all-start.4 = ((bf16[8,128,512]{2,1,0:T(8,128)(2,1)}), bf16[8,128,512]{2,1,0:T(8,128)(2,1)}, u32[]{:S(2)}, u32[]{:S(2)}) async-start(bf16[8,128,512]{2,1,0:T(8,128)(2,1)} %bitcast.16), calls=%async_computation.4 | async-start | bytes 2097152 | tf_op jit(solution)/shard_map/all_to_all | solution.py:212
  157.8 3.0 %all-gather.4.cloned.1.call-done.rows_ref = bf16[2048,1024]{1,0:T(8,128)(2,1)} async-done(((bf16[128,1024]{1,0:T(8,128)(2,1)}), bf16[2048,1024]{1,0:T(8,128)(2,1)}) %all-gather.4.cloned.1.call-update) | async-done | bytes 4194320 | tf_op jit(solution)/shard_map/all_gather | solution.py:183
  160.8 9.0 %shard_map.116 = (bf16[416,512]{1,0:T(8,128)(2,1)}, bf16[416,512]{1,0:T(8,128)(2,1)}, bf16[416,512]{1,0:T(8,128)(2,1)}) custom-call(s32[1]{0:T(128)} %bitcast.6.core_ref, bf16[2048,1024]{1,0:T(8,128)(2,1)} %all-gather.4.cloned.1.call-done.rows_ref, bf16[4,8,32,832]{3,2,1,0:T(8,128)(2,1)} %bitcast.5.refs_0_.hg_ref, ...), custom_call_target="tpu_custom_call" | custom-call | flops 87241523200 | bytes 11862018 | tf_op jit(solution)/shard_map/pallas_call | solution.py:132
  169.8 17.4 %all-to-all-done.4 = bf16[8,128,512]{2,1,0:T(8,128)(2,1)} async-done(((bf16[8,128,512]{2,1,0:T(8,128)(2,1)}), bf16[8,128,512]{2,1,0:T(8,128)(2,1)}, u32[]{:S(2)}, u32[]{:S(2)}) %all-to-all-start.4) | async-done | bytes 1048608 | tf_op jit(solution)/shard_map/all_to_all | solution.py:212
  187.2 2.1 %reduce_sum.25 = bf16[128,512]{1,0:T(8,128)(2,1)} reduce(bf16[8,128,512]{2,1,0:T(8,128)(2,1)} %bitcast.12, bf16[]{:T(256)} %constant.28.clone.1), dimensions={0}, to_apply=%region_1.2 | reduce | flops 458752 | bytes 1179650 | tf_op jit(solution)/shard_map/reduce_sum | solution.py:221
  (43 shorter events, 2.2 us)
Async XLA Ops:
  7.2 26.5 %copy-start.1 = (bf16[416,512]{1,0:T(8,128)(2,1)S(1)}, bf16[416,512]{1,0:T(8,128)(2,1)}, u32[]{:S(2)}) copy-start(bf16[416,512]{1,0:T(8,128)(2,1)} %refs_1_.1) | copy-start | bytes 1277956
  7.2 114.6 %all-gather.6.cloned.1.call-start = ((), (), s32[]{:S(2)}) async-start(), calls=%async_computation.6 | async-start | bytes 3784704 | tf_op jit(solution)/shard_map/all_gather | solution.py:171
  8.9 28.5 %collective-permute-start = (bf16[416,512]{1,0:T(8,128)(2,1)}, bf16[416,512]{1,0:T(8,128)(2,1)S(1)}, u32[]{:S(2)}, u32[]{:S(2)}) collective-permute-start(bf16[416,512]{1,0:T(8,128)(2,1)} %refs_1_.1), channel_id=1, source_target_pairs={{0,16},{16,32},{32,48},{48,0},{1,17},{17,33},{33,49},{49,1},{2,18}... | collective-permute-start | bytes 1277960 | tf_op jit(solution)/shard_map/ppermute | solution.py:147
  12.9 26.5 %collective-permute-start.1 = (bf16[416,512]{1,0:T(8,128)(2,1)}, bf16[416,512]{1,0:T(8,128)(2,1)S(1)}, u32[]{:S(2)}, u32[]{:S(2)}) collective-permute-start(bf16[416,512]{1,0:T(8,128)(2,1)} %refs_1_.1), channel_id=1, source_target_pairs={{0,32},{16,48},{32,0},{48,16},{1,33},{17,49},{33,1},{49,17},{2,34}... | collective-permute-start | bytes 1277960 | tf_op jit(solution)/shard_map/ppermute | solution.py:147
  17.2 24.5 %collective-permute-start.2 = (bf16[416,512]{1,0:T(8,128)(2,1)}, bf16[416,512]{1,0:T(8,128)(2,1)S(1)}, u32[]{:S(2)}, u32[]{:S(2)}) collective-permute-start(bf16[416,512]{1,0:T(8,128)(2,1)} %refs_1_.1), channel_id=1, source_target_pairs={{0,48},{16,0},{32,16},{48,32},{1,49},{17,1},{33,17},{49,33},{2,50}... | collective-permute-start | bytes 1277960 | tf_op jit(solution)/shard_map/ppermute | solution.py:147
  23.0 35.1 %all-to-all-start = ((bf16[32,32,512]{2,1,0:T(8,128)(2,1)}), bf16[32,32,512]{2,1,0:T(8,128)(2,1)}, u32[]{:S(2)}, u32[]{:S(2)}) async-start(bf16[32,32,512]{2,1,0:T(8,128)(2,1)} %bitcast.2), calls=%async_computation | async-start | bytes 2097152 | tf_op jit(solution)/shard_map/all_to_all | solution.py:174
  33.7 10.7 %collective-permute-start.3 = (bf16[416,512]{1,0:T(8,128)(2,1)S(1)}, bf16[416,512]{1,0:T(8,128)(2,1)S(1)}, u32[]{:S(2)}, u32[]{:S(2)}) collective-permute-start(bf16[416,512]{1,0:T(8,128)(2,1)S(1)} %copy-done.1), channel_id=1, source_target_pairs={{0,1},{1,0},{2,3},{3,2},{4,5},{5,4},{6,7},{7,6},{8,9},{9,8},{10,11... | collective-permute-start | bytes 1277960 | tf_op jit(solution)/shard_map/ppermute | solution.py:150
  37.4 6.3 %copy-start.2 = (bf16[416,512]{1,0:T(8,128)(2,1)}, bf16[416,512]{1,0:T(8,128)(2,1)S(1)}, u32[]{:S(2)}) copy-start(bf16[416,512]{1,0:T(8,128)(2,1)S(1)} %collective-permute-done.refs_0_.refs_2_) | copy-start | bytes 1277956
  37.4 6.9 %collective-permute-start.4 = (bf16[416,512]{1,0:T(8,128)(2,1)S(1)}, bf16[416,512]{1,0:T(8,128)(2,1)S(1)}, u32[]{:S(2)}, u32[]{:S(2)}) collective-permute-start(bf16[416,512]{1,0:T(8,128)(2,1)S(1)} %collective-permute-done.refs_0_.refs_2_), channel_id=1, source_target_pairs={{0,1},{1,0},{2,3},{3,2},{4,5},{5,4},{6,7},{7,6},{8,9},{9,8},{10,11... | collective-permute-start | bytes 1277960 | tf_op jit(solution)/shard_map/ppermute | solution.py:150
  39.3 4.4 %copy-start.3 = (bf16[416,512]{1,0:T(8,128)(2,1)}, bf16[416,512]{1,0:T(8,128)(2,1)S(1)}, u32[]{:S(2)}) copy-start(bf16[416,512]{1,0:T(8,128)(2,1)S(1)} %collective-permute-done.1.refs_1_.refs_3_) | copy-start | bytes 1277956
  39.3 5.0 %collective-permute-start.5 = (bf16[416,512]{1,0:T(8,128)(2,1)S(1)}, bf16[416,512]{1,0:T(8,128)(2,1)S(1)}, u32[]{:S(2)}, u32[]{:S(2)}) collective-permute-start(bf16[416,512]{1,0:T(8,128)(2,1)S(1)} %collective-permute-done.1.refs_1_.refs_3_), channel_id=1, source_target_pairs={{0,1},{1,0},{2,3},{3,2},{4,5},{5,4},{6,7},{7,6},{8,9},{9,8},{10,11... | collective-permute-start | bytes 1277960 | tf_op jit(solution)/shard_map/ppermute | solution.py:150
  41.8 2.0 %copy-start.4 = (bf16[416,512]{1,0:T(8,128)(2,1)}, bf16[416,512]{1,0:T(8,128)(2,1)S(1)}, u32[]{:S(2)}) copy-start(bf16[416,512]{1,0:T(8,128)(2,1)S(1)} %collective-permute-done.2.refs_2_.refs_4_) | copy-start | bytes 1277956
  41.8 3.7 %collective-permute-start.6 = (bf16[416,512]{1,0:T(8,128)(2,1)S(1)}, bf16[416,512]{1,0:T(8,128)(2,1)S(1)}, u32[]{:S(2)}, u32[]{:S(2)}) collective-permute-start(bf16[416,512]{1,0:T(8,128)(2,1)S(1)} %collective-permute-done.2.refs_2_.refs_4_), channel_id=1, source_target_pairs={{0,1},{1,0},{2,3},{3,2},{4,5},{5,4},{6,7},{7,6},{8,9},{9,8},{10,11... | collective-permute-start | bytes 1277960 | tf_op jit(solution)/shard_map/ppermute | solution.py:150
  44.3 1.1 copy-start.5
  44.3 13.8 %copy-start.6 = (bf16[416,512]{1,0:T(8,128)(2,1)}, bf16[416,512]{1,0:T(8,128)(2,1)S(1)}, u32[]{:S(2)}) copy-start(bf16[416,512]{1,0:T(8,128)(2,1)S(1)} %collective-permute-done.4.refs_6_) | copy-start | bytes 1277956
  44.4 13.7 %copy-start.7 = (bf16[416,512]{1,0:T(8,128)(2,1)}, bf16[416,512]{1,0:T(8,128)(2,1)S(1)}, u32[]{:S(2)}) copy-start(bf16[416,512]{1,0:T(8,128)(2,1)S(1)} %collective-permute-done.5.refs_7_) | copy-start | bytes 1277956
  45.4 12.7 %copy-start.8 = (bf16[416,512]{1,0:T(8,128)(2,1)}, bf16[416,512]{1,0:T(8,128)(2,1)S(1)}, u32[]{:S(2)}) copy-start(bf16[416,512]{1,0:T(8,128)(2,1)S(1)} %collective-permute-done.6.refs_8_) | copy-start | bytes 1277956
  62.4 26.1 %copy-start.11 = (bf16[128,512]{1,0:T(8,128)(2,1)S(1)}, bf16[128,512]{1,0:T(8,128)(2,1)}, u32[]{:S(2)}) copy-start(bf16[128,512]{1,0:T(8,128)(2,1)} %param.8) | copy-start | bytes 393220
  83.9 19.7 %all-to-all-start.2 = ((bf16[8,32,832]{2,1,0:T(8,128)(2,1)}), bf16[8,32,832]{2,1,0:T(8,128)(2,1)S(1)}, u32[]{:S(2)}, u32[]{:S(2)}) async-start(bf16[8,32,832]{2,1,0:T(8,128)(2,1)} %broadcast_in_dim.10), calls=%async_computation.2 | async-start | bytes 917504 | tf_op jit(solution)/shard_map/all_to_all | solution.py:191
  88.4 72.4 %all-gather.4.cloned.1.call-start = ((), (), s32[]{:S(2)}) async-start(), calls=%async_computation.5 | async-start | bytes 4456448 | tf_op jit(solution)/shard_map/all_gather | solution.py:183
  105.1 4.6 %copy-start.9 = (bf16[512,416]{0,1:T(8,128)(2,1)S(1)}, bf16[512,416]{0,1:T(8,128)(2,1)}, u32[]{:S(2)}) copy-start(bf16[512,416]{0,1:T(8,128)(2,1)} %param.13) | copy-start | bytes 1277956
  105.1 4.6 %copy-start.10 = (bf16[512,416]{0,1:T(8,128)(2,1)S(1)}, bf16[512,416]{0,1:T(8,128)(2,1)}, u32[]{:S(2)}) copy-start(bf16[512,416]{0,1:T(8,128)(2,1)} %param.12) | copy-start | bytes 1277956
  105.1 25.1 %all-to-all-start.3 = ((bf16[32,32,832]{2,1,0:T(8,128)(2,1)}), bf16[32,32,832]{2,1,0:T(8,128)(2,1)}, u32[]{:S(2)}, u32[]{:S(2)}) async-start(bf16[32,32,832]{2,1,0:T(8,128)(2,1)} %bitcast.4), calls=%async_computation.3 | async-start | bytes 3670016 | tf_op jit(solution)/shard_map/all_to_all | solution.py:191
  109.7 18.5 %copy-start = (bf16[832,512]{1,0:T(8,128)(2,1)}, bf16[832,512]{1,0:T(8,128)(2,1)S(1)}, u32[]{:S(2)}) copy-start(bf16[832,512]{1,0:T(8,128)(2,1)S(1)} %pad_maximum_fusion.refs_2_) | copy-start | bytes 2555908
  109.7 21.1 %collective-permute-start.8 = (bf16[832,512]{1,0:T(8,128)(2,1)S(1)}, bf16[832,512]{1,0:T(8,128)(2,1)}, u32[]{:S(2)}, u32[]{:S(2)}) collective-permute-start(bf16[832,512]{1,0:T(8,128)(2,1)S(1)} %pad_maximum_fusion.refs_2_), channel_id=1, source_target_pairs={{0,1},{1,0},{2,3},{3,2},{4,5},{5,4},{6,7},{7,6},{8,9},{9,8},{10,11... | collective-permute-start | bytes 2555912 | tf_op jit(solution)/shard_map/ppermute | solution.py:150
  128.3 6.4 %collective-permute-start.7 = (bf16[2,8,4,32,416]{4,3,2,1,0:T(8,128)(2,1)}, bf16[2,8,4,32,416]{4,3,2,1,0:T(8,128)(2,1)}, u32[]{:S(2)}, u32[]{:S(2)}) collective-permute-start(bf16[2,8,4,32,416]{4,3,2,1,0:T(8,128)(2,1)} %get-tuple-element.15.send_ref), channel_id=1, source_target_pairs={{0,1},{1,0},{2,3},{3,2},{4,5},{5,4},{6,7},{7,6},{8,9},{9,8},{10,11... | collective-permute-start | bytes 5111816 | tf_op jit(solution)/shard_map/ppermute | solution.py:150
  142.3 15.5 %collective-permute-start.9 = (bf16[4,8,32,416]{3,2,1,0:T(8,128)(2,1)}, bf16[4,8,32,416]{3,2,1,0:T(8,128)(2,1)}, u32[]{:S(2)}, u32[]{:S(2)}) collective-permute-start(bf16[4,8,32,416]{3,2,1,0:T(8,128)(2,1)} %get-tuple-element.18), channel_id=1, source_target_pairs={{0,1},{1,0},{2,3},{3,2},{4,5},{5,4},{6,7},{7,6},{8,9},{9,8},{10,11... | collective-permute-start | bytes 2555912 | tf_op jit(solution)/shard_map/ppermute | solution.py:150
  145.1 42.2 %all-to-all-start.4 = ((bf16[8,128,512]{2,1,0:T(8,128)(2,1)}), bf16[8,128,512]{2,1,0:T(8,128)(2,1)}, u32[]{:S(2)}, u32[]{:S(2)}) async-start(bf16[8,128,512]{2,1,0:T(8,128)(2,1)} %bitcast.16), calls=%async_computation.4 | async-start | bytes 2097152 | tf_op jit(solution)/shard_map/all_to_all | solution.py:212
Sparse Core Ops, SparseCore 0:
  11.7 98.7 all-gather.5
  113.2 47.5 all-gather.3

commit v4 on v3

--- a/solution.py
+++ b/solution.py
@@ -178,10 +178,10 @@
         (hidden_part,) = call(
             functools.partial(hidden_kernel, nx),
             [(ny, part, 2 * units)], [], 2 * total * units * width // 2,
-            x_id, got, *down, *down_other, mark, fetched=2 * nx + 1,
+            x_id, got, *down, *down_other, mark, w_other, fetched=2 * nx + 1,
         )
         rows = lax.all_gather(
-            tied(jnp.concatenate([masked, inputs], axis=1), hidden_part),
+            jnp.concatenate([tied(out_grad, hidden_part) * keep[:, None], inputs], axis=1),
             ("z", "core"), axis=0, tiled=True,
         )
 

time: 197 us -> 197 us (level)
  waiting for transfers between devices: 52.5 us -> 49.5 us
    all_to_all x1, waiting for transfers between devices: 12.7 us -> 9.46 us  [body(): got = lax.all_to_all(pieces, ('x', 'z'), 0, 0, tiled=True)]
    ppermute x7, starting transfers between devices: 26.6 us -> 28.6 us  [swap_core(): return lax.ppermute(v, 'core', [(0, 1), (1, 0)])]
  transfers between devices with their start and end apart: 16 -> 16, of which waited for: 6 -> 7; matrix products, arithmetic and copies ran while one was open for 3% -> 3% of each run, Pallas kernels for 15% -> 15%
where the time goes in v4:
time: 197 us; the launch traced here: 196 us
  starting transfers between devices  72.2 us (37%)
  waiting for transfers between devices  49.5 us (25%)
  Pallas kernels  28.5 us (14%)
  blocking collectives  20.7 us (11%)
  between operations  14.4 us (7%)
  other arithmetic  6.35 us (3%)
  local copies, waits for them, and re-layouts  4.31 us (2%)
    ppermute x7, starting transfers between devices, swap_core(): return lax.ppermute(v, 'core', [(0, 1), (1, 0)])  28.6 us
    pallas_call x4, Pallas kernels, call(): pl.pallas_call(kernel, out_shape=outs, in_specs=[pl.BlockSpec(memory_spac...  27.3 us
    all_to_all x1, blocking collectives, body(): lax.all_to_all(hidden_part.reshape(ny * part, 2 * units), 'y', 0, 0, tile...  20.7 us
    all_to_all x1, waiting for transfers between devices, body(): input_terms = lax.all_to_all(input_part, 'z', 0, 0, tiled=True)  17.3 us
    all_to_all x2, waiting for transfers between devices, spread(): return lax.all_to_all(copies, axis, 0, 0, tiled=True).reshape(shape)  14.9 us
    all_to_all x1, starting transfers between devices, body(): input_terms = lax.all_to_all(input_part, 'z', 0, 0, tiled=True)  12.7 us
    ppermute x3, starting transfers between devices, shift_x(): return lax.ppermute(v, 'x', [(i, (i + s) % nx) for i in range(nx)])  11.4 us
    all_to_all x1, starting transfers between devices, body(): got = lax.all_to_all(pieces, ('x', 'z'), 0, 0, tiled=True)  10.6 us
  transfers between devices with their start and end apart: 16, of which 7 were waited for; matrix products, arithmetic and copies ran while one was open for 3% of the time, Pallas kernels for 15%

profile of v4, /device:TPU:1, one launch (start us, length us, event | category | flops | bytes accessed | tf_op | source)
XLA Modules:
  0.0 195.9 jit_solution(16722673771084528252)
XLA Ops:
  7.2 1.7 pad_maximum_fusion.2
  9.0 4.0 %collective-permute-start = (bf16[416,512]{1,0:T(8,128)(2,1)}, bf16[416,512]{1,0:T(8,128)(2,1)S(1)}, u32[]{:S(2)}, u32[]{:S(2)}) collective-permute-start(bf16[416,512]{1,0:T(8,128)(2,1)} %refs_1_.1), channel_id=1, source_target_pairs={{0,16},{16,32},{32,48},{48,0},{1,17},{17,33},{33,49},{49,1},{2,18}... | collective-permute-start | bytes 1277960 | tf_op jit(solution)/shard_map/ppermute | solution.py:147
  12.9 4.4 %collective-permute-start.1 = (bf16[416,512]{1,0:T(8,128)(2,1)}, bf16[416,512]{1,0:T(8,128)(2,1)S(1)}, u32[]{:S(2)}, u32[]{:S(2)}) collective-permute-start(bf16[416,512]{1,0:T(8,128)(2,1)} %refs_1_.1), channel_id=1, source_target_pairs={{0,32},{16,48},{32,0},{48,16},{1,33},{17,49},{33,1},{49,17},{2,34}... | collective-permute-start | bytes 1277960 | tf_op jit(solution)/shard_map/ppermute | solution.py:147
  17.3 3.1 %collective-permute-start.2 = (bf16[416,512]{1,0:T(8,128)(2,1)}, bf16[416,512]{1,0:T(8,128)(2,1)S(1)}, u32[]{:S(2)}, u32[]{:S(2)}) collective-permute-start(bf16[416,512]{1,0:T(8,128)(2,1)} %refs_1_.1), channel_id=1, source_target_pairs={{0,48},{16,0},{32,16},{48,32},{1,49},{17,1},{33,17},{49,33},{2,50}... | collective-permute-start | bytes 1277960 | tf_op jit(solution)/shard_map/ppermute | solution.py:147
  21.0 1.0 broadcast_multiply_fusion.1
  22.0 1.1 broadcast_in_dim.9
  23.1 10.6 %all-to-all-start = ((bf16[32,32,512]{2,1,0:T(8,128)(2,1)}), bf16[32,32,512]{2,1,0:T(8,128)(2,1)}, u32[]{:S(2)}, u32[]{:S(2)}) async-start(bf16[32,32,512]{2,1,0:T(8,128)(2,1)} %bitcast.2), calls=%async_computation | async-start | bytes 2097152 | tf_op jit(solution)/shard_map/all_to_all | solution.py:174
  33.7 3.7 %collective-permute-start.3 = (bf16[416,512]{1,0:T(8,128)(2,1)S(1)}, bf16[416,512]{1,0:T(8,128)(2,1)}, u32[]{:S(2)}, u32[]{:S(2)}) collective-permute-start(bf16[416,512]{1,0:T(8,128)(2,1)S(1)} %copy-done.5), channel_id=1, source_target_pairs={{0,1},{1,0},{2,3},{3,2},{4,5},{5,4},{6,7},{7,6},{8,9},{9,8},{10,11... | collective-permute-start | bytes 1277960 | tf_op jit(solution)/shard_map/ppermute | solution.py:150
  37.5 1.9 collective-permute-start.7
  39.5 2.4 %collective-permute-start.4 = (bf16[416,512]{1,0:T(8,128)(2,1)S(1)}, bf16[416,512]{1,0:T(8,128)(2,1)}, u32[]{:S(2)}, u32[]{:S(2)}) collective-permute-start(bf16[416,512]{1,0:T(8,128)(2,1)S(1)} %collective-permute-done.refs_0_.refs_2_), channel_id=1, source_target_pairs={{0,1},{1,0},{2,3},{3,2},{4,5},{5,4},{6,7},{7,6},{8,9},{9,8},{10,11... | collective-permute-start | bytes 1277960 | tf_op jit(solution)/shard_map/ppermute | solution.py:150
  41.9 1.9 collective-permute-start.5
  43.9 2.4 %collective-permute-start.6 = (bf16[416,512]{1,0:T(8,128)(2,1)S(1)}, bf16[416,512]{1,0:T(8,128)(2,1)}, u32[]{:S(2)}, u32[]{:S(2)}) collective-permute-start(bf16[416,512]{1,0:T(8,128)(2,1)S(1)} %collective-permute-done.2.refs_2_.refs_4_), channel_id=1, source_target_pairs={{0,1},{1,0},{2,3},{3,2},{4,5},{5,4},{6,7},{7,6},{8,9},{9,8},{10,11... | collective-permute-start | bytes 1277960 | tf_op jit(solution)/shard_map/ppermute | solution.py:150
  46.9 0.9 collective-permute-done.6.refs_8_
  47.8 0.9 copy-done.1
  48.7 9.5 %all-to-all-done = bf16[32,32,512]{2,1,0:T(8,128)(2,1)} async-done(((bf16[32,32,512]{2,1,0:T(8,128)(2,1)}), bf16[32,32,512]{2,1,0:T(8,128)(2,1)}, u32[]{:S(2)}, u32[]{:S(2)}) %all-to-all-start) | async-done | bytes 1048608 | tf_op jit(solution)/shard_map/all_to_all | solution.py:174
  58.2 4.3 %shard_map.112 = bf16[8,32,832]{2,1,0:T(8,128)(2,1)} custom-call(s32[1]{0:T(128)} %bitcast.x_ref, bf16[4,256,512]{2,1,0:T(8,128)(2,1)} %bitcast.3.refs_0_, bf16[416,512]{1,0:T(8,128)(2,1)} %refs_1_.1, bf16[416,512]{1,0:T(8,128)(2,1)} %copy-done.6, bf16[416,512]{1,0:T(8,128)(2,1)} %copy-done.7, bf16[416,512]{1,0:T(8,128)(2,1)} %copy-done.8, ...), custom_call_target="tpu_custom_call" | custom-call | flops 436207616 | bytes 5312514 | tf_op jit(solution)/shard_map/pallas_call | solution.py:132
  62.5 20.7 %all_to_all.38 = bf16[8,32,832]{2,1,0:T(8,128)(2,1)S(1)} all-to-all(bf16[8,32,832]{2,1,0:T(8,128)(2,1)} %shard_map.112), channel_id=1, replica_groups=mesh['y'=8,'x'=4,'z'=8,'core'=2] {'y'}, dimensions={0} | all-to-all | bytes 851968 | tf_op jit(solution)/shard_map/all_to_all | solution.py:193
  83.2 0.9 broadcast_in_dim.10
  84.1 4.5 %all-to-all-start.2 = ((bf16[8,32,832]{2,1,0:T(8,128)(2,1)}), bf16[8,32,832]{2,1,0:T(8,128)(2,1)S(1)}, u32[]{:S(2)}, u32[]{:S(2)}) async-start(bf16[8,32,832]{2,1,0:T(8,128)(2,1)} %broadcast_in_dim.10), calls=%async_computation.2 | async-start | bytes 917504 | tf_op jit(solution)/shard_map/all_to_all | solution.py:191
  89.5 14.9 %all-to-all-done.2 = bf16[8,32,832]{2,1,0:T(8,128)(2,1)S(1)} async-done(((bf16[8,32,832]{2,1,0:T(8,128)(2,1)}), bf16[8,32,832]{2,1,0:T(8,128)(2,1)S(1)}, u32[]{:S(2)}, u32[]{:S(2)}) %all-to-all-start.2) | async-done | bytes 426016 | tf_op jit(solution)/shard_map/all_to_all | solution.py:191
  104.4 1.4 broadcast_in_dim.11
  105.8 4.4 %all-to-all-start.3 = ((bf16[32,32,832]{2,1,0:T(8,128)(2,1)}), bf16[32,32,832]{2,1,0:T(8,128)(2,1)}, u32[]{:S(2)}, u32[]{:S(2)}) async-start(bf16[32,32,832]{2,1,0:T(8,128)(2,1)} %bitcast.6), calls=%async_computation.3 | async-start | bytes 3670016 | tf_op jit(solution)/shard_map/all_to_all | solution.py:191
  110.6 6.5 %shard_map.113 = (bf16[2,8,4,32,416]{4,3,2,1,0:T(8,128)(2,1)}, bf16[2,8,4,32,416]{4,3,2,1,0:T(8,128)(2,1)}, bf16[8,2,4,32,416]{4,3,2,1,0:T(8,128)(2,1)}) custom-call(s32[1]{0:T(128)} %bitcast.8.core_ref, bf16[8,2,4,32,832]{4,3,2,1,0:T(8,128)(2,1)} %bitcast.19), custom_call_target="tpu_custom_call" | custom-call | flops 12779520000 | bytes 3407874 | tf_op jit(solution)/shard_map/pallas_call | solution.py:132
  117.1 10.5 %collective-permute-start.8 = (bf16[2,8,4,32,416]{4,3,2,1,0:T(8,128)(2,1)}, bf16[2,8,4,32,416]{4,3,2,1,0:T(8,128)(2,1)}, u32[]{:S(2)}, u32[]{:S(2)}) collective-permute-start(bf16[2,8,4,32,416]{4,3,2,1,0:T(8,128)(2,1)} %get-tuple-element.15.send_ref), channel_id=1, source_target_pairs={{0,1},{1,0},{2,3},{3,2},{4,5},{5,4},{6,7},{7,6},{8,9},{9,8},{10,11... | collective-permute-start | bytes 5111816 | tf_op jit(solution)/shard_map/ppermute | solution.py:150
  128.2 3.5 %collective-permute-done.8.refs_3_ = bf16[2,8,4,32,416]{4,3,2,1,0:T(8,128)(2,1)} collective-permute-done((bf16[2,8,4,32,416]{4,3,2,1,0:T(8,128)(2,1)}, bf16[2,8,4,32,416]{4,3,2,1,0:T(8,128)(2,1)}, u32[]{:S(2)}, u32[]{:S(2)}) %collective-permute-start.8) | collective-permute-done | bytes 1703968 | tf_op jit(solution)/shard_map/ppermute | solution.py:150
  131.7 7.5 %shard_map.115 = (bf16[1024,512]{1,0:T(8,128)(2,1)}, bf16[4,8,32,416]{3,2,1,0:T(8,128)(2,1)}) custom-call(bf16[4,8,32,832]{3,2,1,0:T(8,128)(2,1)} %bitcast.7.refs_0_.hg_ref, bf16[2,8,4,32,416]{4,3,2,1,0:T(8,128)(2,1)} %get-tuple-element.14.refs_1_.own_ref, bf16[832,512]{1,0:T(8,128)(2,1)} %copy-done, ...), custom_call_target="tpu_custom_call" | custom-call | flops 872415232 | bytes 6819840 | tf_op jit(solution)/shard_map/pallas_call | solution.py:132
  139.2 5.7 %collective-permute-start.9 = (bf16[4,8,32,416]{3,2,1,0:T(8,128)(2,1)}, bf16[4,8,32,416]{3,2,1,0:T(8,128)(2,1)}, u32[]{:S(2)}, u32[]{:S(2)}) collective-permute-start(bf16[4,8,32,416]{3,2,1,0:T(8,128)(2,1)} %get-tuple-element.18), channel_id=1, source_target_pairs={{0,1},{1,0},{2,3},{3,2},{4,5},{5,4},{6,7},{7,6},{8,9},{9,8},{10,11... | collective-permute-start | bytes 2555912 | tf_op jit(solution)/shard_map/ppermute | solution.py:150
  144.9 12.7 %all-to-all-start.4 = ((bf16[8,128,512]{2,1,0:T(8,128)(2,1)}), bf16[8,128,512]{2,1,0:T(8,128)(2,1)}, u32[]{:S(2)}, u32[]{:S(2)}) async-start(bf16[8,128,512]{2,1,0:T(8,128)(2,1)} %bitcast.15), calls=%async_computation.4 | async-start | bytes 2097152 | tf_op jit(solution)/shard_map/all_to_all | solution.py:212
  157.6 3.2 %all-gather.4.cloned.1.call-done.rows_ref = bf16[2048,1024]{1,0:T(8,128)(2,1)} async-done(((bf16[128,1024]{1,0:T(8,128)(2,1)}), bf16[2048,1024]{1,0:T(8,128)(2,1)}) %all-gather.4.cloned.1.call-update) | async-done | bytes 4194320 | tf_op jit(solution)/shard_map/all_gather | solution.py:183
  160.8 9.0 %shard_map.116 = (bf16[416,512]{1,0:T(8,128)(2,1)}, bf16[416,512]{1,0:T(8,128)(2,1)}, bf16[416,512]{1,0:T(8,128)(2,1)}) custom-call(s32[1]{0:T(128)} %bitcast.8.core_ref, bf16[2048,1024]{1,0:T(8,128)(2,1)} %all-gather.4.cloned.1.call-done.rows_ref, bf16[4,8,32,832]{3,2,1,0:T(8,128)(2,1)} %bitcast.7.refs_0_.hg_ref, ...), custom_call_target="tpu_custom_call" | custom-call | flops 87241523200 | bytes 11862018 | tf_op jit(solution)/shard_map/pallas_call | solution.py:132
  169.8 17.3 %all-to-all-done.4 = bf16[8,128,512]{2,1,0:T(8,128)(2,1)} async-done(((bf16[8,128,512]{2,1,0:T(8,128)(2,1)}), bf16[8,128,512]{2,1,0:T(8,128)(2,1)}, u32[]{:S(2)}, u32[]{:S(2)}) %all-to-all-start.4) | async-done | bytes 1048608 | tf_op jit(solution)/shard_map/all_to_all | solution.py:212
  187.0 2.1 %reduce_sum.25 = bf16[128,512]{1,0:T(8,128)(2,1)} reduce(bf16[8,128,512]{2,1,0:T(8,128)(2,1)} %bitcast.12, bf16[]{:T(256)} %constant.28.clone.1), dimensions={0}, to_apply=%region_1.2 | reduce | flops 458752 | bytes 1179650 | tf_op jit(solution)/shard_map/reduce_sum | solution.py:221
  (40 shorter events, 3.3 us)
Async XLA Ops:
  7.2 26.5 %copy-start.5 = (bf16[416,512]{1,0:T(8,128)(2,1)S(1)}, bf16[416,512]{1,0:T(8,128)(2,1)}, u32[]{:S(2)}) copy-start(bf16[416,512]{1,0:T(8,128)(2,1)} %refs_1_.1) | copy-start | bytes 1277956
  7.2 30.2 %copy-start.3 = (bf16[512,416]{0,1:T(8,128)(2,1)S(1)}, bf16[512,416]{0,1:T(8,128)(2,1)}, u32[]{:S(2)}) copy-start(bf16[512,416]{0,1:T(8,128)(2,1)} %param.13) | copy-start | bytes 1277956
  7.2 30.2 %copy-start.4 = (bf16[512,416]{0,1:T(8,128)(2,1)S(1)}, bf16[512,416]{0,1:T(8,128)(2,1)}, u32[]{:S(2)}) copy-start(bf16[512,416]{0,1:T(8,128)(2,1)} %param.12) | copy-start | bytes 1277956
  7.2 103.4 %all-gather.6.cloned.1.call-start = ((), (), s32[]{:S(2)}) async-start(), calls=%async_computation.6 | async-start | bytes 3784704 | tf_op jit(solution)/shard_map/all_gather | solution.py:171
  9.0 30.5 %collective-permute-start = (bf16[416,512]{1,0:T(8,128)(2,1)}, bf16[416,512]{1,0:T(8,128)(2,1)S(1)}, u32[]{:S(2)}, u32[]{:S(2)}) collective-permute-start(bf16[416,512]{1,0:T(8,128)(2,1)} %refs_1_.1), channel_id=1, source_target_pairs={{0,16},{16,32},{32,48},{48,0},{1,17},{17,33},{33,49},{49,1},{2,18}... | collective-permute-start | bytes 1277960 | tf_op jit(solution)/shard_map/ppermute | solution.py:147
  12.9 29.0 %collective-permute-start.1 = (bf16[416,512]{1,0:T(8,128)(2,1)}, bf16[416,512]{1,0:T(8,128)(2,1)S(1)}, u32[]{:S(2)}, u32[]{:S(2)}) collective-permute-start(bf16[416,512]{1,0:T(8,128)(2,1)} %refs_1_.1), channel_id=1, source_target_pairs={{0,32},{16,48},{32,0},{48,16},{1,33},{17,49},{33,1},{49,17},{2,34}... | collective-permute-start | bytes 1277960 | tf_op jit(solution)/shard_map/ppermute | solution.py:147
  17.3 26.6 %collective-permute-start.2 = (bf16[416,512]{1,0:T(8,128)(2,1)}, bf16[416,512]{1,0:T(8,128)(2,1)S(1)}, u32[]{:S(2)}, u32[]{:S(2)}) collective-permute-start(bf16[416,512]{1,0:T(8,128)(2,1)} %refs_1_.1), channel_id=1, source_target_pairs={{0,48},{16,0},{32,16},{48,32},{1,49},{17,1},{33,17},{49,33},{2,50}... | collective-permute-start | bytes 1277960 | tf_op jit(solution)/shard_map/ppermute | solution.py:147
  23.1 35.1 %all-to-all-start = ((bf16[32,32,512]{2,1,0:T(8,128)(2,1)}), bf16[32,32,512]{2,1,0:T(8,128)(2,1)}, u32[]{:S(2)}, u32[]{:S(2)}) async-start(bf16[32,32,512]{2,1,0:T(8,128)(2,1)} %bitcast.2), calls=%async_computation | async-start | bytes 2097152 | tf_op jit(solution)/shard_map/all_to_all | solution.py:174
  33.7 13.2 %collective-permute-start.3 = (bf16[416,512]{1,0:T(8,128)(2,1)S(1)}, bf16[416,512]{1,0:T(8,128)(2,1)}, u32[]{:S(2)}, u32[]{:S(2)}) collective-permute-start(bf16[416,512]{1,0:T(8,128)(2,1)S(1)} %copy-done.5), channel_id=1, source_target_pairs={{0,1},{1,0},{2,3},{3,2},{4,5},{5,4},{6,7},{7,6},{8,9},{9,8},{10,11... | collective-permute-start | bytes 1277960 | tf_op jit(solution)/shard_map/ppermute | solution.py:150
  37.5 9.4 %copy-start = (bf16[832,512]{1,0:T(8,128)(2,1)}, bf16[832,512]{1,0:T(8,128)(2,1)S(1)}, u32[]{:S(2)}) copy-start(bf16[832,512]{1,0:T(8,128)(2,1)S(1)} %pad_maximum_fusion.refs_2_) | copy-start | bytes 2555908
  37.5 10.3 %collective-permute-start.7 = (bf16[832,512]{1,0:T(8,128)(2,1)S(1)}, bf16[832,512]{1,0:T(8,128)(2,1)S(1)}, u32[]{:S(2)}, u32[]{:S(2)}) collective-permute-start(bf16[832,512]{1,0:T(8,128)(2,1)S(1)} %pad_maximum_fusion.refs_2_), channel_id=1, source_target_pairs={{0,1},{1,0},{2,3},{3,2},{4,5},{5,4},{6,7},{7,6},{8,9},{9,8},{10,11... | collective-permute-start | bytes 2555912 | tf_op jit(solution)/shard_map/ppermute | solution.py:150
  39.5 6.8 %copy-start.6 = (bf16[416,512]{1,0:T(8,128)(2,1)}, bf16[416,512]{1,0:T(8,128)(2,1)S(1)}, u32[]{:S(2)}) copy-start(bf16[416,512]{1,0:T(8,128)(2,1)S(1)} %collective-permute-done.refs_0_.refs_2_) | copy-start | bytes 1277956
  39.5 7.4 %collective-permute-start.4 = (bf16[416,512]{1,0:T(8,128)(2,1)S(1)}, bf16[416,512]{1,0:T(8,128)(2,1)}, u32[]{:S(2)}, u32[]{:S(2)}) collective-permute-start(bf16[416,512]{1,0:T(8,128)(2,1)S(1)} %collective-permute-done.refs_0_.refs_2_), channel_id=1, source_target_pairs={{0,1},{1,0},{2,3},{3,2},{4,5},{5,4},{6,7},{7,6},{8,9},{9,8},{10,11... | collective-permute-start | bytes 1277960 | tf_op jit(solution)/shard_map/ppermute | solution.py:150
  41.9 4.4 %copy-start.7 = (bf16[416,512]{1,0:T(8,128)(2,1)}, bf16[416,512]{1,0:T(8,128)(2,1)S(1)}, u32[]{:S(2)}) copy-start(bf16[416,512]{1,0:T(8,128)(2,1)S(1)} %collective-permute-done.1.refs_1_.refs_3_) | copy-start | bytes 1277956
  41.9 5.0 %collective-permute-start.5 = (bf16[416,512]{1,0:T(8,128)(2,1)S(1)}, bf16[416,512]{1,0:T(8,128)(2,1)}, u32[]{:S(2)}, u32[]{:S(2)}) collective-permute-start(bf16[416,512]{1,0:T(8,128)(2,1)S(1)} %collective-permute-done.1.refs_1_.refs_3_), channel_id=1, source_target_pairs={{0,1},{1,0},{2,3},{3,2},{4,5},{5,4},{6,7},{7,6},{8,9},{9,8},{10,11... | collective-permute-start | bytes 1277960 | tf_op jit(solution)/shard_map/ppermute | solution.py:150
  43.8 2.4 %copy-start.8 = (bf16[416,512]{1,0:T(8,128)(2,1)}, bf16[416,512]{1,0:T(8,128)(2,1)S(1)}, u32[]{:S(2)}) copy-start(bf16[416,512]{1,0:T(8,128)(2,1)S(1)} %collective-permute-done.2.refs_2_.refs_4_) | copy-start | bytes 1277956
  43.9 3.9 %collective-permute-start.6 = (bf16[416,512]{1,0:T(8,128)(2,1)S(1)}, bf16[416,512]{1,0:T(8,128)(2,1)}, u32[]{:S(2)}, u32[]{:S(2)}) collective-permute-start(bf16[416,512]{1,0:T(8,128)(2,1)S(1)} %collective-permute-done.2.refs_2_.refs_4_), channel_id=1, source_target_pairs={{0,1},{1,0},{2,3},{3,2},{4,5},{5,4},{6,7},{7,6},{8,9},{9,8},{10,11... | collective-permute-start | bytes 1277960 | tf_op jit(solution)/shard_map/ppermute | solution.py:150
  47.8 0.9 copy-start.1
  62.4 26.2 %copy-start.2 = (bf16[128,512]{1,0:T(8,128)(2,1)S(1)}, bf16[128,512]{1,0:T(8,128)(2,1)}, u32[]{:S(2)}) copy-start(bf16[128,512]{1,0:T(8,128)(2,1)} %param.9) | copy-start | bytes 393220
  62.4 26.3 %copy-start.9 = (bf16[128,512]{1,0:T(8,128)(2,1)S(1)}, bf16[128,512]{1,0:T(8,128)(2,1)}, u32[]{:S(2)}) copy-start(bf16[128,512]{1,0:T(8,128)(2,1)} %param.8) | copy-start | bytes 393220
  84.1 20.3 %all-to-all-start.2 = ((bf16[8,32,832]{2,1,0:T(8,128)(2,1)}), bf16[8,32,832]{2,1,0:T(8,128)(2,1)S(1)}, u32[]{:S(2)}, u32[]{:S(2)}) async-start(bf16[8,32,832]{2,1,0:T(8,128)(2,1)} %broadcast_in_dim.10), calls=%async_computation.2 | async-start | bytes 917504 | tf_op jit(solution)/shard_map/all_to_all | solution.py:191
  88.6 72.2 %all-gather.4.cloned.1.call-start = ((), (), s32[]{:S(2)}) async-start(), calls=%async_computation.5 | async-start | bytes 4456448 | tf_op jit(solution)/shard_map/all_gather | solution.py:183
  105.8 21.7 %all-to-all-start.3 = ((bf16[32,32,832]{2,1,0:T(8,128)(2,1)}), bf16[32,32,832]{2,1,0:T(8,128)(2,1)}, u32[]{:S(2)}, u32[]{:S(2)}) async-start(bf16[32,32,832]{2,1,0:T(8,128)(2,1)} %bitcast.6), calls=%async_computation.3 | async-start | bytes 3670016 | tf_op jit(solution)/shard_map/all_to_all | solution.py:191
  117.1 14.6 %collective-permute-start.8 = (bf16[2,8,4,32,416]{4,3,2,1,0:T(8,128)(2,1)}, bf16[2,8,4,32,416]{4,3,2,1,0:T(8,128)(2,1)}, u32[]{:S(2)}, u32[]{:S(2)}) collective-permute-start(bf16[2,8,4,32,416]{4,3,2,1,0:T(8,128)(2,1)} %get-tuple-element.15.send_ref), channel_id=1, source_target_pairs={{0,1},{1,0},{2,3},{3,2},{4,5},{5,4},{6,7},{7,6},{8,9},{9,8},{10,11... | collective-permute-start | bytes 5111816 | tf_op jit(solution)/shard_map/ppermute | solution.py:150
  139.2 18.4 %collective-permute-start.9 = (bf16[4,8,32,416]{3,2,1,0:T(8,128)(2,1)}, bf16[4,8,32,416]{3,2,1,0:T(8,128)(2,1)}, u32[]{:S(2)}, u32[]{:S(2)}) collective-permute-start(bf16[4,8,32,416]{3,2,1,0:T(8,128)(2,1)} %get-tuple-element.18), channel_id=1, source_target_pairs={{0,1},{1,0},{2,3},{3,2},{4,5},{5,4},{6,7},{7,6},{8,9},{9,8},{10,11... | collective-permute-start | bytes 2555912 | tf_op jit(solution)/shard_map/ppermute | solution.py:150
  144.9 42.1 %all-to-all-start.4 = ((bf16[8,128,512]{2,1,0:T(8,128)(2,1)}), bf16[8,128,512]{2,1,0:T(8,128)(2,1)}, u32[]{:S(2)}, u32[]{:S(2)}) async-start(bf16[8,128,512]{2,1,0:T(8,128)(2,1)} %bitcast.15), calls=%async_computation.4 | async-start | bytes 2097152 | tf_op jit(solution)/shard_map/all_to_all | solution.py:212
Sparse Core Ops, SparseCore 0:
  11.8 98.7 all-gather.5
  113.2 47.4 all-gather.3

commit v5 on v4

--- a/solution.py
+++ b/solution.py
@@ -121,7 +121,7 @@
     )(*args)
 
 
-def call(kernel, out_shape, scratch, flops, *args, fetched=0):
+def call(kernel, out_shape, scratch, flops, *args, fetched=0, mib=63):
     outs = [jax.ShapeDtypeStruct(shape, BF) for shape in out_shape]
     spaces = [pltpu.SMEM if a.dtype == jnp.int32 else pltpu.VMEM for a in args]
     scratches = [pltpu.VMEM(shape, BF) for shape in scratch]
@@ -135,7 +135,7 @@
         in_specs=[pl.BlockSpec(memory_space=space) for space in spaces],
         out_specs=[pl.BlockSpec(memory_space=pltpu.VMEM)] * len(outs),
         scratch_shapes=scratches,
-        compiler_params=pltpu.CompilerParams(vmem_limit_bytes=63 * 1024 * 1024),
+        compiler_params=pltpu.CompilerParams(vmem_limit_bytes=mib * 1024 * 1024),
         cost_estimate=pl.CostEstimate(
             flops=flops, bytes_accessed=sum(a.size * 2 for a in args), transcendentals=0
         ),
@@ -213,7 +213,7 @@
         grad_gate, grad_up, grad_down = call(
             functools.partial(weight_kernel, scale),
             [(units, width)] * 3, [(ny, 2, nx, part, units)] * 2, 200 * total * units * width,
-            core_id, rows, hidden_all, swapped, factors, factors_send, hidden,
+            core_id, rows, hidden_all, swapped, factors, factors_send, hidden, mib=62,
         )
 
         input_terms = tied(input_terms, grad_gate, grad_up, grad_down)

time: 197 us -> 195 us (0.990)
  no operation moved by 1% of the time
where the time goes in v5:
time: 195 us
  starting transfers between devices  72.2 us (37%)
  waiting for transfers between devices  49.4 us (25%)
  Pallas kernels  28.5 us (15%)
  blocking collectives  20.7 us (11%)
  between operations  14.4 us (7%)
  other arithmetic  5.11 us (3%)
  local copies, waits for them, and re-layouts  4.31 us (2%)
    ppermute x7, starting transfers between devices, swap_core(): return lax.ppermute(v, 'core', [(0, 1), (1, 0)])  28.6 us
    pallas_call x4, Pallas kernels, call(): pl.pallas_call(kernel, out_shape=outs, in_specs=[pl.BlockSpec(memory_spac...  27.3 us
    all_to_all x1, blocking collectives, body(): lax.all_to_all(hidden_part.reshape(ny * part, 2 * units), 'y', 0, 0, tile...  20.7 us
    all_to_all x1, waiting for transfers between devices, body(): input_terms = lax.all_to_all(input_part, 'z', 0, 0, tiled=True)  17.2 us
    all_to_all x2, waiting for transfers between devices, spread(): return lax.all_to_all(copies, axis, 0, 0, tiled=True).reshape(shape)  14.9 us
    all_to_all x1, starting transfers between devices, body(): input_terms = lax.all_to_all(input_part, 'z', 0, 0, tiled=True)  12.7 us
    ppermute x3, starting transfers between devices, shift_x(): return lax.ppermute(v, 'x', [(i, (i + s) % nx) for i in range(nx)])  11.4 us
    all_to_all x1, starting transfers between devices, body(): got = lax.all_to_all(pieces, ('x', 'z'), 0, 0, tiled=True)  10.6 us
  transfers between devices with their start and end apart: 16, of which 7 were waited for; matrix products, arithmetic and copies ran while one was open for 3% of the time, Pallas kernels for 15%

profile of v5, /device:TPU:1, one launch (start us, length us, event | category | flops | bytes accessed | tf_op | source)
XLA Modules:
  0.0 194.6 jit_solution(11642054757769305688)
XLA Ops:
  7.2 1.7 pad_maximum_fusion.2
  9.0 4.0 %collective-permute-start = (bf16[416,512]{1,0:T(8,128)(2,1)}, bf16[416,512]{1,0:T(8,128)(2,1)S(1)}, u32[]{:S(2)}, u32[]{:S(2)}) collective-permute-start(bf16[416,512]{1,0:T(8,128)(2,1)} %refs_1_.1), channel_id=1, source_target_pairs={{0,16},{16,32},{32,48},{48,0},{1,17},{17,33},{33,49},{49,1},{2,18}... | collective-permute-start | bytes 1277960 | tf_op jit(solution)/shard_map/ppermute | solution.py:147
  12.9 4.4 %collective-permute-start.1 = (bf16[416,512]{1,0:T(8,128)(2,1)}, bf16[416,512]{1,0:T(8,128)(2,1)S(1)}, u32[]{:S(2)}, u32[]{:S(2)}) collective-permute-start(bf16[416,512]{1,0:T(8,128)(2,1)} %refs_1_.1), channel_id=1, source_target_pairs={{0,32},{16,48},{32,0},{48,16},{1,33},{17,49},{33,1},{49,17},{2,34}... | collective-permute-start | bytes 1277960 | tf_op jit(solution)/shard_map/ppermute | solution.py:147
  17.3 3.1 %collective-permute-start.2 = (bf16[416,512]{1,0:T(8,128)(2,1)}, bf16[416,512]{1,0:T(8,128)(2,1)S(1)}, u32[]{:S(2)}, u32[]{:S(2)}) collective-permute-start(bf16[416,512]{1,0:T(8,128)(2,1)} %refs_1_.1), channel_id=1, source_target_pairs={{0,48},{16,0},{32,16},{48,32},{1,49},{17,1},{33,17},{49,33},{2,50}... | collective-permute-start | bytes 1277960 | tf_op jit(solution)/shard_map/ppermute | solution.py:147
  21.0 1.0 broadcast_multiply_fusion.1
  22.0 1.1 broadcast_in_dim.9
  23.1 10.6 %all-to-all-start = ((bf16[32,32,512]{2,1,0:T(8,128)(2,1)}), bf16[32,32,512]{2,1,0:T(8,128)(2,1)}, u32[]{:S(2)}, u32[]{:S(2)}) async-start(bf16[32,32,512]{2,1,0:T(8,128)(2,1)} %bitcast.2), calls=%async_computation | async-start | bytes 2097152 | tf_op jit(solution)/shard_map/all_to_all | solution.py:174
  33.7 3.7 %collective-permute-start.3 = (bf16[416,512]{1,0:T(8,128)(2,1)S(1)}, bf16[416,512]{1,0:T(8,128)(2,1)}, u32[]{:S(2)}, u32[]{:S(2)}) collective-permute-start(bf16[416,512]{1,0:T(8,128)(2,1)S(1)} %copy-done.5), channel_id=1, source_target_pairs={{0,1},{1,0},{2,3},{3,2},{4,5},{5,4},{6,7},{7,6},{8,9},{9,8},{10,11... | collective-permute-start | bytes 1277960 | tf_op jit(solution)/shard_map/ppermute | solution.py:150
  37.5 1.9 collective-permute-start.7
  39.5 2.4 %collective-permute-start.4 = (bf16[416,512]{1,0:T(8,128)(2,1)S(1)}, bf16[416,512]{1,0:T(8,128)(2,1)}, u32[]{:S(2)}, u32[]{:S(2)}) collective-permute-start(bf16[416,512]{1,0:T(8,128)(2,1)S(1)} %collective-permute-done.refs_0_.refs_2_), channel_id=1, source_target_pairs={{0,1},{1,0},{2,3},{3,2},{4,5},{5,4},{6,7},{7,6},{8,9},{9,8},{10,11... | collective-permute-start | bytes 1277960 | tf_op jit(solution)/shard_map/ppermute | solution.py:150
  41.9 1.9 collective-permute-start.5
  43.9 2.4 %collective-permute-start.6 = (bf16[416,512]{1,0:T(8,128)(2,1)S(1)}, bf16[416,512]{1,0:T(8,128)(2,1)}, u32[]{:S(2)}, u32[]{:S(2)}) collective-permute-start(bf16[416,512]{1,0:T(8,128)(2,1)S(1)} %collective-permute-done.2.refs_2_.refs_4_), channel_id=1, source_target_pairs={{0,1},{1,0},{2,3},{3,2},{4,5},{5,4},{6,7},{7,6},{8,9},{9,8},{10,11... | collective-permute-start | bytes 1277960 | tf_op jit(solution)/shard_map/ppermute | solution.py:150
  46.9 0.9 collective-permute-done.6.refs_8_
  47.8 0.9 copy-done.1
  48.7 9.5 %all-to-all-done = bf16[32,32,512]{2,1,0:T(8,128)(2,1)} async-done(((bf16[32,32,512]{2,1,0:T(8,128)(2,1)}), bf16[32,32,512]{2,1,0:T(8,128)(2,1)}, u32[]{:S(2)}, u32[]{:S(2)}) %all-to-all-start) | async-done | bytes 1048608 | tf_op jit(solution)/shard_map/all_to_all | solution.py:174
  58.2 4.3 %shard_map.112 = bf16[8,32,832]{2,1,0:T(8,128)(2,1)} custom-call(s32[1]{0:T(128)} %bitcast.x_ref, bf16[4,256,512]{2,1,0:T(8,128)(2,1)} %bitcast.3.refs_0_, bf16[416,512]{1,0:T(8,128)(2,1)} %refs_1_.1, bf16[416,512]{1,0:T(8,128)(2,1)} %copy-done.6, bf16[416,512]{1,0:T(8,128)(2,1)} %copy-done.7, bf16[416,512]{1,0:T(8,128)(2,1)} %copy-done.8, ...), custom_call_target="tpu_custom_call" | custom-call | flops 436207616 | bytes 5312514 | tf_op jit(solution)/shard_map/pallas_call | solution.py:132
  62.5 20.7 %all_to_all.38 = bf16[8,32,832]{2,1,0:T(8,128)(2,1)S(1)} all-to-all(bf16[8,32,832]{2,1,0:T(8,128)(2,1)} %shard_map.112), channel_id=1, replica_groups=mesh['y'=8,'x'=4,'z'=8,'core'=2] {'y'}, dimensions={0} | all-to-all | bytes 851968 | tf_op jit(solution)/shard_map/all_to_all | solution.py:193
  83.2 0.9 broadcast_in_dim.10
  84.1 4.5 %all-to-all-start.2 = ((bf16[8,32,832]{2,1,0:T(8,128)(2,1)}), bf16[8,32,832]{2,1,0:T(8,128)(2,1)S(1)}, u32[]{:S(2)}, u32[]{:S(2)}) async-start(bf16[8,32,832]{2,1,0:T(8,128)(2,1)} %broadcast_in_dim.10), calls=%async_computation.2 | async-start | bytes 917504 | tf_op jit(solution)/shard_map/all_to_all | solution.py:191
  89.5 14.9 %all-to-all-done.2 = bf16[8,32,832]{2,1,0:T(8,128)(2,1)S(1)} async-done(((bf16[8,32,832]{2,1,0:T(8,128)(2,1)}), bf16[8,32,832]{2,1,0:T(8,128)(2,1)S(1)}, u32[]{:S(2)}, u32[]{:S(2)}) %all-to-all-start.2) | async-done | bytes 426016 | tf_op jit(solution)/shard_map/all_to_all | solution.py:191
  104.4 1.4 broadcast_in_dim.11
  105.8 4.4 %all-to-all-start.3 = ((bf16[32,32,832]{2,1,0:T(8,128)(2,1)}), bf16[32,32,832]{2,1,0:T(8,128)(2,1)}, u32[]{:S(2)}, u32[]{:S(2)}) async-start(bf16[32,32,832]{2,1,0:T(8,128)(2,1)} %bitcast.6), calls=%async_computation.3 | async-start | bytes 3670016 | tf_op jit(solution)/shard_map/all_to_all | solution.py:191
  110.6 6.5 %shard_map.113 = (bf16[2,8,4,32,416]{4,3,2,1,0:T(8,128)(2,1)}, bf16[2,8,4,32,416]{4,3,2,1,0:T(8,128)(2,1)}, bf16[8,2,4,32,416]{4,3,2,1,0:T(8,128)(2,1)}) custom-call(s32[1]{0:T(128)} %bitcast.8.core_ref, bf16[8,2,4,32,832]{4,3,2,1,0:T(8,128)(2,1)} %bitcast.19), custom_call_target="tpu_custom_call" | custom-call | flops 12779520000 | bytes 3407874 | tf_op jit(solution)/shard_map/pallas_call | solution.py:132
  117.1 10.5 %collective-permute-start.8 = (bf16[2,8,4,32,416]{4,3,2,1,0:T(8,128)(2,1)}, bf16[2,8,4,32,416]{4,3,2,1,0:T(8,128)(2,1)}, u32[]{:S(2)}, u32[]{:S(2)}) collective-permute-start(bf16[2,8,4,32,416]{4,3,2,1,0:T(8,128)(2,1)} %get-tuple-element.15.send_ref), channel_id=1, source_target_pairs={{0,1},{1,0},{2,3},{3,2},{4,5},{5,4},{6,7},{7,6},{8,9},{9,8},{10,11... | collective-permute-start | bytes 5111816 | tf_op jit(solution)/shard_map/ppermute | solution.py:150
  128.2 3.5 %collective-permute-done.8.refs_3_ = bf16[2,8,4,32,416]{4,3,2,1,0:T(8,128)(2,1)} collective-permute-done((bf16[2,8,4,32,416]{4,3,2,1,0:T(8,128)(2,1)}, bf16[2,8,4,32,416]{4,3,2,1,0:T(8,128)(2,1)}, u32[]{:S(2)}, u32[]{:S(2)}) %collective-permute-start.8) | collective-permute-done | bytes 1703968 | tf_op jit(solution)/shard_map/ppermute | solution.py:150
  131.7 7.5 %shard_map.115 = (bf16[1024,512]{1,0:T(8,128)(2,1)}, bf16[4,8,32,416]{3,2,1,0:T(8,128)(2,1)}) custom-call(bf16[4,8,32,832]{3,2,1,0:T(8,128)(2,1)} %bitcast.7.refs_0_.hg_ref, bf16[2,8,4,32,416]{4,3,2,1,0:T(8,128)(2,1)} %get-tuple-element.14.refs_1_.own_ref, bf16[832,512]{1,0:T(8,128)(2,1)} %copy-done, ...), custom_call_target="tpu_custom_call" | custom-call | flops 872415232 | bytes 6819840 | tf_op jit(solution)/shard_map/pallas_call | solution.py:132
  139.2 5.7 %collective-permute-start.9 = (bf16[4,8,32,416]{3,2,1,0:T(8,128)(2,1)}, bf16[4,8,32,416]{3,2,1,0:T(8,128)(2,1)}, u32[]{:S(2)}, u32[]{:S(2)}) collective-permute-start(bf16[4,8,32,416]{3,2,1,0:T(8,128)(2,1)} %get-tuple-element.18), channel_id=1, source_target_pairs={{0,1},{1,0},{2,3},{3,2},{4,5},{5,4},{6,7},{7,6},{8,9},{9,8},{10,11... | collective-permute-start | bytes 2555912 | tf_op jit(solution)/shard_map/ppermute | solution.py:150
  144.9 12.7 %all-to-all-start.4 = ((bf16[8,128,512]{2,1,0:T(8,128)(2,1)}), bf16[8,128,512]{2,1,0:T(8,128)(2,1)S(1)}, u32[]{:S(2)}, u32[]{:S(2)}) async-start(bf16[8,128,512]{2,1,0:T(8,128)(2,1)} %bitcast.15), calls=%async_computation.4 | async-start | bytes 2097152 | tf_op jit(solution)/shard_map/all_to_all | solution.py:212
  157.6 3.2 %all-gather.4.cloned.1.call-done.rows_ref = bf16[2048,1024]{1,0:T(8,128)(2,1)} async-done(((bf16[128,1024]{1,0:T(8,128)(2,1)}), bf16[2048,1024]{1,0:T(8,128)(2,1)}) %all-gather.4.cloned.1.call-update) | async-done | bytes 4194320 | tf_op jit(solution)/shard_map/all_gather | solution.py:183
  160.8 9.0 %shard_map.116 = (bf16[416,512]{1,0:T(8,128)(2,1)}, bf16[416,512]{1,0:T(8,128)(2,1)}, bf16[416,512]{1,0:T(8,128)(2,1)}) custom-call(s32[1]{0:T(128)} %bitcast.8.core_ref, bf16[2048,1024]{1,0:T(8,128)(2,1)} %all-gather.4.cloned.1.call-done.rows_ref, bf16[4,8,32,832]{3,2,1,0:T(8,128)(2,1)} %bitcast.7.refs_0_.hg_ref, ...), custom_call_target="tpu_custom_call" | custom-call | flops 87241523200 | bytes 11862018 | tf_op jit(solution)/shard_map/pallas_call | solution.py:132
  169.8 17.2 %all-to-all-done.4 = bf16[8,128,512]{2,1,0:T(8,128)(2,1)S(1)} async-done(((bf16[8,128,512]{2,1,0:T(8,128)(2,1)}), bf16[8,128,512]{2,1,0:T(8,128)(2,1)S(1)}, u32[]{:S(2)}, u32[]{:S(2)}) %all-to-all-start.4) | async-done | bytes 1048608 | tf_op jit(solution)/shard_map/all_to_all | solution.py:212
  186.9 0.8 reduce_sum.25
  (40 shorter events, 3.3 us)
Async XLA Ops:
  7.2 26.5 %copy-start.5 = (bf16[416,512]{1,0:T(8,128)(2,1)S(1)}, bf16[416,512]{1,0:T(8,128)(2,1)}, u32[]{:S(2)}) copy-start(bf16[416,512]{1,0:T(8,128)(2,1)} %refs_1_.1) | copy-start | bytes 1277956
  7.2 30.2 %copy-start.3 = (bf16[512,416]{0,1:T(8,128)(2,1)S(1)}, bf16[512,416]{0,1:T(8,128)(2,1)}, u32[]{:S(2)}) copy-start(bf16[512,416]{0,1:T(8,128)(2,1)} %param.13) | copy-start | bytes 1277956
  7.2 30.2 %copy-start.4 = (bf16[512,416]{0,1:T(8,128)(2,1)S(1)}, bf16[512,416]{0,1:T(8,128)(2,1)}, u32[]{:S(2)}) copy-start(bf16[512,416]{0,1:T(8,128)(2,1)} %param.12) | copy-start | bytes 1277956
  7.2 103.4 %all-gather.6.cloned.1.call-start = ((), (), s32[]{:S(2)}) async-start(), calls=%async_computation.6 | async-start | bytes 3784704 | tf_op jit(solution)/shard_map/all_gather | solution.py:171
  9.0 30.5 %collective-permute-start = (bf16[416,512]{1,0:T(8,128)(2,1)}, bf16[416,512]{1,0:T(8,128)(2,1)S(1)}, u32[]{:S(2)}, u32[]{:S(2)}) collective-permute-start(bf16[416,512]{1,0:T(8,128)(2,1)} %refs_1_.1), channel_id=1, source_target_pairs={{0,16},{16,32},{32,48},{48,0},{1,17},{17,33},{33,49},{49,1},{2,18}... | collective-permute-start | bytes 1277960 | tf_op jit(solution)/shard_map/ppermute | solution.py:147
  12.9 29.0 %collective-permute-start.1 = (bf16[416,512]{1,0:T(8,128)(2,1)}, bf16[416,512]{1,0:T(8,128)(2,1)S(1)}, u32[]{:S(2)}, u32[]{:S(2)}) collective-permute-start(bf16[416,512]{1,0:T(8,128)(2,1)} %refs_1_.1), channel_id=1, source_target_pairs={{0,32},{16,48},{32,0},{48,16},{1,33},{17,49},{33,1},{49,17},{2,34}... | collective-permute-start | bytes 1277960 | tf_op jit(solution)/shard_map/ppermute | solution.py:147
  17.3 26.6 %collective-permute-start.2 = (bf16[416,512]{1,0:T(8,128)(2,1)}, bf16[416,512]{1,0:T(8,128)(2,1)S(1)}, u32[]{:S(2)}, u32[]{:S(2)}) collective-permute-start(bf16[416,512]{1,0:T(8,128)(2,1)} %refs_1_.1), channel_id=1, source_target_pairs={{0,48},{16,0},{32,16},{48,32},{1,49},{17,1},{33,17},{49,33},{2,50}... | collective-permute-start | bytes 1277960 | tf_op jit(solution)/shard_map/ppermute | solution.py:147
  23.1 35.1 %all-to-all-start = ((bf16[32,32,512]{2,1,0:T(8,128)(2,1)}), bf16[32,32,512]{2,1,0:T(8,128)(2,1)}, u32[]{:S(2)}, u32[]{:S(2)}) async-start(bf16[32,32,512]{2,1,0:T(8,128)(2,1)} %bitcast.2), calls=%async_computation | async-start | bytes 2097152 | tf_op jit(solution)/shard_map/all_to_all | solution.py:174
  33.7 13.2 %collective-permute-start.3 = (bf16[416,512]{1,0:T(8,128)(2,1)S(1)}, bf16[416,512]{1,0:T(8,128)(2,1)}, u32[]{:S(2)}, u32[]{:S(2)}) collective-permute-start(bf16[416,512]{1,0:T(8,128)(2,1)S(1)} %copy-done.5), channel_id=1, source_target_pairs={{0,1},{1,0},{2,3},{3,2},{4,5},{5,4},{6,7},{7,6},{8,9},{9,8},{10,11... | collective-permute-start | bytes 1277960 | tf_op jit(solution)/shard_map/ppermute | solution.py:150
  37.5 9.4 %copy-start = (bf16[832,512]{1,0:T(8,128)(2,1)}, bf16[832,512]{1,0:T(8,128)(2,1)S(1)}, u32[]{:S(2)}) copy-start(bf16[832,512]{1,0:T(8,128)(2,1)S(1)} %pad_maximum_fusion.refs_2_) | copy-start | bytes 2555908
  37.5 10.3 %collective-permute-start.7 = (bf16[832,512]{1,0:T(8,128)(2,1)S(1)}, bf16[832,512]{1,0:T(8,128)(2,1)S(1)}, u32[]{:S(2)}, u32[]{:S(2)}) collective-permute-start(bf16[832,512]{1,0:T(8,128)(2,1)S(1)} %pad_maximum_fusion.refs_2_), channel_id=1, source_target_pairs={{0,1},{1,0},{2,3},{3,2},{4,5},{5,4},{6,7},{7,6},{8,9},{9,8},{10,11... | collective-permute-start | bytes 2555912 | tf_op jit(solution)/shard_map/ppermute | solution.py:150
  39.5 6.8 %copy-start.6 = (bf16[416,512]{1,0:T(8,128)(2,1)}, bf16[416,512]{1,0:T(8,128)(2,1)S(1)}, u32[]{:S(2)}) copy-start(bf16[416,512]{1,0:T(8,128)(2,1)S(1)} %collective-permute-done.refs_0_.refs_2_) | copy-start | bytes 1277956
  39.5 7.4 %collective-permute-start.4 = (bf16[416,512]{1,0:T(8,128)(2,1)S(1)}, bf16[416,512]{1,0:T(8,128)(2,1)}, u32[]{:S(2)}, u32[]{:S(2)}) collective-permute-start(bf16[416,512]{1,0:T(8,128)(2,1)S(1)} %collective-permute-done.refs_0_.refs_2_), channel_id=1, source_target_pairs={{0,1},{1,0},{2,3},{3,2},{4,5},{5,4},{6,7},{7,6},{8,9},{9,8},{10,11... | collective-permute-start | bytes 1277960 | tf_op jit(solution)/shard_map/ppermute | solution.py:150
  41.9 4.4 %copy-start.7 = (bf16[416,512]{1,0:T(8,128)(2,1)}, bf16[416,512]{1,0:T(8,128)(2,1)S(1)}, u32[]{:S(2)}) copy-start(bf16[416,512]{1,0:T(8,128)(2,1)S(1)} %collective-permute-done.1.refs_1_.refs_3_) | copy-start | bytes 1277956
  41.9 5.0 %collective-permute-start.5 = (bf16[416,512]{1,0:T(8,128)(2,1)S(1)}, bf16[416,512]{1,0:T(8,128)(2,1)}, u32[]{:S(2)}, u32[]{:S(2)}) collective-permute-start(bf16[416,512]{1,0:T(8,128)(2,1)S(1)} %collective-permute-done.1.refs_1_.refs_3_), channel_id=1, source_target_pairs={{0,1},{1,0},{2,3},{3,2},{4,5},{5,4},{6,7},{7,6},{8,9},{9,8},{10,11... | collective-permute-start | bytes 1277960 | tf_op jit(solution)/shard_map/ppermute | solution.py:150
  43.8 2.4 %copy-start.8 = (bf16[416,512]{1,0:T(8,128)(2,1)}, bf16[416,512]{1,0:T(8,128)(2,1)S(1)}, u32[]{:S(2)}) copy-start(bf16[416,512]{1,0:T(8,128)(2,1)S(1)} %collective-permute-done.2.refs_2_.refs_4_) | copy-start | bytes 1277956
  43.9 3.9 %collective-permute-start.6 = (bf16[416,512]{1,0:T(8,128)(2,1)S(1)}, bf16[416,512]{1,0:T(8,128)(2,1)}, u32[]{:S(2)}, u32[]{:S(2)}) collective-permute-start(bf16[416,512]{1,0:T(8,128)(2,1)S(1)} %collective-permute-done.2.refs_2_.refs_4_), channel_id=1, source_target_pairs={{0,1},{1,0},{2,3},{3,2},{4,5},{5,4},{6,7},{7,6},{8,9},{9,8},{10,11... | collective-permute-start | bytes 1277960 | tf_op jit(solution)/shard_map/ppermute | solution.py:150
  47.8 0.9 copy-start.1
  62.4 26.2 %copy-start.2 = (bf16[128,512]{1,0:T(8,128)(2,1)S(1)}, bf16[128,512]{1,0:T(8,128)(2,1)}, u32[]{:S(2)}) copy-start(bf16[128,512]{1,0:T(8,128)(2,1)} %param.9) | copy-start | bytes 393220
  62.4 26.3 %copy-start.9 = (bf16[128,512]{1,0:T(8,128)(2,1)S(1)}, bf16[128,512]{1,0:T(8,128)(2,1)}, u32[]{:S(2)}) copy-start(bf16[128,512]{1,0:T(8,128)(2,1)} %param.8) | copy-start | bytes 393220
  84.1 20.3 %all-to-all-start.2 = ((bf16[8,32,832]{2,1,0:T(8,128)(2,1)}), bf16[8,32,832]{2,1,0:T(8,128)(2,1)S(1)}, u32[]{:S(2)}, u32[]{:S(2)}) async-start(bf16[8,32,832]{2,1,0:T(8,128)(2,1)} %broadcast_in_dim.10), calls=%async_computation.2 | async-start | bytes 917504 | tf_op jit(solution)/shard_map/all_to_all | solution.py:191
  88.6 72.2 %all-gather.4.cloned.1.call-start = ((), (), s32[]{:S(2)}) async-start(), calls=%async_computation.5 | async-start | bytes 4456448 | tf_op jit(solution)/shard_map/all_gather | solution.py:183
  105.8 21.7 %all-to-all-start.3 = ((bf16[32,32,832]{2,1,0:T(8,128)(2,1)}), bf16[32,32,832]{2,1,0:T(8,128)(2,1)}, u32[]{:S(2)}, u32[]{:S(2)}) async-start(bf16[32,32,832]{2,1,0:T(8,128)(2,1)} %bitcast.6), calls=%async_computation.3 | async-start | bytes 3670016 | tf_op jit(solution)/shard_map/all_to_all | solution.py:191
  117.1 14.6 %collective-permute-start.8 = (bf16[2,8,4,32,416]{4,3,2,1,0:T(8,128)(2,1)}, bf16[2,8,4,32,416]{4,3,2,1,0:T(8,128)(2,1)}, u32[]{:S(2)}, u32[]{:S(2)}) collective-permute-start(bf16[2,8,4,32,416]{4,3,2,1,0:T(8,128)(2,1)} %get-tuple-element.15.send_ref), channel_id=1, source_target_pairs={{0,1},{1,0},{2,3},{3,2},{4,5},{5,4},{6,7},{7,6},{8,9},{9,8},{10,11... | collective-permute-start | bytes 5111816 | tf_op jit(solution)/shard_map/ppermute | solution.py:150
  139.2 18.4 %collective-permute-start.9 = (bf16[4,8,32,416]{3,2,1,0:T(8,128)(2,1)}, bf16[4,8,32,416]{3,2,1,0:T(8,128)(2,1)}, u32[]{:S(2)}, u32[]{:S(2)}) collective-permute-start(bf16[4,8,32,416]{3,2,1,0:T(8,128)(2,1)} %get-tuple-element.18), channel_id=1, source_target_pairs={{0,1},{1,0},{2,3},{3,2},{4,5},{5,4},{6,7},{7,6},{8,9},{9,8},{10,11... | collective-permute-start | bytes 2555912 | tf_op jit(solution)/shard_map/ppermute | solution.py:150
  144.9 42.0 %all-to-all-start.4 = ((bf16[8,128,512]{2,1,0:T(8,128)(2,1)}), bf16[8,128,512]{2,1,0:T(8,128)(2,1)S(1)}, u32[]{:S(2)}, u32[]{:S(2)}) async-start(bf16[8,128,512]{2,1,0:T(8,128)(2,1)} %bitcast.15), calls=%async_computation.4 | async-start | bytes 2097152 | tf_op jit(solution)/shard_map/all_to_all | solution.py:212
Sparse Core Ops, SparseCore 0:
  11.8 98.7 all-gather.5
  113.2 47.4 all-gather.3

commit v6 on v5

--- a/solution.py
+++ b/solution.py
@@ -39,6 +39,21 @@
             total = term if total is None else total + term
         total = total.astype(BF).reshape(ny, part, units)
         out_ref[:, :, half * units : (half + 1) * units] = total
+
+
+def piece_kernel(grad_ref, keep_ref, out_ref):
+    nx, nz, part, _ = out_ref.shape
+    for x in range(nx):
+        cut = slice(x * part, (x + 1) * part)
+        block = grad_ref[cut, :] * keep_ref[cut, :]
+        for z in range(nz):
+            out_ref[x, z] = block
+
+
+def sum_kernel(terms_ref, out_ref):
+    total = jnp.sum(terms_ref[...].astype(F32), axis=0).astype(BF)
+    for y in range(out_ref.shape[0]):
+        out_ref[y] = total
 
 
 def factor_kernel(core_ref, saved_ref, own_ref, send_ref, hidden_ref):
@@ -164,10 +179,10 @@
         w_other = swap_core(both_w)
 
         keep = (segment_ids % 2 == 1).astype(BF)
-        masked = out_grad * keep[:, None]
-        pieces = jnp.broadcast_to(
-            masked.reshape(nx, 1, part, width), (nx, nz, part, width)
-        ).reshape(nx * nz * part, width)
+        (pieces,) = call(
+            piece_kernel, [(nx, nz, part, width)], [], 10**6, out_grad, keep[:, None], mib=16
+        )
+        pieces = pieces.reshape(nx * nz * part, width)
         saved = lax.all_gather(
             tied(jnp.concatenate([gate_pre, up_pre], axis=1), pieces), ("y", "x"), axis=0
         ).reshape(ny, 2, nx, part, 2 * units)
@@ -193,8 +208,10 @@
         terms = lax.all_to_all(
             hidden_part.reshape(ny * part, 2 * units), "y", 0, 0, tiled=True
         ).reshape(ny, part, 2 * units)
-        hidden_sum = jnp.sum(terms.astype(F32), axis=0).astype(BF)
-        hidden_y = spread(hidden_sum, "y", ny)
+        (copies,) = call(sum_kernel, [(ny, part, 2 * units)], [], 10**6, terms, mib=16)
+        hidden_y = lax.all_to_all(
+            copies.reshape(ny * part, 2 * units), "y", 0, 0, tiled=True
+        ).reshape(ny, part, 2 * units)
         hidden_all = spread(hidden_y, "x", nx)
 
         pair = (2, ny, nx, part, units)

time: 195 us -> 196 us (level)
  Pallas kernels: 28.5 us -> 30.5 us
    all_to_all x0 -> x1, waiting for transfers between devices: none -> 14.9 us  [body(): lax.all_to_all(copies.reshape(ny * part, 2 * units), 'y', 0, 0, tiled=True)]
    all_to_all x2 -> x1, waiting for transfers between devices: 14.9 us -> 0.01 us  [spread(): return lax.all_to_all(copies, axis, 0, 0, tiled=True).reshape(shape)]
    all_to_all x0 -> x1, starting transfers between devices: none -> 4.57 us  [body(): lax.all_to_all(copies.reshape(ny * part, 2 * units), 'y', 0, 0, tiled=True)]
    all_to_all x2 -> x1, starting transfers between devices: 8.89 us -> 4.44 us  [spread(): return lax.all_to_all(copies, axis, 0, 0, tiled=True).reshape(shape)]
    pallas_call x4 -> x6, Pallas kernels: 27.3 us -> 29.3 us  [call(): pl.pallas_call(kernel, out_shape=outs, in_specs=[pl.BlockSpec(memory_spac...]
  transfers between devices with their start and end apart: 16 -> 16, of which waited for: 7 -> 7; matrix products, arithmetic and copies ran while one was open for 3% -> 2% of each run, Pallas kernels for 15% -> 16%
where the time goes in v6:
time: 196 us; the launch traced here: 195 us
  starting transfers between devices  72.3 us (37%)
  waiting for transfers between devices  49.2 us (25%)
  Pallas kernels  30.5 us (16%)
  blocking collectives  20.8 us (11%)
  between operations  14.4 us (7%)
  other arithmetic  3.97 us (2%)
  local copies, waits for them, and re-layouts  3.43 us (2%)
    pallas_call x6, Pallas kernels, call(): pl.pallas_call(kernel, out_shape=outs, in_specs=[pl.BlockSpec(memory_spac...  29.3 us
    ppermute x7, starting transfers between devices, swap_core(): return lax.ppermute(v, 'core', [(0, 1), (1, 0)])  28.8 us
    all_to_all x1, blocking collectives, body(): lax.all_to_all(hidden_part.reshape(ny * part, 2 * units), 'y', 0, 0, tile...  20.8 us
    all_to_all x1, waiting for transfers between devices, body(): input_terms = lax.all_to_all(input_part, 'z', 0, 0, tiled=True)  17.3 us
    all_to_all x1, waiting for transfers between devices, body(): lax.all_to_all(copies.reshape(ny * part, 2 * units), 'y', 0, 0, tiled=True)  14.9 us
    all_to_all x1, starting transfers between devices, body(): input_terms = lax.all_to_all(input_part, 'z', 0, 0, tiled=True)  12.5 us
    ppermute x3, starting transfers between devices, shift_x(): return lax.ppermute(v, 'x', [(i, (i + s) % nx) for i in range(nx)])  11.4 us
    all_to_all x1, starting transfers between devices, body(): got = lax.all_to_all(pieces, ('x', 'z'), 0, 0, tiled=True)  10.6 us
  transfers between devices with their start and end apart: 16, of which 7 were waited for; matrix products, arithmetic and copies ran while one was open for 2% of the time, Pallas kernels for 16%

profile of v6, /device:TPU:1, one launch (start us, length us, event | category | flops | bytes accessed | tf_op | source)
XLA Modules:
  0.0 194.6 jit_solution(2038031720061416399)
XLA Ops:
  7.2 1.6 pad_maximum_fusion.2
  8.8 4.0 %collective-permute-start = (bf16[416,512]{1,0:T(8,128)(2,1)}, bf16[416,512]{1,0:T(8,128)(2,1)S(1)}, u32[]{:S(2)}, u32[]{:S(2)}) collective-permute-start(bf16[416,512]{1,0:T(8,128)(2,1)} %refs_1_.1), channel_id=1, source_target_pairs={{0,16},{16,32},{32,48},{48,0},{1,17},{17,33},{33,49},{49,1},{2,18}... | collective-permute-start | bytes 1277960 | tf_op jit(solution)/shard_map/ppermute | solution.py:162
  12.8 4.4 %collective-permute-start.1 = (bf16[416,512]{1,0:T(8,128)(2,1)}, bf16[416,512]{1,0:T(8,128)(2,1)S(1)}, u32[]{:S(2)}, u32[]{:S(2)}) collective-permute-start(bf16[416,512]{1,0:T(8,128)(2,1)} %refs_1_.1), channel_id=1, source_target_pairs={{0,32},{16,48},{32,0},{48,16},{1,33},{17,49},{33,1},{49,17},{2,34}... | collective-permute-start | bytes 1277960 | tf_op jit(solution)/shard_map/ppermute | solution.py:162
  17.2 3.0 %collective-permute-start.2 = (bf16[416,512]{1,0:T(8,128)(2,1)}, bf16[416,512]{1,0:T(8,128)(2,1)S(1)}, u32[]{:S(2)}, u32[]{:S(2)}) collective-permute-start(bf16[416,512]{1,0:T(8,128)(2,1)} %refs_1_.1), channel_id=1, source_target_pairs={{0,48},{16,0},{32,16},{48,32},{1,49},{17,1},{33,17},{49,33},{2,50}... | collective-permute-start | bytes 1277960 | tf_op jit(solution)/shard_map/ppermute | solution.py:162
  21.1 0.9 copy-done
  22.0 1.1 shard_map.111
  23.1 10.6 %all-to-all-start = ((bf16[32,32,512]{2,1,0:T(8,128)(2,1)}), bf16[32,32,512]{2,1,0:T(8,128)(2,1)}, u32[]{:S(2)}, u32[]{:S(2)}) async-start(bf16[32,32,512]{2,1,0:T(8,128)(2,1)} %bitcast.2), calls=%async_computation | async-start | bytes 2097152 | tf_op jit(solution)/shard_map/all_to_all | solution.py:189
  33.7 3.7 %collective-permute-start.3 = (bf16[416,512]{1,0:T(8,128)(2,1)S(1)}, bf16[416,512]{1,0:T(8,128)(2,1)}, u32[]{:S(2)}, u32[]{:S(2)}) collective-permute-start(bf16[416,512]{1,0:T(8,128)(2,1)S(1)} %copy-done.6), channel_id=1, source_target_pairs={{0,1},{1,0},{2,3},{3,2},{4,5},{5,4},{6,7},{7,6},{8,9},{9,8},{10,11... | collective-permute-start | bytes 1277960 | tf_op jit(solution)/shard_map/ppermute | solution.py:165
  37.5 1.9 collective-permute-start.7
  39.4 2.4 %collective-permute-start.4 = (bf16[416,512]{1,0:T(8,128)(2,1)S(1)}, bf16[416,512]{1,0:T(8,128)(2,1)}, u32[]{:S(2)}, u32[]{:S(2)}) collective-permute-start(bf16[416,512]{1,0:T(8,128)(2,1)S(1)} %collective-permute-done.refs_0_.refs_2_), channel_id=1, source_target_pairs={{0,1},{1,0},{2,3},{3,2},{4,5},{5,4},{6,7},{7,6},{8,9},{9,8},{10,11... | collective-permute-start | bytes 1277960 | tf_op jit(solution)/shard_map/ppermute | solution.py:165
  41.9 1.9 collective-permute-start.5
  43.8 2.4 %collective-permute-start.6 = (bf16[416,512]{1,0:T(8,128)(2,1)S(1)}, bf16[416,512]{1,0:T(8,128)(2,1)}, u32[]{:S(2)}, u32[]{:S(2)}) collective-permute-start(bf16[416,512]{1,0:T(8,128)(2,1)S(1)} %collective-permute-done.2.refs_2_.refs_4_), channel_id=1, source_target_pairs={{0,1},{1,0},{2,3},{3,2},{4,5},{5,4},{6,7},{7,6},{8,9},{9,8},{10,11... | collective-permute-start | bytes 1277960 | tf_op jit(solution)/shard_map/ppermute | solution.py:165
  46.9 0.9 collective-permute-done.6.refs_8_
  47.7 0.9 copy-done.3
  48.6 9.5 %all-to-all-done = bf16[32,32,512]{2,1,0:T(8,128)(2,1)} async-done(((bf16[32,32,512]{2,1,0:T(8,128)(2,1)}), bf16[32,32,512]{2,1,0:T(8,128)(2,1)}, u32[]{:S(2)}, u32[]{:S(2)}) %all-to-all-start) | async-done | bytes 1048608 | tf_op jit(solution)/shard_map/all_to_all | solution.py:189
  58.1 4.3 %shard_map.113 = bf16[8,32,832]{2,1,0:T(8,128)(2,1)} custom-call(s32[1]{0:T(128)} %bitcast.x_ref, bf16[4,256,512]{2,1,0:T(8,128)(2,1)} %bitcast.3.refs_0_, bf16[416,512]{1,0:T(8,128)(2,1)} %refs_1_.1, bf16[416,512]{1,0:T(8,128)(2,1)} %copy-done.7, bf16[416,512]{1,0:T(8,128)(2,1)} %copy-done.8, bf16[416,512]{1,0:T(8,128)(2,1)} %copy-done.9, ...), custom_call_target="tpu_custom_call" | custom-call | flops 436207616 | bytes 5312514 | tf_op jit(solution)/shard_map/pallas_call | solution.py:147
  62.4 20.8 %all_to_all.38.terms_ref = bf16[8,32,832]{2,1,0:T(8,128)(2,1)S(1)} all-to-all(bf16[8,32,832]{2,1,0:T(8,128)(2,1)} %shard_map.113), channel_id=1, replica_groups=mesh['y'=8,'x'=4,'z'=8,'core'=2] {'y'}, dimensions={0} | all-to-all | bytes 851968 | tf_op jit(solution)/shard_map/all_to_all | solution.py:208
  83.2 0.9 shard_map.114
  84.1 4.6 %all-to-all-start.2 = ((bf16[8,32,832]{2,1,0:T(8,128)(2,1)}), bf16[8,32,832]{2,1,0:T(8,128)(2,1)S(1)}, u32[]{:S(2)}, u32[]{:S(2)}) async-start(bf16[8,32,832]{2,1,0:T(8,128)(2,1)} %shard_map.114), calls=%async_computation.2 | async-start | bytes 917504 | tf_op jit(solution)/shard_map/all_to_all | solution.py:212
  89.6 14.9 %all-to-all-done.2 = bf16[8,32,832]{2,1,0:T(8,128)(2,1)S(1)} async-done(((bf16[8,32,832]{2,1,0:T(8,128)(2,1)}), bf16[8,32,832]{2,1,0:T(8,128)(2,1)S(1)}, u32[]{:S(2)}, u32[]{:S(2)}) %all-to-all-start.2) | async-done | bytes 426016 | tf_op jit(solution)/shard_map/all_to_all | solution.py:212
  104.5 1.4 broadcast_in_dim.10
  106.0 4.4 %all-to-all-start.3 = ((bf16[32,32,832]{2,1,0:T(8,128)(2,1)}), bf16[32,32,832]{2,1,0:T(8,128)(2,1)}, u32[]{:S(2)}, u32[]{:S(2)}) async-start(bf16[32,32,832]{2,1,0:T(8,128)(2,1)} %bitcast.6), calls=%async_computation.3 | async-start | bytes 3670016 | tf_op jit(solution)/shard_map/all_to_all | solution.py:206
  110.5 6.5 %shard_map.115 = (bf16[2,8,4,32,416]{4,3,2,1,0:T(8,128)(2,1)}, bf16[2,8,4,32,416]{4,3,2,1,0:T(8,128)(2,1)}, bf16[8,2,4,32,416]{4,3,2,1,0:T(8,128)(2,1)}) custom-call(s32[1]{0:T(128)} %bitcast.8.core_ref, bf16[8,2,4,32,832]{4,3,2,1,0:T(8,128)(2,1)} %bitcast.19), custom_call_target="tpu_custom_call" | custom-call | flops 12779520000 | bytes 3407874 | tf_op jit(solution)/shard_map/pallas_call | solution.py:147
  117.0 10.5 %collective-permute-start.8 = (bf16[2,8,4,32,416]{4,3,2,1,0:T(8,128)(2,1)}, bf16[2,8,4,32,416]{4,3,2,1,0:T(8,128)(2,1)}, u32[]{:S(2)}, u32[]{:S(2)}) collective-permute-start(bf16[2,8,4,32,416]{4,3,2,1,0:T(8,128)(2,1)} %get-tuple-element.15.send_ref), channel_id=1, source_target_pairs={{0,1},{1,0},{2,3},{3,2},{4,5},{5,4},{6,7},{7,6},{8,9},{9,8},{10,11... | collective-permute-start | bytes 5111816 | tf_op jit(solution)/shard_map/ppermute | solution.py:165
  128.1 3.5 %collective-permute-done.8.refs_3_ = bf16[2,8,4,32,416]{4,3,2,1,0:T(8,128)(2,1)} collective-permute-done((bf16[2,8,4,32,416]{4,3,2,1,0:T(8,128)(2,1)}, bf16[2,8,4,32,416]{4,3,2,1,0:T(8,128)(2,1)}, u32[]{:S(2)}, u32[]{:S(2)}) %collective-permute-start.8) | collective-permute-done | bytes 1703968 | tf_op jit(solution)/shard_map/ppermute | solution.py:165
  131.6 7.5 %shard_map.117 = (bf16[1024,512]{1,0:T(8,128)(2,1)}, bf16[4,8,32,416]{3,2,1,0:T(8,128)(2,1)}) custom-call(bf16[4,8,32,832]{3,2,1,0:T(8,128)(2,1)} %bitcast.7.refs_0_.hg_ref, bf16[2,8,4,32,416]{4,3,2,1,0:T(8,128)(2,1)} %get-tuple-element.14.refs_1_.own_ref, bf16[832,512]{1,0:T(8,128)(2,1)} %copy-done.2, ...), custom_call_target="tpu_custom_call" | custom-call | flops 872415232 | bytes 6819840 | tf_op jit(solution)/shard_map/pallas_call | solution.py:147
  139.2 5.9 %collective-permute-start.9 = (bf16[4,8,32,416]{3,2,1,0:T(8,128)(2,1)}, bf16[4,8,32,416]{3,2,1,0:T(8,128)(2,1)}, u32[]{:S(2)}, u32[]{:S(2)}) collective-permute-start(bf16[4,8,32,416]{3,2,1,0:T(8,128)(2,1)} %get-tuple-element.18), channel_id=1, source_target_pairs={{0,1},{1,0},{2,3},{3,2},{4,5},{5,4},{6,7},{7,6},{8,9},{9,8},{10,11... | collective-permute-start | bytes 2555912 | tf_op jit(solution)/shard_map/ppermute | solution.py:165
  145.1 12.5 %all-to-all-start.4 = ((bf16[8,128,512]{2,1,0:T(8,128)(2,1)}), bf16[8,128,512]{2,1,0:T(8,128)(2,1)S(1)}, u32[]{:S(2)}, u32[]{:S(2)}) async-start(bf16[8,128,512]{2,1,0:T(8,128)(2,1)} %bitcast.16), calls=%async_computation.4 | async-start | bytes 2097152 | tf_op jit(solution)/shard_map/all_to_all | solution.py:229
  157.6 3.0 %all-gather.4.cloned.1.call-done.rows_ref = bf16[2048,1024]{1,0:T(8,128)(2,1)} async-done(((bf16[128,1024]{1,0:T(8,128)(2,1)}), bf16[2048,1024]{1,0:T(8,128)(2,1)}) %all-gather.4.cloned.1.call-update) | async-done | bytes 4194320 | tf_op jit(solution)/shard_map/all_gather | solution.py:198
  160.7 9.0 %shard_map.118 = (bf16[416,512]{1,0:T(8,128)(2,1)}, bf16[416,512]{1,0:T(8,128)(2,1)}, bf16[416,512]{1,0:T(8,128)(2,1)}) custom-call(s32[1]{0:T(128)} %bitcast.8.core_ref, bf16[2048,1024]{1,0:T(8,128)(2,1)} %all-gather.4.cloned.1.call-done.rows_ref, bf16[4,8,32,832]{3,2,1,0:T(8,128)(2,1)} %bitcast.7.refs_0_.hg_ref, ...), custom_call_target="tpu_custom_call" | custom-call | flops 87241523200 | bytes 11862018 | tf_op jit(solution)/shard_map/pallas_call | solution.py:147
  169.7 17.3 %all-to-all-done.4 = bf16[8,128,512]{2,1,0:T(8,128)(2,1)S(1)} async-done(((bf16[8,128,512]{2,1,0:T(8,128)(2,1)}), bf16[8,128,512]{2,1,0:T(8,128)(2,1)S(1)}, u32[]{:S(2)}, u32[]{:S(2)}) %all-to-all-start.4) | async-done | bytes 1048608 | tf_op jit(solution)/shard_map/all_to_all | solution.py:229
  186.9 0.8 reduce_sum.12
  (44 shorter events, 3.2 us)
Async XLA Ops:
  7.2 103.4 %all-gather.6.cloned.1.call-start = ((), (), s32[]{:S(2)}) async-start(), calls=%async_computation.6 | async-start | bytes 3784704 | tf_op jit(solution)/shard_map/all_gather | solution.py:186
  8.8 30.6 %collective-permute-start = (bf16[416,512]{1,0:T(8,128)(2,1)}, bf16[416,512]{1,0:T(8,128)(2,1)S(1)}, u32[]{:S(2)}, u32[]{:S(2)}) collective-permute-start(bf16[416,512]{1,0:T(8,128)(2,1)} %refs_1_.1), channel_id=1, source_target_pairs={{0,16},{16,32},{32,48},{48,0},{1,17},{17,33},{33,49},{49,1},{2,18}... | collective-permute-start | bytes 1277960 | tf_op jit(solution)/shard_map/ppermute | solution.py:162
  12.8 29.0 %collective-permute-start.1 = (bf16[416,512]{1,0:T(8,128)(2,1)}, bf16[416,512]{1,0:T(8,128)(2,1)S(1)}, u32[]{:S(2)}, u32[]{:S(2)}) collective-permute-start(bf16[416,512]{1,0:T(8,128)(2,1)} %refs_1_.1), channel_id=1, source_target_pairs={{0,32},{16,48},{32,0},{48,16},{1,33},{17,49},{33,1},{49,17},{2,34}... | collective-permute-start | bytes 1277960 | tf_op jit(solution)/shard_map/ppermute | solution.py:162
  17.2 26.6 %collective-permute-start.2 = (bf16[416,512]{1,0:T(8,128)(2,1)}, bf16[416,512]{1,0:T(8,128)(2,1)S(1)}, u32[]{:S(2)}, u32[]{:S(2)}) collective-permute-start(bf16[416,512]{1,0:T(8,128)(2,1)} %refs_1_.1), channel_id=1, source_target_pairs={{0,48},{16,0},{32,16},{48,32},{1,49},{17,1},{33,17},{49,33},{2,50}... | collective-permute-start | bytes 1277960 | tf_op jit(solution)/shard_map/ppermute | solution.py:162
  21.0 0.9 copy-start
  22.0 11.7 %copy-start.6 = (bf16[416,512]{1,0:T(8,128)(2,1)S(1)}, bf16[416,512]{1,0:T(8,128)(2,1)}, u32[]{:S(2)}) copy-start(bf16[416,512]{1,0:T(8,128)(2,1)} %refs_1_.1) | copy-start | bytes 1277956
  22.0 15.4 %copy-start.4 = (bf16[512,416]{0,1:T(8,128)(2,1)S(1)}, bf16[512,416]{0,1:T(8,128)(2,1)}, u32[]{:S(2)}) copy-start(bf16[512,416]{0,1:T(8,128)(2,1)} %param.13) | copy-start | bytes 1277956
  22.0 15.4 %copy-start.5 = (bf16[512,416]{0,1:T(8,128)(2,1)S(1)}, bf16[512,416]{0,1:T(8,128)(2,1)}, u32[]{:S(2)}) copy-start(bf16[512,416]{0,1:T(8,128)(2,1)} %param.12) | copy-start | bytes 1277956
  23.1 35.0 %all-to-all-start = ((bf16[32,32,512]{2,1,0:T(8,128)(2,1)}), bf16[32,32,512]{2,1,0:T(8,128)(2,1)}, u32[]{:S(2)}, u32[]{:S(2)}) async-start(bf16[32,32,512]{2,1,0:T(8,128)(2,1)} %bitcast.2), calls=%async_computation | async-start | bytes 2097152 | tf_op jit(solution)/shard_map/all_to_all | solution.py:189
  33.7 13.2 %collective-permute-start.3 = (bf16[416,512]{1,0:T(8,128)(2,1)S(1)}, bf16[416,512]{1,0:T(8,128)(2,1)}, u32[]{:S(2)}, u32[]{:S(2)}) collective-permute-start(bf16[416,512]{1,0:T(8,128)(2,1)S(1)} %copy-done.6), channel_id=1, source_target_pairs={{0,1},{1,0},{2,3},{3,2},{4,5},{5,4},{6,7},{7,6},{8,9},{9,8},{10,11... | collective-permute-start | bytes 1277960 | tf_op jit(solution)/shard_map/ppermute | solution.py:165
  37.4 9.4 %copy-start.2 = (bf16[832,512]{1,0:T(8,128)(2,1)}, bf16[832,512]{1,0:T(8,128)(2,1)S(1)}, u32[]{:S(2)}) copy-start(bf16[832,512]{1,0:T(8,128)(2,1)S(1)} %pad_maximum_fusion.refs_2_) | copy-start | bytes 2555908
  37.5 10.3 %collective-permute-start.7 = (bf16[832,512]{1,0:T(8,128)(2,1)S(1)}, bf16[832,512]{1,0:T(8,128)(2,1)S(1)}, u32[]{:S(2)}, u32[]{:S(2)}) collective-permute-start(bf16[832,512]{1,0:T(8,128)(2,1)S(1)} %pad_maximum_fusion.refs_2_), channel_id=1, source_target_pairs={{0,1},{1,0},{2,3},{3,2},{4,5},{5,4},{6,7},{7,6},{8,9},{9,8},{10,11... | collective-permute-start | bytes 2555912 | tf_op jit(solution)/shard_map/ppermute | solution.py:165
  39.4 6.8 %copy-start.7 = (bf16[416,512]{1,0:T(8,128)(2,1)}, bf16[416,512]{1,0:T(8,128)(2,1)S(1)}, u32[]{:S(2)}) copy-start(bf16[416,512]{1,0:T(8,128)(2,1)S(1)} %collective-permute-done.refs_0_.refs_2_) | copy-start | bytes 1277956
  39.4 7.4 %collective-permute-start.4 = (bf16[416,512]{1,0:T(8,128)(2,1)S(1)}, bf16[416,512]{1,0:T(8,128)(2,1)}, u32[]{:S(2)}, u32[]{:S(2)}) collective-permute-start(bf16[416,512]{1,0:T(8,128)(2,1)S(1)} %collective-permute-done.refs_0_.refs_2_), channel_id=1, source_target_pairs={{0,1},{1,0},{2,3},{3,2},{4,5},{5,4},{6,7},{7,6},{8,9},{9,8},{10,11... | collective-permute-start | bytes 1277960 | tf_op jit(solution)/shard_map/ppermute | solution.py:165
  41.8 4.4 %copy-start.8 = (bf16[416,512]{1,0:T(8,128)(2,1)}, bf16[416,512]{1,0:T(8,128)(2,1)S(1)}, u32[]{:S(2)}) copy-start(bf16[416,512]{1,0:T(8,128)(2,1)S(1)} %collective-permute-done.1.refs_1_.refs_3_) | copy-start | bytes 1277956
  41.9 5.0 %collective-permute-start.5 = (bf16[416,512]{1,0:T(8,128)(2,1)S(1)}, bf16[416,512]{1,0:T(8,128)(2,1)}, u32[]{:S(2)}, u32[]{:S(2)}) collective-permute-start(bf16[416,512]{1,0:T(8,128)(2,1)S(1)} %collective-permute-done.1.refs_1_.refs_3_), channel_id=1, source_target_pairs={{0,1},{1,0},{2,3},{3,2},{4,5},{5,4},{6,7},{7,6},{8,9},{9,8},{10,11... | collective-permute-start | bytes 1277960 | tf_op jit(solution)/shard_map/ppermute | solution.py:165
  43.8 2.4 %copy-start.9 = (bf16[416,512]{1,0:T(8,128)(2,1)}, bf16[416,512]{1,0:T(8,128)(2,1)S(1)}, u32[]{:S(2)}) copy-start(bf16[416,512]{1,0:T(8,128)(2,1)S(1)} %collective-permute-done.2.refs_2_.refs_4_) | copy-start | bytes 1277956
  43.8 3.9 %collective-permute-start.6 = (bf16[416,512]{1,0:T(8,128)(2,1)S(1)}, bf16[416,512]{1,0:T(8,128)(2,1)}, u32[]{:S(2)}, u32[]{:S(2)}) collective-permute-start(bf16[416,512]{1,0:T(8,128)(2,1)S(1)} %collective-permute-done.2.refs_2_.refs_4_), channel_id=1, source_target_pairs={{0,1},{1,0},{2,3},{3,2},{4,5},{5,4},{6,7},{7,6},{8,9},{9,8},{10,11... | collective-permute-start | bytes 1277960 | tf_op jit(solution)/shard_map/ppermute | solution.py:165
  47.7 0.9 copy-start.3
  62.4 26.3 %copy-start.11 = (s32[128]{0:T(128)S(1)}, s32[128]{0:T(128)}, u32[]{:S(2)}) copy-start(s32[128]{0:T(128)} %param.15) | copy-start | bytes 1540
  62.4 26.3 %copy-start.1 = (bf16[128,512]{1,0:T(8,128)(2,1)S(1)}, bf16[128,512]{1,0:T(8,128)(2,1)}, u32[]{:S(2)}) copy-start(bf16[128,512]{1,0:T(8,128)(2,1)} %grad_ref.1) | copy-start | bytes 393220
  62.4 26.4 %copy-start.10 = (bf16[128,512]{1,0:T(8,128)(2,1)S(1)}, bf16[128,512]{1,0:T(8,128)(2,1)}, u32[]{:S(2)}) copy-start(bf16[128,512]{1,0:T(8,128)(2,1)} %param.8) | copy-start | bytes 393220
  84.1 20.4 %all-to-all-start.2 = ((bf16[8,32,832]{2,1,0:T(8,128)(2,1)}), bf16[8,32,832]{2,1,0:T(8,128)(2,1)S(1)}, u32[]{:S(2)}, u32[]{:S(2)}) async-start(bf16[8,32,832]{2,1,0:T(8,128)(2,1)} %shard_map.114), calls=%async_computation.2 | async-start | bytes 917504 | tf_op jit(solution)/shard_map/all_to_all | solution.py:212
  88.7 72.0 %all-gather.4.cloned.1.call-start = ((), (), s32[]{:S(2)}) async-start(), calls=%async_computation.5 | async-start | bytes 4456448 | tf_op jit(solution)/shard_map/all_gather | solution.py:198
  106.0 21.6 %all-to-all-start.3 = ((bf16[32,32,832]{2,1,0:T(8,128)(2,1)}), bf16[32,32,832]{2,1,0:T(8,128)(2,1)}, u32[]{:S(2)}, u32[]{:S(2)}) async-start(bf16[32,32,832]{2,1,0:T(8,128)(2,1)} %bitcast.6), calls=%async_computation.3 | async-start | bytes 3670016 | tf_op jit(solution)/shard_map/all_to_all | solution.py:206
  117.0 14.6 %collective-permute-start.8 = (bf16[2,8,4,32,416]{4,3,2,1,0:T(8,128)(2,1)}, bf16[2,8,4,32,416]{4,3,2,1,0:T(8,128)(2,1)}, u32[]{:S(2)}, u32[]{:S(2)}) collective-permute-start(bf16[2,8,4,32,416]{4,3,2,1,0:T(8,128)(2,1)} %get-tuple-element.15.send_ref), channel_id=1, source_target_pairs={{0,1},{1,0},{2,3},{3,2},{4,5},{5,4},{6,7},{7,6},{8,9},{9,8},{10,11... | collective-permute-start | bytes 5111816 | tf_op jit(solution)/shard_map/ppermute | solution.py:165
  139.2 18.4 %collective-permute-start.9 = (bf16[4,8,32,416]{3,2,1,0:T(8,128)(2,1)}, bf16[4,8,32,416]{3,2,1,0:T(8,128)(2,1)}, u32[]{:S(2)}, u32[]{:S(2)}) collective-permute-start(bf16[4,8,32,416]{3,2,1,0:T(8,128)(2,1)} %get-tuple-element.18), channel_id=1, source_target_pairs={{0,1},{1,0},{2,3},{3,2},{4,5},{5,4},{6,7},{7,6},{8,9},{9,8},{10,11... | collective-permute-start | bytes 2555912 | tf_op jit(solution)/shard_map/ppermute | solution.py:165
  145.1 41.8 %all-to-all-start.4 = ((bf16[8,128,512]{2,1,0:T(8,128)(2,1)}), bf16[8,128,512]{2,1,0:T(8,128)(2,1)S(1)}, u32[]{:S(2)}, u32[]{:S(2)}) async-start(bf16[8,128,512]{2,1,0:T(8,128)(2,1)} %bitcast.16), calls=%async_computation.4 | async-start | bytes 2097152 | tf_op jit(solution)/shard_map/all_to_all | solution.py:229
Sparse Core Ops, SparseCore 0:
  11.7 98.7 all-gather.5
  113.2 47.4 all-gather.3
